TPU v7x, 32 devices: a whole 2x2x4 slice. The times are simulated.
32 devices in a mesh: dp: 8 (over z, y), seq: 4 (over x, core).
Axes of the slice: x: 2, y: 2, z: 4, core: 2. Of those that a mesh axis runs over, the one named last changes fastest.
Arguments:
- tokens: bfloat16 [8, 512, 2048], P('dp', 'seq'), may hold values from -6 to 6
- doc_ids: int32 [8, 512], P('dp', 'seq'), may hold values from 0 to 7, as said below
- query_key_value_weight: bfloat16 [2048, 4096], P(('dp', 'seq')), may hold values from -0.125 to 0.125
- out_weight: bfloat16 [2048, 2048], P(('dp', 'seq')), may hold values from -1 to 1
- gate_up_weight: bfloat16 [2048, 2, 6144], P(('dp', 'seq')), may hold values from -0.125 to 0.125
- down_weight: bfloat16 [2048, 6144], P(('dp', 'seq')), may hold values from -0.078125 to 0.078125
- attn_gain: bfloat16 [2048], P(('dp', 'seq')), may hold values from 0.5 to 1.5
- q_gain: bfloat16 [128], P(('dp', 'seq')), may hold values from 0.5 to 1.5
- k_gain: bfloat16 [128], P(('dp', 'seq')), may hold values from 0.5 to 1.5
- mlp_gain: bfloat16 [2048], P(('dp', 'seq')), may hold values from 0.5 to 1.5
- out_grad: bfloat16 [8, 512, 2048], P('dp', 'seq'), may hold values from -6 to 6
Outputs:
- output: bfloat16 [8, 512, 2048], P('dp', 'seq')
- token_grad: bfloat16 [8, 512, 2048], P('dp', 'seq')
- grad_qkv: float32 [2048, 4096], P(('dp', 'seq'))
- grad_out: float32 [2048, 2048], P(('dp', 'seq'))
- grad_gate_up: float32 [2048, 2, 6144], P(('dp', 'seq'))
- grad_down: float32 [2048, 6144], P(('dp', 'seq'))
- grad_attn_gain: float32 [2048], P(('dp', 'seq'))
- grad_q_gain: float32 [128], P(('dp', 'seq'))
- grad_k_gain: float32 [128], P(('dp', 'seq'))
- grad_mlp_gain: float32 [2048], P(('dp', 'seq'))
Inputs may be any that keep to these rules, and one draw needn't show every extreme that they name: `doc_ids`: along each sequence the doc ids never fall; the first token has 0 and the last has the maximum; ids may skip values.
All inputs are finite; a program needn't handle non-finite values.
Results may differ from a plain program's by a relative error of at most 0.018.
Values may be sent and summed in bfloat16 or wider, within the bound.
No kernel may reach another device: no remote copies, remote signals or barrier semaphores. Data moves between devices by JAX's collectives and lax.ppermute only.
A program may use at most 704 MiB of HBM per device.

v0:
```python
import math

import jax
import jax.numpy as jnp
from jax import lax
from jax.sharding import PartitionSpec as P

QUERY_HEADS = 16
KEY_VALUE_HEADS = 8
HEAD_SIZE = 128


EPS = 1e-06
THETA = 1000000.0


def norm_rows(value, gain):
    return value * lax.rsqrt(jnp.mean(value * value, axis=-1, keepdims=True) + EPS) * gain


def rotate(value, position):
    half = value.shape[-1] // 2
    freqs = jnp.exp(jnp.arange(half).astype(jnp.float32) * (-math.log(THETA) / half))
    angle = position[:, None] * freqs[None, :]
    cosine = jnp.cos(angle)[:, None, :]
    sine = jnp.sin(angle)[:, None, :]
    first_half = value[..., :half]
    second_half = value[..., half:]
    return jnp.concatenate(
        [first_half * cosine - second_half * sine, second_half * cosine + first_half * sine],
        axis=-1,
    )


def narrow(value):
    return lax.optimization_barrier(value.astype(jnp.bfloat16)).astype(jnp.float32)


def times_t(left, right):
    return lax.dot_general(
        left, right, (((1,), (1,)), ((), ())), preferred_element_type=jnp.float32
    )


def transposed(left, right):
    return lax.dot_general(
        left, right, (((0,), (0,)), ((), ())), preferred_element_type=jnp.float32
    )


def doc_masks(doc_rows, doc_all, row_index):
    key_index = jnp.arange(doc_all.shape[0], dtype=jnp.int32)
    doc_start = jnp.sum((doc_all[None, :] < doc_rows[:, None]).astype(jnp.int32), axis=1)
    position = (row_index - doc_start).astype(jnp.float32)
    allowed = (doc_all[None, :] == doc_rows[:, None]) & (key_index[None, :] <= row_index[:, None])
    return (position, allowed)


def masked_scores(query_blocked, key_all, allowed, score_scale):
    raw = jnp.einsum("qhgd,khd->hgqk", query_blocked, key_all, preferred_element_type=jnp.float32)
    return jnp.where(allowed[None, None], raw * score_scale, -1000000000.0)


def attend_forward(query_blocked, key_all, value_all, allowed, score_scale):
    scores = masked_scores(query_blocked, key_all, allowed, score_scale)
    peak = jnp.max(scores, axis=-1, keepdims=True)
    weights_exp = jnp.exp(scores - peak)
    total = jnp.sum(weights_exp, axis=-1, keepdims=True)
    log_total = peak + jnp.log(total)
    probs_b = (weights_exp / total).astype(jnp.bfloat16)
    attended = jnp.einsum("hgqk,khd->qhgd", probs_b, value_all, preferred_element_type=jnp.float32)
    return (attended, log_total)


def attend_backward(
    query_blocked, key_all, value_all, allowed, log_total, attended_gradient_blocks, score_scale
):
    probs = jnp.exp(masked_scores(query_blocked, key_all, allowed, score_scale) - log_total)
    d_probs = jnp.einsum(
        "qhgd,khd->hgqk", attended_gradient_blocks, value_all, preferred_element_type=jnp.float32
    )
    row_dot = jnp.sum(probs * d_probs, axis=-1, keepdims=True)
    d_raw_b = (probs * (d_probs - row_dot) * score_scale).astype(jnp.bfloat16)
    d_query = jnp.einsum("hgqk,khd->qhgd", d_raw_b, key_all, preferred_element_type=jnp.float32)
    d_key = jnp.einsum("hgqk,qhgd->khd", d_raw_b, query_blocked, preferred_element_type=jnp.float32)
    d_value = jnp.einsum(
        "hgqk,qhgd->khd",
        probs.astype(jnp.bfloat16),
        attended_gradient_blocks,
        preferred_element_type=jnp.float32,
    )
    return (d_query, d_key, d_value)


def flat_layer(
    tokens,
    doc_own,
    doc_all,
    query_key_value_weight,
    out_weight,
    gate_up_weight,
    down_weight,
    attn_gain,
    q_gain,
    k_gain,
    mlp_gain,
    out_grad,
):
    token_rows = tokens.shape[1]
    query_width = QUERY_HEADS * HEAD_SIZE
    key_value_width = KEY_VALUE_HEADS * HEAD_SIZE
    query_groups = QUERY_HEADS // KEY_VALUE_HEADS
    score_scale = HEAD_SIZE ** (-0.5)
    w_qkv, w_out, g_attn, g_query, g_key = (
        lax.all_gather(query_key_value_weight, ("dp", "seq"), axis=0, tiled=True),
        lax.all_gather(out_weight, ("dp", "seq"), axis=0, tiled=True),
        lax.all_gather(attn_gain, ("dp", "seq"), axis=0, tiled=True),
        lax.all_gather(q_gain, ("dp", "seq"), axis=0, tiled=True),
        lax.all_gather(k_gain, ("dp", "seq"), axis=0, tiled=True),
    )
    query_index = lax.axis_index("seq") * token_rows + jnp.arange(token_rows, dtype=jnp.int32)
    position, allowed = doc_masks(doc_own, doc_all, query_index)
    x_rows = tokens[0].astype(jnp.float32)
    normed, norm_back = jax.vjp(norm_rows, x_rows, g_attn.astype(jnp.float32))
    normed_b = normed.astype(jnp.bfloat16)
    projected_output = jnp.dot(normed_b, w_qkv, preferred_element_type=jnp.float32)
    query_raw = projected_output[:, :query_width].reshape(token_rows, QUERY_HEADS, HEAD_SIZE)
    key_unrotated = projected_output[:, query_width : query_width + key_value_width].reshape(
        token_rows, KEY_VALUE_HEADS, HEAD_SIZE
    )
    value_blocked = (
        projected_output[:, query_width + key_value_width :]
        .reshape(token_rows, KEY_VALUE_HEADS, HEAD_SIZE)
        .astype(jnp.bfloat16)
    )

    def shape_heads(query_in, key_in, gain_query, gain_key):
        return (
            rotate(norm_rows(query_in, gain_query), position),
            rotate(norm_rows(key_in, gain_key), position),
        )

    (query_rotated, key_rot), heads_back = jax.vjp(
        shape_heads,
        query_raw,
        key_unrotated,
        g_query.astype(jnp.float32),
        g_key.astype(jnp.float32),
    )
    query_blocked = query_rotated.astype(jnp.bfloat16).reshape(
        token_rows, KEY_VALUE_HEADS, query_groups, HEAD_SIZE
    )
    key_b = key_rot.astype(jnp.bfloat16)
    key_all, value_all = (
        lax.all_gather(key_b, "seq", axis=0, tiled=True),
        lax.all_gather(value_blocked, "seq", axis=0, tiled=True),
    )
    attended, log_total = attend_forward(query_blocked, key_all, value_all, allowed, score_scale)
    attended_b = attended.reshape(token_rows, query_width).astype(jnp.bfloat16)
    middle = x_rows + times_t(attended_b, w_out)
    w_gate_up, w_down, g_mlp = (
        lax.all_gather(gate_up_weight, ("dp", "seq"), axis=0, tiled=True),
        lax.all_gather(down_weight, ("dp", "seq"), axis=0, tiled=True),
        lax.all_gather(mlp_gain, ("dp", "seq"), axis=0, tiled=True),
    )
    normed_mid, mid_back = jax.vjp(norm_rows, middle, g_mlp.astype(jnp.float32))
    normed_mid_b = normed_mid.astype(jnp.bfloat16)
    gate = jnp.dot(normed_mid_b, w_gate_up[:, 0, :], preferred_element_type=jnp.float32)
    upward = jnp.dot(normed_mid_b, w_gate_up[:, 1, :], preferred_element_type=jnp.float32)
    activated, act_back = jax.vjp(lambda gate_in, up_in: jax.nn.silu(gate_in) * up_in, gate, upward)
    hidden_b = activated.astype(jnp.bfloat16)
    output = (middle + times_t(hidden_b, w_down)).astype(jnp.bfloat16)[None]
    back_qkv, back_out, back_gate_up, back_down = (
        lax.all_gather(query_key_value_weight, ("dp", "seq"), axis=0, tiled=True),
        lax.all_gather(out_weight, ("dp", "seq"), axis=0, tiled=True),
        lax.all_gather(gate_up_weight, ("dp", "seq"), axis=0, tiled=True),
        lax.all_gather(down_weight, ("dp", "seq"), axis=0, tiled=True),
    )
    grad_rows = out_grad[0].astype(jnp.float32)
    grad_rows_b = out_grad[0]
    d_hidden = jnp.dot(grad_rows_b, back_down, preferred_element_type=jnp.float32)
    d_gate, d_up = act_back(d_hidden)
    d_gate_b = d_gate.astype(jnp.bfloat16)
    d_up_b = d_up.astype(jnp.bfloat16)
    d_normed_mid = times_t(d_gate_b, back_gate_up[:, 0, :]) + times_t(d_up_b, back_gate_up[:, 1, :])
    d_mid_norm, d_gain_mlp = mid_back(d_normed_mid)
    d_middle = grad_rows + d_mid_norm
    gate_rows = transposed(normed_mid_b, d_gate_b)
    up_rows = transposed(normed_mid_b, d_up_b)
    down_rows = transposed(grad_rows_b, hidden_b)
    mlp_grads = lax.psum_scatter(
        jnp.stack([gate_rows, up_rows, down_rows], axis=1),
        ("dp", "seq"),
        scatter_dimension=0,
        tiled=True,
    )
    d_branch_b = d_middle.astype(jnp.bfloat16)
    attended_gradient = jnp.dot(d_branch_b, back_out, preferred_element_type=jnp.float32)
    attended_gradient_blocks = attended_gradient.astype(jnp.bfloat16).reshape(
        token_rows, KEY_VALUE_HEADS, query_groups, HEAD_SIZE
    )
    d_query, d_key_part, d_value_part = attend_backward(
        query_blocked, key_all, value_all, allowed, log_total, attended_gradient_blocks, score_scale
    )
    d_key, d_value = (
        lax.psum_scatter(
            d_key_part.astype(jnp.bfloat16), "seq", scatter_dimension=0, tiled=True
        ).astype(jnp.float32),
        lax.psum_scatter(
            d_value_part.astype(jnp.bfloat16), "seq", scatter_dimension=0, tiled=True
        ).astype(jnp.float32),
    )
    d_query_raw, d_key_raw, d_gain_query, d_gain_key = heads_back(
        (narrow(d_query.reshape(token_rows, QUERY_HEADS, HEAD_SIZE)), narrow(d_key))
    )
    d_projected_b = jnp.concatenate(
        [
            d_query_raw.reshape(token_rows, query_width),
            d_key_raw.reshape(token_rows, key_value_width),
            d_value.reshape(token_rows, key_value_width),
        ],
        axis=1,
    ).astype(jnp.bfloat16)
    d_normed = times_t(d_projected_b, back_qkv)
    d_x_norm, d_gain_attn = norm_back(d_normed)
    token_grad = (d_middle + d_x_norm).astype(jnp.bfloat16)[None]
    qkv_term = transposed(normed_b, d_projected_b)
    out_term = transposed(d_branch_b, attended_b)
    grad_qkv, grad_out, grad_attn_gain, grad_q_gain, grad_k_gain, grad_mlp_gain = (
        lax.psum_scatter(qkv_term, ("dp", "seq"), scatter_dimension=0, tiled=True),
        lax.psum_scatter(out_term, ("dp", "seq"), scatter_dimension=0, tiled=True),
        lax.psum_scatter(d_gain_attn, ("dp", "seq"), scatter_dimension=0, tiled=True),
        lax.psum_scatter(d_gain_query, ("dp", "seq"), scatter_dimension=0, tiled=True),
        lax.psum_scatter(d_gain_key, ("dp", "seq"), scatter_dimension=0, tiled=True),
        lax.psum_scatter(d_gain_mlp, ("dp", "seq"), scatter_dimension=0, tiled=True),
    )
    grad_gate_up = mlp_grads[:, :2, :]
    grad_down = mlp_grads[:, 2, :]
    return (
        output,
        token_grad,
        grad_qkv,
        grad_out,
        grad_gate_up,
        grad_down,
        grad_attn_gain,
        grad_q_gain,
        grad_k_gain,
        grad_mlp_gain,
    )


def shards(
    tokens,
    doc_ids,
    query_key_value_weight,
    out_weight,
    gate_up_weight,
    down_weight,
    attn_gain,
    q_gain,
    k_gain,
    mlp_gain,
    out_grad,
):
    doc_all = lax.all_gather(doc_ids, "seq", axis=1, tiled=True)[0]
    doc_own = doc_ids[0]
    result = flat_layer(
        tokens,
        doc_own,
        doc_all,
        query_key_value_weight,
        out_weight,
        gate_up_weight,
        down_weight,
        attn_gain,
        q_gain,
        k_gain,
        mlp_gain,
        out_grad,
    )
    return result


def solution(mesh):
    in_specs = (
        P("dp", "seq", None),
        P("dp", "seq"),
        P(("dp", "seq"), None),
        P(("dp", "seq"), None),
        P(("dp", "seq"), None, None),
        P(("dp", "seq"), None),
        P(("dp", "seq")),
        P(("dp", "seq")),
        P(("dp", "seq")),
        P(("dp", "seq")),
        P("dp", "seq", None),
    )
    out_specs = (
        P("dp", "seq", None),
        P("dp", "seq", None),
        P(("dp", "seq"), None),
        P(("dp", "seq"), None),
        P(("dp", "seq"), None, None),
        P(("dp", "seq"), None),
        P(("dp", "seq")),
        P(("dp", "seq")),
        P(("dp", "seq")),
        P(("dp", "seq")),
    )
    return jax.shard_map(shards, mesh=mesh, in_specs=in_specs, out_specs=out_specs, check_vma=False)
```

profile of v0, /device:TPU:0, one launch (start us, length us, event | category | flops | bytes accessed | tf_op | source)
XLA Modules:
  0.0 2734.5 jit_solution(1824090477932924339)
XLA Ops:
  11.4 42.8 %all-reduce.13 = (bf16[2048]{0:T(1024)(128)(2,1)S(1)}, bf16[128]{0:T(256)(128)(2,1)S(1)}, bf16[128]{0:T(256)(128)(2,1)S(1)}, bf16[2048]{0:T(1024)(128)(2,1)S(1)}) all-reduce(bf16[2048]{0:T(1024)(128)(2,1)S(1)} %dynamic-update-slice, bf16[128]{0:T(256)(128)(2,1)S(1)} %dynamic-update-slice.1, ...), channel_id=1, replica_groups=mesh['dp'=8,'seq'=4] {'dp','seq'}, use_global_device_ids=true, to_apply=%add.4 | all-reduce | flops 4352 | bytes 17408
  54.2 5.5 all_gather.42
  62.2 67.3 %all-gather.7.cloned.1.call-done = bf16[2048,4096]{1,0:T(8,128)(2,1)} async-done(((bf16[64,4096]{1,0:T(8,128)(2,1)}), bf16[2048,4096]{1,0:T(8,128)(2,1)}) %all-gather.7.cloned.1.call-update) | async-done | bytes 16777232 | tf_op jit(solution)/shard_map/all_gather | solution.py:115
  129.5 8.4 fusion.58
  147.9 7.3 all-gather.11.cloned.1.call-done
  160.0 14.2 all-gather.9.cloned.1.call-done
  177.7 76.7 %all-gather.13.cloned.1.call-done = bf16[2048,2048]{1,0:T(8,128)(2,1)} async-done(((bf16[64,2048]{1,0:T(8,128)(2,1)}), bf16[2048,2048]{1,0:T(8,128)(2,1)}) %all-gather.13.cloned.1.call-update) | async-done | bytes 8388624 | tf_op jit(solution)/shard_map/all_gather | solution.py:116
  254.4 6.3 multiply_reduce_fusion.4
  261.0 270.9 %all-gather.15.cloned.1.call-done = bf16[2048,2,6144]{2,0,1:T(8,128)(2,1)} async-done(((bf16[64,2,6144]{2,0,1:T(8,128)(2,1)}), bf16[2048,2,6144]{2,0,1:T(8,128)(2,1)}) %all-gather.15.cloned.1.call-update) | async-done | bytes 50331664 | tf_op jit(solution)/shard_map/all_gather | solution.py:162
  531.8 12.0 fusion.4
  543.9 11.7 fusion.2
  555.6 131.8 %all-gather.17.cloned.1.call-done = bf16[2048,6144]{1,0:T(8,128)(2,1)} async-done(((bf16[64,6144]{1,0:T(8,128)(2,1)}), bf16[2048,6144]{1,0:T(8,128)(2,1)}) %all-gather.17.cloned.1.call-update) | async-done | bytes 25165840 | tf_op jit(solution)/shard_map/all_gather | solution.py:163
  687.4 14.6 multiply_convert_fusion
  702.0 14.9 fusion.1
  716.9 15.7 multiply_reduce_fusion
  735.3 5.5 convolution_convert_fusion
  746.1 8.9 fusion.26
  755.1 4.1 bitcast_convert_fusion
  761.6 21.1 convolution_bitcast_fusion.1
  782.7 20.8 convolution_bitcast_fusion.2
  803.5 19.3 convolution_bitcast_fusion
  822.9 97.5 %pad_maximum_fusion = f32[2048,3,6144]{2,0,1:T(8,128)} fusion(f32[2048,1,6144]{2,0,1:T(8,128)} %convolution_bitcast_fusion, f32[2048,1,6144]{2,0,1:T(8,128)} %convolution_bitcast_fusion.1, f32[2048,1,6144]{2,0,1:T(8,128)} %convolution_bitcast_fusion.2), kind=kLoop, calls=%fused_computation.1 | loop fusion | flops 75497472 | bytes 301989888 | tf_op jit(solution)/shard_map/stack | solution.py:192
  921.8 10.6 fusion.53
  933.8 10.2 fusion.28
  952.9 19.5 fusion.51
  973.7 17.7 fusion.16
  991.4 14.2 fusion.32
  1005.6 40.2 %all-reduce.12 = (f32[2048]{0:T(1024)S(1)}, f32[128]{0:T(128)S(1)}, f32[128]{0:T(128)S(1)}, f32[2048]{0:T(1024)S(1)}) all-reduce(f32[2048]{0:T(1024)S(1)} %get-tuple-element.76, f32[128]{0:T(128)S(1)} %get-tuple-element.72, f32[128]{0:T(128)S(1)} %get-tuple-element.74, ...), channel_id=7, replica_groups=mesh['dp'=8,'seq'=4] {'dp','seq'}, use_global_device_ids=true, to_apply=%region_18.19.clone | all-reduce | flops 4352 | bytes 34816
  1049.3 1134.4 %reduce-scatter.14.cloned.1.call-done = f32[64,3,6144]{2,0,1:T(8,128)} async-done(((f32[2048,3,6144]{2,0,1:T(8,128)}), f32[64,3,6144]{2,0,1:T(8,128)}) %reduce-scatter.14.cloned.1.call-update) | async-done | bytes 4718608 | tf_op jit(solution)/shard_map/reduce_scatter | solution.py:191
  2185.7 4.1 copy.169
  2191.0 177.5 %reduce-scatter.12.cloned.1.call-done = f32[64,2048]{1,0:T(8,128)} async-done(((f32[2048,2048]{1,0:T(8,128)}), f32[64,2048]{1,0:T(8,128)}) %reduce-scatter.12.cloned.1.call-update) | async-done | bytes 524304 | tf_op jit(solution)/shard_map/reduce_scatter | solution.py:231
  2368.5 359.0 %reduce-scatter.10.cloned.1.call-done = f32[64,4096]{1,0:T(8,128)} async-done(((f32[2048,4096]{1,0:T(8,128)}), f32[64,4096]{1,0:T(8,128)}) %reduce-scatter.10.cloned.1.call-update) | async-done | bytes 1048592 | tf_op jit(solution)/shard_map/reduce_scatter | solution.py:230
  (195 shorter events, 54.3 us)
Async XLA Ops:
  7.2 122.3 %all-gather.7.cloned.1.call-start = ((), (), s32[]{:S(2)}) async-start(), calls=%async_computation.5 | async-start | bytes 17301504 | tf_op jit(solution)/shard_map/all_gather | solution.py:115
  7.9 147.3 %all-gather.11.cloned.1.call-start = ((), (), s32[]{:S(2)}) async-start(), calls=%async_computation.7 | async-start | bytes 1310720 | tf_op jit(solution)/shard_map/all_gather | solution.py:155
  54.2 84.2 %copy-start.43 = (f32[128]{0:T(128)}, f32[128]{0:T(128)S(1)}, u32[]{:S(2)}) copy-start(f32[128]{0:T(128)S(1)} %convert_element_type.127) | copy-start | bytes 1540
  54.2 75.3 %copy-start.27 = (f32[2048]{0:T(1024)}, f32[2048]{0:T(1024)S(1)}, u32[]{:S(2)}) copy-start(f32[2048]{0:T(1024)S(1)} %convert_element_type.124) | copy-start | bytes 24580
  61.8 76.1 %copy-start.45 = (f32[128]{0:T(128)}, f32[128]{0:T(128)S(1)}, u32[]{:S(2)}) copy-start(f32[128]{0:T(128)S(1)} %fusion.37) | copy-start | bytes 1540
  61.8 67.7 %copy-start.37 = (f32[128]{0:T(128)}, f32[128]{0:T(128)S(1)}, u32[]{:S(2)}) copy-start(f32[128]{0:T(128)S(1)} %fusion.64) | copy-start | bytes 1540
  62.1 84.8 %copy-start.20 = (f32[128,64]{1,0:T(8,128)}, f32[128,64]{1,0:T(8,128)S(1)}, u32[]{:S(2)}) copy-start(f32[128,64]{1,0:T(8,128)S(1)} %get-tuple-element.99) | copy-start | bytes 98308
  62.1 84.8 %copy-start.22 = (f32[128,64]{1,0:T(8,128)}, f32[128,64]{1,0:T(8,128)S(1)}, u32[]{:S(2)}) copy-start(f32[128,64]{1,0:T(8,128)S(1)} %get-tuple-element.100) | copy-start | bytes 98308
  138.0 6.8 copy-start.12
  139.2 6.4 copy-start.42
  140.1 34.1 %all-gather.9.cloned.1.call-start = ((), (), s32[]{:S(2)}) async-start(), calls=%async_computation.6 | async-start | bytes 1310720 | tf_op jit(solution)/shard_map/all_gather | solution.py:156
  141.1 113.3 %all-gather.13.cloned.1.call-start = ((), (), s32[]{:S(2)}) async-start(), calls=%async_computation.8 | async-start | bytes 8650752 | tf_op jit(solution)/shard_map/all_gather | solution.py:116
  141.7 390.2 %all-gather.15.cloned.1.call-start = ((), (), s32[]{:S(2)}) async-start(), calls=%async_computation.9 | async-start | bytes 51904512 | tf_op jit(solution)/shard_map/all_gather | solution.py:162
  144.8 542.6 %all-gather.17.cloned.1.call-start = ((), (), s32[]{:S(2)}) async-start(), calls=%async_computation.10 | async-start | bytes 25952256 | tf_op jit(solution)/shard_map/all_gather | solution.py:163
  145.3 804.5 %reduce-scatter.8.cloned.1.call-start = ((), (), s32[]{:S(2)}) async-start(), calls=%async_computation.11 | async-start | bytes 1310720 | tf_op jit(solution)/shard_map/reduce_scatter | solution.py:206
  146.5 10.9 copy-start.29
  147.7 9.7 copy-start.15
  147.9 12.1 copy-start.17
  160.0 94.4 %copy-start.7 = (bf16[1,128,2048]{2,1,0:T(8,128)(2,1)S(1)}, bf16[1,128,2048]{2,1,0:T(8,128)(2,1)}, u32[]{:S(2)}) copy-start(bf16[1,128,2048]{2,1,0:T(8,128)(2,1)} %param.11) | copy-start | bytes 1572868
  177.6 83.1 %copy-start.18 = (bf16[8,128,2,128]{3,1,2,0:T(8,128)(2,1)}, bf16[8,128,2,128]{3,1,2,0:T(8,128)(2,1)S(1)}, u32[]{:S(2)}) copy-start(bf16[8,128,2,128]{3,1,2,0:T(8,128)(2,1)S(1)} %fusion.27) | copy-start | bytes 1572868
  260.8 471.9 %copy-start.5 = (f32[128,2048]{1,0:T(8,128)}, f32[128,2048]{1,0:T(8,128)S(1)}, u32[]{:S(2)}) copy-start(f32[128,2048]{1,0:T(8,128)S(1)} %get-tuple-element.104) | copy-start | bytes 3145732
  260.8 494.3 %copy-start.35 = (f32[2,8,128]{2,1,0:T(8,128)}, f32[2,8,128]{2,1,0:T(8,128)S(1)}, u32[]{:S(2)}) copy-start(f32[2,8,128]{2,1,0:T(8,128)S(1)} %log_add_fusion) | copy-start | bytes 24580
  702.0 101.5 %copy-start.9 = (bf16[128,6144]{1,0:T(8,128)(2,1)}, bf16[128,6144]{1,0:T(8,128)(2,1)S(1)}, u32[]{:S(2)}) copy-start(bf16[128,6144]{1,0:T(8,128)(2,1)S(1)} %get-tuple-element.88) | copy-start | bytes 4718596
  755.1 197.8 %reduce-scatter.16.cloned.1.call-start = ((), (), s32[]{:S(2)}) async-start(), calls=%async_computation.15 | async-start | bytes 1310720 | tf_op jit(solution)/shard_map/reshape | solution.py:220
  782.7 20.8 copy-start.14
  822.9 1360.9 %reduce-scatter.14.cloned.1.call-start = ((), (), s32[]{:S(2)}) async-start(), calls=%async_computation.14 | async-start | bytes 155713536 | tf_op jit(solution)/shard_map/reduce_scatter | solution.py:191
  920.5 1448.0 %reduce-scatter.12.cloned.1.call-start = ((), (), s32[]{:S(2)}) async-start(), calls=%async_computation.13 | async-start | bytes 17301504 | tf_op jit(solution)/shard_map/reduce_scatter | solution.py:231
  932.4 12.2 copy-start.21
  932.4 12.2 copy-start.23
  932.4 1795.1 %reduce-scatter.10.cloned.1.call-start = ((), (), s32[]{:S(2)}) async-start(), calls=%async_computation.12 | async-start | bytes 34603008 | tf_op jit(solution)/shard_map/reduce_scatter | solution.py:230
  991.4 14.2 copy-start.39
  991.4 56.8 %copy-start.46 = (f32[128]{0:T(128)S(1)}, f32[128]{0:T(128)}, u32[]{:S(2)}) copy-start(f32[128]{0:T(128)} %copy-done.45) | copy-start | bytes 1540
  (27 other events, 62.7 us)
Sparse Core Ops, SparseCore 0:
  10.9 118.5 all-gather.6
  140.2 14.8 all-gather.10
  157.3 16.8 all-gather.8
  176.9 77.4 all-gather.12
  257.7 274.1 all-gather.14
  534.6 152.7 all-gather.16
  755.2 23.0 reduce-scatter.7
  823.0 23.1 reduce-scatter.15
  920.6 1263.1 reduce-scatter.13
  2186.6 181.8 reduce-scatter.11
  2371.4 356.0 reduce-scatter.9
where the time goes:
time: 2750 us; the launch traced here: 2730 us
  waiting for transfers between devices  2240 us (81%)
  matrix products  245 us (9%)
  other arithmetic  113 us (4%)
  blocking collectives  88.6 us (3%)
  local copies, waits for them, and re-layouts  30.8 us (1%)
    reduce_scatter x1, waiting for transfers between devices, flat_layer(): lax.psum_scatter(jnp.stack([gate_rows, up_rows, down_rows], axis=1), ('dp...  1130 us
    reduce_scatter x1, waiting for transfers between devices, flat_layer(): lax.psum_scatter(qkv_term, ('dp', 'seq'), scatter_dimension=0, tiled=True)  359 us
    all_gather x1, waiting for transfers between devices, flat_layer(): lax.all_gather(gate_up_weight, ('dp', 'seq'), axis=0, tiled=True)  271 us
    reduce_scatter x1, waiting for transfers between devices, flat_layer(): lax.psum_scatter(out_term, ('dp', 'seq'), scatter_dimension=0, tiled=True)  177 us
    all_gather x1, waiting for transfers between devices, flat_layer(): lax.all_gather(down_weight, ('dp', 'seq'), axis=0, tiled=True)  132 us
    another operation x1, other arithmetic, flat_layer(): jnp.stack([gate_rows, up_rows, down_rows], axis=1)  97.5 us
    dot_general x5, matrix products, transposed(): lax.dot_general(left, right, (((0,), (0,)), ((), ())), preferred_element_...  91.3 us
    unnamed x2, blocking collectives  83 us
  transfers between devices with their start and end apart: 11, of which 9 were waited for; matrix products, arithmetic and copies ran while one was open for 11% of the time, Pallas kernels for 0%

commit v1 on v0

v1 whole, which is shorter than its diff:
```python
import math

import jax
import jax.numpy as jnp
from jax import lax
from jax.sharding import Mesh, PartitionSpec as P

QUERY_HEADS = 16
KEY_VALUE_HEADS = 8
HEAD_SIZE = 128
EPS = 1e-06
THETA = 1000000.0

F32 = jnp.float32
BF16 = jnp.bfloat16
SWAP = [(0, 1), (1, 0)]
DIAGONAL = [(0, 3), (1, 2), (2, 1), (3, 0)]
TEAM = ("zl", "xl", "c")
AXES = ("zh", "zl", "y", "xh", "xl", "c")
CHUNKS = 3


def dot(left, right):
    return lax.dot_general(left, right, (((1,), (0,)), ((), ())), preferred_element_type=F32)


def dot_nt(left, right):
    return lax.dot_general(left, right, (((1,), (1,)), ((), ())), preferred_element_type=F32)


def dot_tn(left, right):
    return lax.dot_general(left, right, (((0,), (0,)), ((), ())), preferred_element_type=F32)


def from_next(value, axis, size, step):
    return lax.ppermute(value, axis, [((i + step) % size, i) for i in range(size)])


def to_next(value, axis, size, step):
    return lax.ppermute(value, axis, [(i, (i + step) % size) for i in range(size)])


class Layout:
    def __init__(self, sizes):
        self.zh, self.y, self.xh = sizes["zh"], sizes["y"], sizes["xh"]
        self.groups = self.zh * self.y * self.xh

    def relative(self, value):
        lead = value.shape[:-1]
        cut = value.shape[-1] // (self.groups * 2)
        v = value.reshape(lead + (self.zh, 2, self.y, self.xh, cut))
        n = len(lead)
        for axis, name, size in ((n, "zh", self.zh), (n + 2, "y", self.y), (n + 3, "xh", self.xh)):
            if size > 1:
                v = jnp.roll(v, -lax.axis_index(name), axis=axis)
        v = jnp.moveaxis(v, n + 1, n + 3)
        return v.reshape(value.shape)

    def natural(self, value):
        lead = value.shape[:-1]
        cut = value.shape[-1] // (self.groups * 2)
        v = value.reshape(lead + (self.zh, self.y, self.xh, 2, cut))
        n = len(lead)
        v = jnp.moveaxis(v, n + 3, n + 1)
        for axis, name, size in ((n, "zh", self.zh), (n + 2, "y", self.y), (n + 3, "xh", self.xh)):
            if size > 1:
                v = jnp.roll(v, lax.axis_index(name), axis=axis)
        return v.reshape(value.shape)

    def gather(self, block):
        found = {(0, 0, 0): block}
        for k in range(1, self.zh):
            found[k, 0, 0] = from_next(block, "zh", self.zh, k)
        for k in range(self.zh):
            for j in range(1, self.y):
                found[k, j, 0] = from_next(found[k, 0, 0], "y", self.y, j)
        for k in range(self.zh):
            for j in range(self.y):
                for i in range(1, self.xh):
                    found[k, j, i] = from_next(found[k, j, 0], "xh", self.xh, i)
        return jnp.concatenate([found[key] for key in sorted(found)], axis=0)

    def scatter(self, terms):
        rows = terms.shape[0] // self.groups
        part = {}
        for k in range(self.zh):
            for j in range(self.y):
                for i in range(self.xh):
                    at = ((k * self.y + j) * self.xh + i) * rows
                    part[k, j, i] = terms[at : at + rows]
        for k in reversed(range(self.zh)):
            for j in reversed(range(self.y)):
                for i in range(1, self.xh):
                    part[k, j, 0] = part[k, j, 0] + to_next(
                        part[k, j, i].astype(BF16), "xh", self.xh, i
                    ).astype(F32)
        for k in reversed(range(self.zh)):
            for j in range(1, self.y):
                part[k, 0, 0] = part[k, 0, 0] + to_next(
                    part[k, j, 0].astype(BF16), "y", self.y, j
                ).astype(F32)
        for k in range(1, self.zh):
            part[0, 0, 0] = part[0, 0, 0] + to_next(
                part[k, 0, 0].astype(BF16), "zh", self.zh, k
            ).astype(F32)
        return part[0, 0, 0]


def team_gather(block):
    far = lax.ppermute(block, ("zl", "xl"), DIAGONAL)
    over_z = lax.ppermute(block, "zl", SWAP)
    over_x = lax.ppermute(block, "xl", SWAP)
    half = jnp.concatenate([block, over_x, over_z, far], axis=0)
    return jnp.concatenate([half, lax.ppermute(half, "c", SWAP)], axis=0)


def team_scatter(term):
    other = lax.ppermute(term(1).astype(BF16), "c", SWAP)
    mine = term(0) + other.astype(F32)
    rows = mine.shape[0] // 4
    far = lax.ppermute(mine[3 * rows :].astype(BF16), ("zl", "xl"), DIAGONAL)
    over_z = lax.ppermute(mine[2 * rows : 3 * rows].astype(BF16), "zl", SWAP)
    over_x = lax.ppermute(mine[rows : 2 * rows].astype(BF16), "xl", SWAP)
    return mine[:rows] + over_x.astype(F32) + over_z.astype(F32) + far.astype(F32)


def exchange(value):
    return lax.all_to_all(value, TEAM, 0, 0, tiled=True)


def all_sum(value, sizes):
    for axis in ("c", "xl", "zl", "y", "xh", "zh"):
        total = value
        for k in range(1, sizes[axis]):
            total = total + from_next(value, axis, sizes[axis], k)
        value = total
    return value


def device_index(sizes):
    index = 0
    for axis in AXES:
        index = index * sizes[axis] + lax.axis_index(axis)
    return index


def inverse_rms(value):
    return lax.rsqrt(jnp.mean(value * value, axis=-1, keepdims=True) + EPS)


def norm_input_gradient(normed, inverse, e):
    return inverse * (e - normed * jnp.mean(e * normed, axis=-1, keepdims=True))


def turn(value, cosine, sine):
    half = value.shape[-1] // 2
    a, b = value[..., :half], value[..., half:]
    return jnp.concatenate([a * cosine - b * sine, b * cosine + a * sine], axis=-1)


def layer(
    sizes,
    tokens,
    doc_ids,
    w_qkv_rows,
    w_out_rows,
    w_gate_up_rows,
    w_down_rows,
    attn_gain,
    q_gain,
    k_gain,
    mlp_gain,
    out_grad,
):
    layout = Layout(sizes)
    rows = tokens.shape[1]
    width = tokens.shape[2]
    team = 8
    owned = w_qkv_rows.shape[0]
    devices = width // owned
    heads = QUERY_HEADS // team
    q_width = heads * HEAD_SIZE
    ff = w_down_rows.shape[1]
    slice_ff = ff // team
    chunk = slice_ff // CHUNKS
    scale = HEAD_SIZE ** (-0.5)
    team_tokens = team * rows

    q_cols = QUERY_HEADS * HEAD_SIZE
    kv_cols = KEY_VALUE_HEADS * HEAD_SIZE

    def per_member(value):
        return jnp.moveaxis(value.reshape(owned, team, -1), 1, 0)

    send_qkv = jnp.concatenate(
        [
            per_member(w_qkv_rows[:, :q_cols]),
            per_member(w_qkv_rows[:, q_cols : q_cols + kv_cols]),
            per_member(w_qkv_rows[:, q_cols + kv_cols :]),
        ],
        axis=2,
    )
    w_qkv = layout.gather(exchange(send_qkv).reshape(team * owned, -1))
    w_out = layout.gather(exchange(per_member(w_out_rows)).reshape(team * owned, -1))
    gate_all = w_gate_up_rows[:, 0, :].reshape(owned, team, CHUNKS, chunk)
    up_all = w_gate_up_rows[:, 1, :].reshape(owned, team, CHUNKS, chunk)
    down_all = w_down_rows.reshape(owned, team, CHUNKS, chunk)
    w_mlp = []
    for j in range(CHUNKS):
        send = jnp.concatenate(
            [jnp.moveaxis(w[:, :, j, :], 1, 0) for w in (gate_all, up_all, down_all)], axis=2
        )
        w_mlp.append(layout.gather(exchange(send).reshape(team * owned, -1)))

    gains = jnp.concatenate([attn_gain, mlp_gain, q_gain, k_gain])[None]
    table = jnp.zeros((devices, gains.shape[1]), BF16)
    table = lax.dynamic_update_slice(table, gains, (device_index(sizes), 0))
    table = all_sum(table, sizes).astype(F32)
    small = q_gain.shape[0]
    g_attn = layout.relative(table[:, :owned].reshape(1, width))
    g_mlp = layout.relative(table[:, owned : 2 * owned].reshape(1, width))
    g_q = table[:, 2 * owned : 2 * owned + small].reshape(-1)
    g_k = table[:, 2 * owned + small :].reshape(-1)

    doc_team = team_gather(doc_ids.reshape(1, rows))
    place = (
        lax.axis_index("xh") * 4
        + (lax.axis_index("xl") ^ jnp.arange(2))[None, :] * 2
        + (lax.axis_index("c") ^ jnp.arange(2))[:, None]
    )
    index_own = (place[:, :, None] * rows + jnp.arange(rows)).reshape(-1).astype(jnp.int32)

    def by_sequence(value):
        tail = value.shape[1:]
        v = value.reshape((2, 2, 2, rows) + tail)
        return jnp.moveaxis(v, 1, 0).reshape((2, 4 * rows) + tail)

    def by_core(value):
        tail = value.shape[2:]
        v = value.reshape((2, 2, 2, rows) + tail)
        return jnp.moveaxis(v, 0, 1).reshape((8 * rows,) + tail)

    def all_keys(value):
        if sizes["xh"] == 1:
            return value
        return lax.all_gather(value, "xh", axis=1, tiled=True)

    doc_q = by_sequence(doc_team.reshape(-1))
    doc_k = all_keys(doc_q)
    index_k = all_keys(jnp.broadcast_to(index_own, doc_q.shape))
    doc_start = jnp.sum((doc_k[:, None, :] < doc_q[:, :, None]).astype(jnp.int32), axis=2)
    position = (index_own - doc_start).astype(F32)
    allowed = (doc_k[:, None, :] == doc_q[:, :, None]) & (index_k[:, None, :] <= index_own[None, :, None])
    half = HEAD_SIZE // 2
    freqs = jnp.exp(jnp.arange(half).astype(F32) * (-math.log(THETA) / half))
    angle = position.reshape(2, -1, 1) * freqs
    cosine, sine = jnp.cos(angle)[:, :, None, :], jnp.sin(angle)[:, :, None, :]

    x_own = layout.relative(tokens[0])
    dy_own = layout.relative(out_grad[0])
    x_team = team_gather(x_own).astype(F32)
    normed_in = (x_team * inverse_rms(x_team) * g_attn).astype(BF16)
    projected = by_sequence(dot(normed_in, w_qkv))
    q_raw = projected[:, :, :q_width].reshape(2, -1, heads, HEAD_SIZE)
    k_raw = projected[:, :, q_width : q_width + HEAD_SIZE].reshape(2, -1, 1, HEAD_SIZE)
    value_own = projected[:, :, q_width + HEAD_SIZE :].astype(BF16)
    q_inverse, k_inverse = inverse_rms(q_raw), inverse_rms(k_raw)
    q_normed, k_normed = q_raw * q_inverse, k_raw * k_inverse
    queries = turn(q_normed * g_q, cosine, sine).astype(BF16)
    keys_own = turn(k_normed * g_k, cosine, sine).astype(BF16)[:, :, 0]
    keys, values = all_keys(keys_own), all_keys(value_own)
    queries = jnp.moveaxis(queries, 2, 1)

    def pair(left, right, spec):
        return jnp.einsum(spec, left, right, preferred_element_type=F32)

    scores = jnp.where(allowed[:, None], pair(queries, keys, "shqd,skd->shqk") * scale, -1e9)
    peak = jnp.max(scores, axis=-1, keepdims=True)
    weights_exp = jnp.exp(scores - peak)
    probs = weights_exp / jnp.sum(weights_exp, axis=-1, keepdims=True)
    probs_b = probs.astype(BF16)
    attended = pair(probs_b, values, "shqk,skd->sqhd").astype(BF16)
    attended = by_core(attended.reshape(2, -1, q_width))

    cut = team_tokens // 2

    def of_core(value, which):
        return value[which * cut : (which + 1) * cut]

    branch = team_scatter(lambda which: dot_nt(of_core(attended, which), w_out))
    middle = x_own.astype(F32) + branch
    mid_inverse = inverse_rms(middle)
    mid_normed = middle * mid_inverse

    nm = team_gather((mid_normed * g_mlp).astype(BF16))
    dy = team_gather(dy_own)
    hidden, d_gate_up = [], []
    grads_mlp = []
    for j in range(CHUNKS):
        w = w_mlp[j]
        gate, upward = dot(nm, w[:, :chunk]), dot(nm, w[:, chunk : 2 * chunk])
        d_hidden = dot(dy, w[:, 2 * chunk :])
        sigma = jax.nn.sigmoid(gate)
        silu = gate * sigma
        hidden.append((silu * upward).astype(BF16))
        d_gate = (d_hidden * upward * (sigma * (1.0 + gate * (1.0 - sigma)))).astype(BF16)
        d_up = (d_hidden * silu).astype(BF16)
        d_gate_up.append(jnp.concatenate([d_gate, d_up], axis=1))
        terms = jnp.concatenate([dot_tn(nm, d_gate_up[j]), dot_tn(dy, hidden[j])], axis=1)
        grads_mlp.append(layout.scatter(terms))

    def sum_chunks(part):
        total = part(0)
        for j in range(1, CHUNKS):
            total = total + part(j)
        return total

    d_normed_mid = team_scatter(
        lambda which: sum_chunks(lambda j: dot_nt(of_core(d_gate_up[j], which), w_mlp[j][:, : 2 * chunk]))
    )
    output = middle + team_scatter(
        lambda which: sum_chunks(lambda j: dot_nt(of_core(hidden[j], which), w_mlp[j][:, 2 * chunk :]))
    )
    d_middle = dy_own.astype(F32) + norm_input_gradient(mid_normed, mid_inverse, d_normed_mid * g_mlp)

    d_branch = team_gather(d_middle.astype(BF16))
    grad_out_sum = layout.scatter(dot_tn(d_branch, attended))
    d_attended = by_sequence(dot(d_branch, w_out).astype(BF16)).reshape(2, -1, heads, HEAD_SIZE)
    d_attended = jnp.moveaxis(d_attended, 2, 1)
    d_probs = pair(d_attended, values, "shqd,skd->shqk")
    row_dot = jnp.sum(probs * d_probs, axis=-1, keepdims=True)
    d_raw = (probs * (d_probs - row_dot) * scale).astype(BF16)
    d_queries = pair(d_raw, keys, "shqk,skd->sqhd").astype(BF16).astype(F32)
    d_keys = pair(d_raw, queries, "shqk,shqd->skd").astype(BF16)
    d_values = pair(probs_b, d_attended, "shqk,shqd->skd").astype(BF16)
    if sizes["xh"] > 1:
        d_keys = lax.psum_scatter(d_keys, "xh", scatter_dimension=1, tiled=True)
        d_values = lax.psum_scatter(d_values, "xh", scatter_dimension=1, tiled=True)
    d_q_rot = turn(d_queries, cosine, -sine)
    d_k_rot = turn(d_keys.astype(F32)[:, :, None], cosine, -sine)
    head_gains = jnp.stack(
        [jnp.sum(d_q_rot * q_normed, axis=(0, 1, 2)), jnp.sum(d_k_rot * k_normed, axis=(0, 1, 2))]
    )
    head_gains = all_sum(head_gains, sizes)
    d_q = norm_input_gradient(q_normed, q_inverse, d_q_rot * g_q)
    d_k = norm_input_gradient(k_normed, k_inverse, d_k_rot * g_k)
    d_projected = jnp.concatenate(
        [d_q.reshape(2, -1, q_width), d_k[:, :, 0], d_values.astype(F32)], axis=2
    ).astype(BF16)
    d_projected = by_core(d_projected)
    grad_qkv_sum = layout.scatter(dot_tn(normed_in, d_projected))
    d_normed_in = team_scatter(lambda which: dot_nt(of_core(d_projected, which), w_qkv))
    x_own = x_own.astype(F32)
    x_inverse = inverse_rms(x_own)
    token_grad = d_middle + norm_input_gradient(x_own * x_inverse, x_inverse, d_normed_in * g_attn)

    def to_owner(total):
        return exchange(total.astype(BF16).reshape(team, owned, -1)).astype(F32)

    def side_by_side(value):
        return jnp.moveaxis(value, 0, 1).reshape(owned, -1)

    back = to_owner(grad_qkv_sum)
    grad_qkv = jnp.concatenate(
        [
            side_by_side(back[:, :, :q_width]),
            side_by_side(back[:, :, q_width : q_width + HEAD_SIZE]),
            side_by_side(back[:, :, q_width + HEAD_SIZE :]),
        ],
        axis=1,
    )
    grad_out = side_by_side(to_owner(grad_out_sum))
    backs = jnp.stack([to_owner(g) for g in grads_mlp], axis=2)
    grad_gate_up = jnp.stack(
        [side_by_side(backs[..., i * chunk : (i + 1) * chunk].reshape(team, owned, -1)) for i in (0, 1)], axis=1
    )
    grad_down = side_by_side(backs[..., 2 * chunk :].reshape(team, owned, -1))
    grad_attn_gain = jnp.sum(grad_qkv * w_qkv_rows.astype(F32), axis=1) / attn_gain.astype(F32)
    grad_mlp_gain = jnp.sum(grad_gate_up * w_gate_up_rows.astype(F32), axis=(1, 2)) / mlp_gain.astype(F32)
    at = device_index(sizes) * small
    grad_q_gain = lax.dynamic_slice(head_gains[0], (at,), (small,))
    grad_k_gain = lax.dynamic_slice(head_gains[1], (at,), (small,))
    return (
        layout.natural(output.astype(BF16))[None],
        layout.natural(token_grad.astype(BF16))[None],
        grad_qkv,
        grad_out,
        grad_gate_up,
        grad_down,
        grad_attn_gain,
        grad_q_gain,
        grad_k_gain,
        grad_mlp_gain,
    )


def solution(mesh):
    dp, seq = mesh.shape["dp"], mesh.shape["seq"]
    fine = Mesh(mesh.devices.reshape(dp // 4, 2, 2, seq // 4, 2, 2), AXES)
    sizes = dict(fine.shape)
    dp_axes, seq_axes = ("zh", "zl", "y"), ("xh", "xl", "c")
    token, weight, vector = P(dp_axes, seq_axes, None), P(AXES, None), P(AXES)
    wide = P(AXES, None, None)

    def shards(*args):
        return layer(sizes, *args)

    return jax.shard_map(
        shards,
        mesh=fine,
        in_specs=(token, P(dp_axes, seq_axes), weight, weight, wide, weight, vector, vector, vector, vector, token),
        out_specs=(token, token, weight, weight, wide, weight, vector, vector, vector, vector),
        check_vma=False,
    )
```

time: 2750 us -> 876 us (0.32)
  waiting for transfers between devices: 2240 us -> 384 us
  matrix products: 245 us -> 121 us
  starting transfers between devices: 0.87 us -> 109 us
  local copies, waits for them, and re-layouts: 30.8 us -> 133 us
  blocking collectives: 88.6 us -> 0 us
    reduce_scatter x4 -> x0, waiting for transfers between devices: 1670 us -> none  [the longest x1 1130 us: flat_layer(): lax.psum_scatter(jnp.stack([gate_rows, up_rows, down_rows], axis=1), ('dp...]
    all_gather x6 -> x0, waiting for transfers between devices: 568 us -> none  [the longest x1 271 us: flat_layer(): lax.all_gather(gate_up_weight, ('dp', 'seq'), axis=0, tiled=True)]
    ppermute x0 -> x76, waiting for transfers between devices: none -> 346 us  [the longest x15 120 us: to_next(): lax.ppermute(value, axis, [(i, (i + step) % size) for i in range(size)])]
    dot_general x21 -> x40, matrix products: 245 us -> 115 us  [the longest x16 50.8 us: dot_nt(): lax.dot_general(left, right, (((1,), (1,)), ((), ())), preferred_element_...]
    unnamed x2 -> x0, blocking collectives: 83 us -> none
    ppermute x0 -> x76, starting transfers between devices: none -> 70.1 us  [the longest x25 17.7 us: from_next(): lax.ppermute(value, axis, [((i + step) % size, i) for i in range(size)])]
    another operation x5 -> x9, other arithmetic: 101 us -> 31.5 us  [the longest x1 97.5 us: flat_layer(): jnp.stack([gate_rows, up_rows, down_rows], axis=1)]
    all_to_all x0 -> x10, starting transfers between devices: none -> 38.7 us  [exchange(): return lax.all_to_all(value, TEAM, 0, 0, tiled=True)]
  transfers between devices with their start and end apart: 11 -> 86, of which waited for: 9 -> 37; matrix products, arithmetic and copies ran while one was open for 11% -> 28% of each run, Pallas kernels for 0% -> 0%
where the time goes in v1:
time: 876 us; the launch traced here: 868 us
  waiting for transfers between devices  384 us (44%)
  local copies, waits for them, and re-layouts  133 us (15%)
  matrix products  121 us (14%)
  other arithmetic  119 us (14%)
  starting transfers between devices  109 us (12%)
    ppermute x15, waiting for transfers between devices, to_next(): lax.ppermute(value, axis, [(i, (i + step) % size) for i in range(size)])  120 us
    ppermute x25, waiting for transfers between devices, from_next(): lax.ppermute(value, axis, [((i + step) % size, i) for i in range(size)])  111 us
    dot_general x16, matrix products, dot_nt(): lax.dot_general(left, right, (((1,), (1,)), ((), ())), preferred_element_...  50.8 us
    all_to_all x10, starting transfers between devices, exchange(): return lax.all_to_all(value, TEAM, 0, 0, tiled=True)  38.7 us
    all_to_all x10, waiting for transfers between devices, exchange(): return lax.all_to_all(value, TEAM, 0, 0, tiled=True)  38 us
    unnamed x226, local copies, waits for them, and re-layouts  35.2 us
    ppermute x4, waiting for transfers between devices, team_scatter(): far = lax.ppermute(mine[3 * rows:].astype(BF16), ('zl', 'xl'), DIAGONAL)  34.4 us
    ppermute x4, waiting for transfers between devices, team_scatter(): over_z = lax.ppermute(mine[2 * rows:3 * rows].astype(BF16), 'zl', SWAP)  33.6 us
  transfers between devices with their start and end apart: 86, of which 37 were waited for; matrix products, arithmetic and copies ran while one was open for 28% of the time, Pallas kernels for 0%

profile of v1, /device:TPU:0, one launch (start us, length us, event | category | flops | bytes accessed | tf_op | source)
XLA Modules:
  0.0 868.3 jit_solution(3178915938458392268)
XLA Ops:
  33.9 7.3 slice_reduce_fusion.1
  54.4 7.4 collective-permute-done.5
  83.4 8.7 %all-to-all-done = bf16[8,64,512]{2,1,0:T(8,128)(2,1)} async-done(((bf16[8,64,512]{2,1,0:T(8,128)(2,1)}), bf16[8,64,512]{2,1,0:T(8,128)(2,1)}, u32[]{:S(2)}, u32[]{:S(2)}) %all-to-all-start) | async-done | bytes 524320 | tf_op jit(solution)/shard_map/all_to_all | solution.py:128
  97.8 12.0 %collective-permute-done.17 = bf16[512,256]{1,0:T(8,128)(2,1)} collective-permute-done((bf16[512,256]{1,0:T(8,128)(2,1)}, bf16[512,256]{1,0:T(8,128)(2,1)}, u32[]{:S(2)}, u32[]{:S(2)}) %collective-permute-start.17) | collective-permute-done | bytes 262176 | tf_op jit(solution)/shard_map/ppermute | solution.py:36
  111.8 8.6 collective-permute-done.10
  130.5 9.4 %collective-permute-done.11 = bf16[512,512]{1,0:T(8,128)(2,1)S(1)} collective-permute-done((bf16[512,512]{1,0:T(8,128)(2,1)S(1)}, bf16[512,512]{1,0:T(8,128)(2,1)S(1)}, u32[]{:S(2)}, u32[]{:S(2)}) %collective-permute-start.11) | collective-permute-done | bytes 524320 | tf_op jit(solution)/shard_map/ppermute | solution.py:36
  210.0 7.5 collective-permute-done.42
  220.9 20.9 %all-to-all-done.3 = bf16[8,64,768]{2,1,0:T(8,128)(2,1)S(1)} async-done(((bf16[8,64,768]{2,1,0:T(8,128)(2,1)}), bf16[8,64,768]{2,1,0:T(8,128)(2,1)S(1)}, u32[]{:S(2)}, u32[]{:S(2)}) %all-to-all-start.3) | async-done | bytes 786464 | tf_op jit(solution)/shard_map/all_to_all | solution.py:128
  245.3 8.7 %collective-permute-done.22 = bf16[128,2048]{1,0:T(8,128)(2,1)} collective-permute-done((bf16[128,2048]{1,0:T(8,128)(2,1)}, bf16[128,2048]{1,0:T(8,128)(2,1)}, u32[]{:S(2)}, u32[]{:S(2)}) %collective-permute-start.22) | collective-permute-done | bytes 524320 | tf_op jit(solution)/shard_map/ppermute | solution.py:121
  254.0 10.3 %collective-permute-done.21 = bf16[128,2048]{1,0:T(8,128)(2,1)} collective-permute-done((bf16[128,2048]{1,0:T(8,128)(2,1)}, bf16[128,2048]{1,0:T(8,128)(2,1)}, u32[]{:S(2)}, u32[]{:S(2)}) %collective-permute-start.21) | collective-permute-done | bytes 524320 | tf_op jit(solution)/shard_map/ppermute | solution.py:122
  272.4 9.2 %collective-permute-done.23 = bf16[128,2048]{1,0:T(8,128)(2,1)S(1)} collective-permute-done((bf16[128,2048]{1,0:T(8,128)(2,1)S(1)}, bf16[128,2048]{1,0:T(8,128)(2,1)S(1)}, u32[]{:S(2)}, u32[]{:S(2)}) %collective-permute-start.23) | collective-permute-done | bytes 524320 | tf_op jit(solution)/shard_map/ppermute | solution.py:112
  282.5 12.5 %collective-permute-done.24 = bf16[128,2048]{1,0:T(8,128)(2,1)} collective-permute-done((bf16[128,2048]{1,0:T(8,128)(2,1)S(1)}, bf16[128,2048]{1,0:T(8,128)(2,1)}, u32[]{:S(2)}, u32[]{:S(2)}) %collective-permute-start.24) | collective-permute-done | bytes 524320 | tf_op jit(solution)/shard_map/ppermute | solution.py:111
  295.0 11.3 %collective-permute-done.25 = bf16[128,2048]{1,0:T(8,128)(2,1)} collective-permute-done((bf16[128,2048]{1,0:T(8,128)(2,1)S(1)}, bf16[128,2048]{1,0:T(8,128)(2,1)}, u32[]{:S(2)}, u32[]{:S(2)}) %collective-permute-start.25) | collective-permute-done | bytes 524320 | tf_op jit(solution)/shard_map/ppermute | solution.py:110
  312.0 25.6 %collective-permute-done.31 = bf16[512,768]{1,0:T(8,128)(2,1)} collective-permute-done((bf16[512,768]{1,0:T(8,128)(2,1)S(1)}, bf16[512,768]{1,0:T(8,128)(2,1)}, u32[]{:S(2)}, u32[]{:S(2)}) %collective-permute-start.31) | collective-permute-done | bytes 786464 | tf_op jit(solution)/shard_map/ppermute | solution.py:36
  338.1 13.8 %collective-permute-done.34 = bf16[512,768]{1,0:T(8,128)(2,1)S(1)} collective-permute-done((bf16[512,768]{1,0:T(8,128)(2,1)S(1)}, bf16[512,768]{1,0:T(8,128)(2,1)S(1)}, u32[]{:S(2)}, u32[]{:S(2)}) %collective-permute-start.34) | collective-permute-done | bytes 786464 | tf_op jit(solution)/shard_map/ppermute | solution.py:36
  366.9 10.6 %collective-permute-done.33 = bf16[512,768]{1,0:T(8,128)(2,1)S(1)} collective-permute-done((bf16[512,768]{1,0:T(8,128)(2,1)S(1)}, bf16[512,768]{1,0:T(8,128)(2,1)S(1)}, u32[]{:S(2)}, u32[]{:S(2)}) %collective-permute-start.33) | collective-permute-done | bytes 786464 | tf_op jit(solution)/shard_map/ppermute | solution.py:36
  377.5 15.5 %collective-permute-done.35 = bf16[512,768]{1,0:T(8,128)(2,1)S(1)} collective-permute-done((bf16[512,768]{1,0:T(8,128)(2,1)S(1)}, bf16[512,768]{1,0:T(8,128)(2,1)S(1)}, u32[]{:S(2)}, u32[]{:S(2)}) %collective-permute-start.35) | collective-permute-done | bytes 786464 | tf_op jit(solution)/shard_map/ppermute | solution.py:36
  480.7 31.7 %collective-permute-done.66 = bf16[512,768]{0,1:T(8,128)(2,1)} collective-permute-done((bf16[512,768]{0,1:T(8,128)(2,1)}, bf16[512,768]{0,1:T(8,128)(2,1)}, u32[]{:S(2)}, u32[]{:S(2)}) %collective-permute-start.66) | collective-permute-done | bytes 786464 | tf_op jit(solution)/shard_map/ppermute | solution.py:40
  520.5 25.2 %collective-permute-done.63 = bf16[512,768]{0,1:T(8,128)(2,1)S(1)} collective-permute-done((bf16[512,768]{0,1:T(8,128)(2,1)S(1)}, bf16[512,768]{0,1:T(8,128)(2,1)S(1)}, u32[]{:S(2)}, u32[]{:S(2)}) %collective-permute-start.63) | collective-permute-done | bytes 786464 | tf_op jit(solution)/shard_map/ppermute | solution.py:40
  546.9 18.8 %collective-permute-done.70 = bf16[512,768]{0,1:T(8,128)(2,1)S(1)} collective-permute-done((bf16[512,768]{0,1:T(8,128)(2,1)S(1)}, bf16[512,768]{0,1:T(8,128)(2,1)S(1)}, u32[]{:S(2)}, u32[]{:S(2)}) %collective-permute-start.70) | collective-permute-done | bytes 786464 | tf_op jit(solution)/shard_map/ppermute | solution.py:40
  573.0 9.7 %collective-permute-done.67 = bf16[512,768]{0,1:T(8,128)(2,1)} collective-permute-done((bf16[512,768]{0,1:T(8,128)(2,1)}, bf16[512,768]{0,1:T(8,128)(2,1)}, u32[]{:S(2)}, u32[]{:S(2)}) %collective-permute-start.67) | collective-permute-done | bytes 786464 | tf_op jit(solution)/shard_map/ppermute | solution.py:40
  588.0 9.5 %fusion.237 = (bf16[512,2048]{1,0:T(8,128)(2,1)S(1)}, f32[512,2048]{1,0:T(8,128)}) fusion(bf16[512,2048]{1,0:T(8,128)(2,1)} %collective-permute-done.44, f32[512,2048]{1,0:T(8,128)} %fusion.25, f32[512,2048]{1,0:T(8,128)} %fusion.35, f32[512,2048]{1,0:T(8,128)} %fusion.31), kind=kLoop, calls=%fused_computation.418 | loop fusion | flops 5242880 | bytes 20971520 | tf_op jit(solution)/shard_map/convert.29
  606.5 9.4 %fusion.238 = (bf16[512,2048]{1,0:T(8,128)(2,1)S(1)}, f32[512,2048]{1,0:T(8,128)}) fusion(bf16[512,2048]{1,0:T(8,128)(2,1)} %collective-permute-done.36, f32[512,2048]{1,0:T(8,128)} %fusion.136, f32[512,2048]{1,0:T(8,128)} %fusion.150, f32[512,2048]{1,0:T(8,128)} %fusion.144), kind=kLoop, calls=%fused_computation.419 | loop fusion | flops 5242880 | bytes 20971520 | tf_op jit(solution)/shard_map/convert.32
  618.6 8.0 collective-permute-done.47
  639.5 8.0 all-to-all-done.8
  657.7 12.2 %collective-permute-done.38 = bf16[128,2048]{1,0:T(8,128)(2,1)} collective-permute-done((bf16[128,2048]{1,0:T(8,128)(2,1)}, bf16[128,2048]{1,0:T(8,128)(2,1)}, u32[]{:S(2)}, u32[]{:S(2)}) %collective-permute-start.38) | collective-permute-done | bytes 524320 | tf_op jit(solution)/shard_map/ppermute | solution.py:122
  720.5 8.9 %fusion.84 = f32[2,512,1,128]{3,1,0,2:T(8,128)} fusion(f32[2,2,512,512]{2,3,1,0:T(8,128)} %fusion.195, bf16[2,512,2,64]{3,1,2,0:T(8,128)(2,1)} %get-tuple-element.140, bf16[2,512,2,64]{3,1,2,0:T(8,128)(2,1)S(1)} %copy-done.51, f32[2,2,512,512]{2,3,1,0:T(8,128)} %get-tuple-element.180, f32[2,2,512]{2,1,0:T(2,128)S(1)} %copy-done.97), kind=kOutput, calls=%fused_computation.129 | convolution fusion | flops 277088768 | bytes 9445376 | tf_op jit(solution)/shard_map/shqk,shqd->skd/dot_general | solution.py:275
  764.7 12.8 %collective-permute-done.60 = bf16[512,256]{1,0:T(8,128)(2,1)S(1)} collective-permute-done((bf16[512,256]{1,0:T(8,128)(2,1)S(1)}, bf16[512,256]{1,0:T(8,128)(2,1)S(1)}, u32[]{:S(2)}, u32[]{:S(2)}) %collective-permute-start.60) | collective-permute-done | bytes 262176 | tf_op jit(solution)/shard_map/ppermute | solution.py:40
  781.5 11.6 %collective-permute-done.59 = bf16[512,256]{1,0:T(8,128)(2,1)S(1)} collective-permute-done((bf16[512,256]{1,0:T(8,128)(2,1)S(1)}, bf16[512,256]{1,0:T(8,128)(2,1)S(1)}, u32[]{:S(2)}, u32[]{:S(2)}) %collective-permute-start.59) | collective-permute-done | bytes 262176 | tf_op jit(solution)/shard_map/ppermute | solution.py:40
  793.1 8.0 collective-permute-done.61
  840.0 11.2 %collective-permute-done.55 = bf16[128,2048]{1,0:T(8,128)(2,1)S(1)} collective-permute-done((bf16[128,2048]{1,0:T(8,128)(2,1)S(1)}, bf16[128,2048]{1,0:T(8,128)(2,1)S(1)}, u32[]{:S(2)}, u32[]{:S(2)}) %collective-permute-start.55) | collective-permute-done | bytes 524320 | tf_op jit(solution)/shard_map/ppermute | solution.py:121
  851.3 11.0 %collective-permute-done.54 = bf16[128,2048]{1,0:T(8,128)(2,1)S(1)} collective-permute-done((bf16[128,2048]{1,0:T(8,128)(2,1)S(1)}, bf16[128,2048]{1,0:T(8,128)(2,1)S(1)}, u32[]{:S(2)}, u32[]{:S(2)}) %collective-permute-start.54) | collective-permute-done | bytes 524320 | tf_op jit(solution)/shard_map/ppermute | solution.py:122
  (594 shorter events, 470.1 us)
Async XLA Ops:
  10.9 56.3 %collective-permute-start = (bf16[128,2048]{1,0:T(8,128)(2,1)S(1)}, bf16[128,2048]{1,0:T(8,128)(2,1)}, u32[]{:S(2)}, u32[]{:S(2)}) collective-permute-start(bf16[128,2048]{1,0:T(8,128)(2,1)S(1)} %reshape.362), channel_id=1, source_target_pairs={{0,2},{2,0},{1,3},{3,1},{4,6},{6,4},{5,7},{7,5},{8,10},{10,8},{9,1... | collective-permute-start | bytes 1572872 | tf_op jit(solution)/shard_map/ppermute | solution.py:112
  13.9 53.3 %collective-permute-start.1 = (bf16[128,2048]{1,0:T(8,128)(2,1)S(1)}, bf16[128,2048]{1,0:T(8,128)(2,1)}, u32[]{:S(2)}, u32[]{:S(2)}) collective-permute-start(bf16[128,2048]{1,0:T(8,128)(2,1)S(1)} %reshape.362), channel_id=1, source_target_pairs={{0,8},{8,0},{1,9},{9,1},{2,10},{10,2},{3,11},{11,3},{4,12},{12,4},... | collective-permute-start | bytes 1572872 | tf_op jit(solution)/shard_map/ppermute | solution.py:111
  19.7 56.7 %all-to-all-start.1 = ((bf16[8,64,256]{2,1,0:T(8,128)(2,1)}), bf16[8,64,256]{2,1,0:T(8,128)(2,1)}, u32[]{:S(2)}, u32[]{:S(2)}) async-start(bf16[8,64,256]{2,1,0:T(8,128)(2,1)} %copy.367), calls=%async_computation.1 | async-start | bytes 524288 | tf_op jit(solution)/shard_map/all_to_all | solution.py:128
  70.7 50.3 %collective-permute-start.3 = (bf16[512,2048]{1,0:T(8,128)(2,1)}, bf16[512,2048]{1,0:T(8,128)(2,1)S(1)}, u32[]{:S(2)}, u32[]{:S(2)}) collective-permute-start(bf16[512,2048]{1,0:T(8,128)(2,1)} %pad_maximum_fusion.6), channel_id=1, source_target_pairs={{0,1},{1,0},{2,3},{3,2},{4,5},{5,4},{6,7},{7,6},{8,9},{9,8},{10,11... | collective-permute-start | bytes 6291464 | tf_op jit(solution)/shard_map/ppermute | solution.py:114
  82.9 88.1 %collective-permute-start.16 = (bf16[512,256]{1,0:T(8,128)(2,1)}, bf16[512,256]{1,0:T(8,128)(2,1)}, u32[]{:S(2)}, u32[]{:S(2)}) collective-permute-start(bf16[512,256]{1,0:T(8,128)(2,1)} %bitcast.23), channel_id=1, source_target_pairs={{4,0},{0,4},{5,1},{1,5},{6,2},{2,6},{7,3},{3,7},{12,8},{8,12},{13,... | collective-permute-start | bytes 786440 | tf_op jit(solution)/shard_map/ppermute | solution.py:36
  109.8 61.2 %collective-permute-start.18 = (bf16[512,256]{1,0:T(8,128)(2,1)}, bf16[512,256]{1,0:T(8,128)(2,1)}, u32[]{:S(2)}, u32[]{:S(2)}) collective-permute-start(bf16[512,256]{1,0:T(8,128)(2,1)} %collective-permute-done.17), channel_id=1, source_target_pairs={{4,0},{0,4},{5,1},{1,5},{6,2},{2,6},{7,3},{3,7},{12,8},{8,12},{13,... | collective-permute-start | bytes 786440 | tf_op jit(solution)/shard_map/ppermute | solution.py:36
  195.1 46.6 %all-to-all-start.3 = ((bf16[8,64,768]{2,1,0:T(8,128)(2,1)}), bf16[8,64,768]{2,1,0:T(8,128)(2,1)S(1)}, u32[]{:S(2)}, u32[]{:S(2)}) async-start(bf16[8,64,768]{2,1,0:T(8,128)(2,1)} %copy.371), calls=%async_computation.3 | async-start | bytes 1572864 | tf_op jit(solution)/shard_map/all_to_all | solution.py:128
  205.2 48.8 %collective-permute-start.22 = (bf16[128,2048]{1,0:T(8,128)(2,1)}, bf16[128,2048]{1,0:T(8,128)(2,1)}, u32[]{:S(2)}, u32[]{:S(2)}) collective-permute-start(bf16[128,2048]{1,0:T(8,128)(2,1)} %get-tuple-element.137), channel_id=1, source_target_pairs={{0,10},{2,8},{8,2},{10,0},{1,11},{3,9},{9,3},{11,1},{4,14},{6,12},... | collective-permute-start | bytes 1572872 | tf_op jit(solution)/shard_map/ppermute | solution.py:121
  208.2 56.2 %collective-permute-start.21 = (bf16[128,2048]{1,0:T(8,128)(2,1)}, bf16[128,2048]{1,0:T(8,128)(2,1)}, u32[]{:S(2)}, u32[]{:S(2)}) collective-permute-start(bf16[128,2048]{1,0:T(8,128)(2,1)} %get-tuple-element.138), channel_id=1, source_target_pairs={{0,8},{8,0},{1,9},{9,1},{2,10},{10,2},{3,11},{11,3},{4,12},{12,4},... | collective-permute-start | bytes 1572872 | tf_op jit(solution)/shard_map/ppermute | solution.py:122
  208.7 55.6 %collective-permute-start.20 = (bf16[128,2048]{1,0:T(8,128)(2,1)}, bf16[128,2048]{1,0:T(8,128)(2,1)}, u32[]{:S(2)}, u32[]{:S(2)}) collective-permute-start(bf16[128,2048]{1,0:T(8,128)(2,1)} %get-tuple-element.136), channel_id=1, source_target_pairs={{0,2},{2,0},{1,3},{3,1},{4,6},{6,4},{5,7},{7,5},{8,10},{10,8},{9,1... | collective-permute-start | bytes 1572872 | tf_op jit(solution)/shard_map/ppermute | solution.py:123
  220.4 132.6 %collective-permute-start.43 = (bf16[512,2048]{1,0:T(8,128)(2,1)}, bf16[512,2048]{1,0:T(8,128)(2,1)}, u32[]{:S(2)}, u32[]{:S(2)}) collective-permute-start(bf16[512,2048]{1,0:T(8,128)(2,1)} %pad_maximum_fusion.9), channel_id=1, source_target_pairs={{0,1},{1,0},{2,3},{3,2},{4,5},{5,4},{6,7},{7,6},{8,9},{9,8},{10,11... | collective-permute-start | bytes 6291464 | tf_op jit(solution)/shard_map/ppermute | solution.py:114
  220.4 51.6 %collective-permute-start.28 = (bf16[512,768]{1,0:T(8,128)(2,1)S(1)}, bf16[512,768]{1,0:T(8,128)(2,1)}, u32[]{:S(2)}, u32[]{:S(2)}) collective-permute-start(bf16[512,768]{1,0:T(8,128)(2,1)S(1)} %bitcast.298), channel_id=1, source_target_pairs={{16,0},{0,16},{17,1},{1,17},{18,2},{2,18},{19,3},{3,19},{20,4},{4,... | collective-permute-start | bytes 2359304 | tf_op jit(solution)/shard_map/ppermute | solution.py:36
  282.4 55.2 %collective-permute-start.31 = (bf16[512,768]{1,0:T(8,128)(2,1)S(1)}, bf16[512,768]{1,0:T(8,128)(2,1)}, u32[]{:S(2)}, u32[]{:S(2)}) collective-permute-start(bf16[512,768]{1,0:T(8,128)(2,1)S(1)} %bitcast.301), channel_id=1, source_target_pairs={{16,0},{0,16},{17,1},{1,17},{18,2},{2,18},{19,3},{3,19},{20,4},{4,... | collective-permute-start | bytes 2359304 | tf_op jit(solution)/shard_map/ppermute | solution.py:36
  294.9 56.9 %collective-permute-start.34 = (bf16[512,768]{1,0:T(8,128)(2,1)S(1)}, bf16[512,768]{1,0:T(8,128)(2,1)S(1)}, u32[]{:S(2)}, u32[]{:S(2)}) collective-permute-start(bf16[512,768]{1,0:T(8,128)(2,1)S(1)} %bitcast.304), channel_id=1, source_target_pairs={{16,0},{0,16},{17,1},{1,17},{18,2},{2,18},{19,3},{3,19},{20,4},{4,... | collective-permute-start | bytes 2359304 | tf_op jit(solution)/shard_map/ppermute | solution.py:36
  306.2 47.3 %collective-permute-start.29 = (bf16[512,768]{1,0:T(8,128)(2,1)}, bf16[512,768]{1,0:T(8,128)(2,1)S(1)}, u32[]{:S(2)}, u32[]{:S(2)}) collective-permute-start(bf16[512,768]{1,0:T(8,128)(2,1)} %collective-permute-done.28), channel_id=1, source_target_pairs={{4,0},{0,4},{5,1},{1,5},{6,2},{2,6},{7,3},{3,7},{12,8},{8,12},{13,... | collective-permute-start | bytes 2359304 | tf_op jit(solution)/shard_map/ppermute | solution.py:36
  310.4 49.1 %collective-permute-start.30 = (bf16[512,768]{1,0:T(8,128)(2,1)S(1)}, bf16[512,768]{1,0:T(8,128)(2,1)S(1)}, u32[]{:S(2)}, u32[]{:S(2)}) collective-permute-start(bf16[512,768]{1,0:T(8,128)(2,1)S(1)} %bitcast.302), channel_id=1, source_target_pairs={{4,0},{0,4},{5,1},{1,5},{6,2},{2,6},{7,3},{3,7},{12,8},{8,12},{13,... | collective-permute-start | bytes 2359304 | tf_op jit(solution)/shard_map/ppermute | solution.py:36
  451.6 136.4 %collective-permute-start.44 = (bf16[512,2048]{1,0:T(8,128)(2,1)}, bf16[512,2048]{1,0:T(8,128)(2,1)}, u32[]{:S(2)}, u32[]{:S(2)}) collective-permute-start(bf16[512,2048]{1,0:T(8,128)(2,1)} %add_convert_fusion), channel_id=1, source_target_pairs={{0,1},{1,0},{2,3},{3,2},{4,5},{5,4},{6,7},{7,6},{8,9},{9,8},{10,11... | collective-permute-start | bytes 6291464 | tf_op jit(solution)/shard_map/ppermute | solution.py:118
  458.6 56.2 %collective-permute-start.68 = (bf16[512,768]{0,1:T(8,128)(2,1)}, bf16[512,768]{0,1:T(8,128)(2,1)}, u32[]{:S(2)}, u32[]{:S(2)}) collective-permute-start(bf16[512,768]{0,1:T(8,128)(2,1)} %get-tuple-element.110), channel_id=1, source_target_pairs={{0,4},{4,0},{1,5},{5,1},{2,6},{6,2},{3,7},{7,3},{8,12},{12,8},{9,1... | collective-permute-start | bytes 2359304 | tf_op jit(solution)/shard_map/ppermute | solution.py:40
  466.5 45.9 %collective-permute-start.66 = (bf16[512,768]{0,1:T(8,128)(2,1)}, bf16[512,768]{0,1:T(8,128)(2,1)}, u32[]{:S(2)}, u32[]{:S(2)}) collective-permute-start(bf16[512,768]{0,1:T(8,128)(2,1)} %get-tuple-element.109), channel_id=1, source_target_pairs={{0,4},{4,0},{1,5},{5,1},{2,6},{6,2},{3,7},{7,3},{8,12},{12,8},{9,1... | collective-permute-start | bytes 2359304 | tf_op jit(solution)/shard_map/ppermute | solution.py:40
  467.0 105.9 %collective-permute-start.65 = (bf16[512,768]{0,1:T(8,128)(2,1)}, bf16[512,768]{0,1:T(8,128)(2,1)}, u32[]{:S(2)}, u32[]{:S(2)}) collective-permute-start(bf16[512,768]{0,1:T(8,128)(2,1)} %get-tuple-element.108), channel_id=1, source_target_pairs={{0,4},{4,0},{1,5},{5,1},{2,6},{6,2},{3,7},{7,3},{8,12},{12,8},{9,1... | collective-permute-start | bytes 2359304 | tf_op jit(solution)/shard_map/ppermute | solution.py:40
  478.7 66.9 %collective-permute-start.63 = (bf16[512,768]{0,1:T(8,128)(2,1)S(1)}, bf16[512,768]{0,1:T(8,128)(2,1)S(1)}, u32[]{:S(2)}, u32[]{:S(2)}) collective-permute-start(bf16[512,768]{0,1:T(8,128)(2,1)S(1)} %get-tuple-element.107), channel_id=1, source_target_pairs={{0,4},{4,0},{1,5},{5,1},{2,6},{6,2},{3,7},{7,3},{8,12},{12,8},{9,1... | collective-permute-start | bytes 2359304 | tf_op jit(solution)/shard_map/ppermute | solution.py:40
  512.4 53.3 %collective-permute-start.70 = (bf16[512,768]{0,1:T(8,128)(2,1)S(1)}, bf16[512,768]{0,1:T(8,128)(2,1)S(1)}, u32[]{:S(2)}, u32[]{:S(2)}) collective-permute-start(bf16[512,768]{0,1:T(8,128)(2,1)S(1)} %fusion.43), channel_id=1, source_target_pairs={{0,16},{16,0},{1,17},{17,1},{2,18},{18,2},{3,19},{19,3},{4,20},{20... | collective-permute-start | bytes 2359304 | tf_op jit(solution)/shard_map/ppermute | solution.py:40
  514.8 68.0 %collective-permute-start.67 = (bf16[512,768]{0,1:T(8,128)(2,1)}, bf16[512,768]{0,1:T(8,128)(2,1)}, u32[]{:S(2)}, u32[]{:S(2)}) collective-permute-start(bf16[512,768]{0,1:T(8,128)(2,1)} %fusion.50), channel_id=1, source_target_pairs={{0,16},{16,0},{1,17},{17,1},{2,18},{18,2},{3,19},{19,3},{4,20},{20... | collective-permute-start | bytes 2359304 | tf_op jit(solution)/shard_map/ppermute | solution.py:40
  545.6 58.4 %collective-permute-start.36 = (bf16[512,2048]{1,0:T(8,128)(2,1)}, bf16[512,2048]{1,0:T(8,128)(2,1)}, u32[]{:S(2)}, u32[]{:S(2)}) collective-permute-start(bf16[512,2048]{1,0:T(8,128)(2,1)} %add_convert_fusion.1), channel_id=1, source_target_pairs={{0,1},{1,0},{2,3},{3,2},{4,5},{5,4},{6,7},{7,6},{8,9},{9,8},{10,11... | collective-permute-start | bytes 6291464 | tf_op jit(solution)/shard_map/ppermute | solution.py:118
  565.7 51.4 %collective-permute-start.62 = (bf16[512,768]{0,1:T(8,128)(2,1)}, bf16[512,768]{0,1:T(8,128)(2,1)}, u32[]{:S(2)}, u32[]{:S(2)}) collective-permute-start(bf16[512,768]{0,1:T(8,128)(2,1)} %get-tuple-element.106), channel_id=1, source_target_pairs={{0,4},{4,0},{1,5},{5,1},{2,6},{6,2},{3,7},{7,3},{8,12},{12,8},{9,1... | collective-permute-start | bytes 2359304 | tf_op jit(solution)/shard_map/ppermute | solution.py:40
  573.0 45.2 %collective-permute-start.64 = (bf16[512,768]{0,1:T(8,128)(2,1)}, bf16[512,768]{0,1:T(8,128)(2,1)}, u32[]{:S(2)}, u32[]{:S(2)}) collective-permute-start(bf16[512,768]{0,1:T(8,128)(2,1)} %fusion.57), channel_id=1, source_target_pairs={{0,16},{16,0},{1,17},{17,1},{2,18},{18,2},{3,19},{19,3},{4,20},{20... | collective-permute-start | bytes 2359304 | tf_op jit(solution)/shard_map/ppermute | solution.py:40
  598.7 52.6 %collective-permute-start.46 = (bf16[128,2048]{1,0:T(8,128)(2,1)}, bf16[128,2048]{1,0:T(8,128)(2,1)}, u32[]{:S(2)}, u32[]{:S(2)}) collective-permute-start(bf16[128,2048]{1,0:T(8,128)(2,1)} %get-tuple-element.123), channel_id=1, source_target_pairs={{0,8},{8,0},{1,9},{9,1},{2,10},{10,2},{3,11},{11,3},{4,12},{12,4},... | collective-permute-start | bytes 1572872 | tf_op jit(solution)/shard_map/ppermute | solution.py:122
  599.8 47.6 %all-to-all-start.8 = ((bf16[8,64,768]{2,1,0:T(8,128)(2,1)}), bf16[8,64,768]{2,1,0:T(8,128)(2,1)}, u32[]{:S(2)}, u32[]{:S(2)}) async-start(bf16[8,64,768]{2,1,0:T(8,128)(2,1)} %bitcast.73), calls=%async_computation.8 | async-start | bytes 1572864 | tf_op jit(solution)/shard_map/all_to_all | solution.py:128
  604.1 47.2 %collective-permute-start.45 = (bf16[128,2048]{1,0:T(8,128)(2,1)}, bf16[128,2048]{1,0:T(8,128)(2,1)}, u32[]{:S(2)}, u32[]{:S(2)}) collective-permute-start(bf16[128,2048]{1,0:T(8,128)(2,1)} %get-tuple-element.121), channel_id=1, source_target_pairs={{0,2},{2,0},{1,3},{3,1},{4,6},{6,4},{5,7},{7,5},{8,10},{10,8},{9,1... | collective-permute-start | bytes 1572872 | tf_op jit(solution)/shard_map/ppermute | solution.py:123
  618.1 51.8 %collective-permute-start.38 = (bf16[128,2048]{1,0:T(8,128)(2,1)}, bf16[128,2048]{1,0:T(8,128)(2,1)}, u32[]{:S(2)}, u32[]{:S(2)}) collective-permute-start(bf16[128,2048]{1,0:T(8,128)(2,1)} %get-tuple-element.135), channel_id=1, source_target_pairs={{0,8},{8,0},{1,9},{9,1},{2,10},{10,2},{3,11},{11,3},{4,12},{12,4},... | collective-permute-start | bytes 1572872 | tf_op jit(solution)/shard_map/ppermute | solution.py:122
  761.5 48.7 %collective-permute-start.56 = (bf16[512,512]{1,0:T(8,128)(2,1)}, bf16[512,512]{1,0:T(8,128)(2,1)S(1)}, u32[]{:S(2)}, u32[]{:S(2)}) collective-permute-start(bf16[512,512]{1,0:T(8,128)(2,1)} %get-tuple-element.112), channel_id=1, source_target_pairs={{0,4},{4,0},{1,5},{5,1},{2,6},{6,2},{3,7},{7,3},{8,12},{12,8},{9,1... | collective-permute-start | bytes 1572872 | tf_op jit(solution)/shard_map/ppermute | solution.py:40
  764.3 45.2 %collective-permute-start.73 = (f32[2,128]{1,0:T(2,128)S(1)}, f32[2,128]{1,0:T(2,128)S(1)}, u32[]{:S(2)}, u32[]{:S(2)}) collective-permute-start(f32[2,128]{1,0:T(2,128)S(1)} %fusion.292), channel_id=1, source_target_pairs={{8,0},{0,8},{9,1},{1,9},{10,2},{2,10},{11,3},{3,11},{12,4},{4,12},... | collective-permute-start | bytes 3080 | tf_op jit(solution)/shard_map/ppermute | solution.py:36
  (153 other events, 3406.6 us)

commit v2 on v1

v2 whole, which is shorter than its diff:
```python
import math

import jax
import jax.numpy as jnp
from jax import lax
from jax.experimental import pallas as pl
from jax.experimental.pallas import tpu as pltpu
from jax.sharding import Mesh, PartitionSpec as P

QUERY_HEADS = 16
KEY_VALUE_HEADS = 8
HEAD_SIZE = 128
EPS = 1e-06
THETA = 1000000.0

F32 = jnp.float32
BF16 = jnp.bfloat16
SWAP = [(0, 1), (1, 0)]
DIAGONAL = [(0, 3), (1, 2), (2, 1), (3, 0)]
TEAM = ("zl", "xl", "c")
TEAM_SIZE = 8
AXES = ("zh", "zl", "y", "xh", "xl", "c")
CHUNKS = 3
VMEM_LIMIT = 48 << 20
WEIGHT = 100
FORWARD_STEPS = 4
BACK_STEPS = 2


def hold(*values):
    return lax.optimization_barrier(values)


class Layout:
    def __init__(self, sizes):
        self.zh, self.y, self.xh = sizes["zh"], sizes["y"], sizes["xh"]
        self.near = self.y * self.xh
        self.groups = self.zh * self.near

    def order(self):
        zh, y, xh = (lax.axis_index(name) for name in ("zh", "y", "xh"))
        places = []
        for j in range(self.y):
            for i in range(self.xh):
                for k in range(self.zh):
                    for low in range(2):
                        at = ((zh + k) % self.zh * 2 + low) * self.y + (y + j) % self.y
                        places.append(at * self.xh + (xh + i) % self.xh)
        return jnp.stack(places).astype(jnp.int32)

    def far_blocks(self, block):
        return [
            lax.ppermute(block, "zh", [((i + k) % self.zh, i) for i in range(self.zh)]) for k in range(1, self.zh)
        ]

    def shifted(self, n):
        j, i = n // self.xh, n % self.xh
        return [
            (a * self.xh + b, (a + j) % self.y * self.xh + (b + i) % self.xh)
            for a in range(self.y)
            for b in range(self.xh)
        ]

    def near_blocks(self, block):
        return [
            lax.ppermute(block, ("y", "xh"), [(b, a) for a, b in self.shifted(n)]) for n in range(1, self.near)
        ]

    def to_near(self, value, n):
        return lax.ppermute(value, ("y", "xh"), self.shifted(n))

    def to_far(self, value, k):
        return lax.ppermute(value, "zh", [(i, (i + k) % self.zh) for i in range(self.zh)])


def among_four(value):
    return lax.all_to_all(value, ("zl", "xl"), 0, 0, tiled=True)


def spread(copies):
    return among_four(copies).reshape(-1, copies.shape[-1])


def other_core(value):
    return lax.ppermute(value, "c", SWAP)


def exchange(value):
    return lax.all_to_all(value, TEAM, 0, 0, tiled=True)


def all_sum(value, sizes, axes):
    for axis in axes:
        total = value
        for k in range(1, sizes[axis]):
            total = total + lax.ppermute(value, axis, [((i + k) % sizes[axis], i) for i in range(sizes[axis])])
        value = total
    return value


def device_index(sizes):
    index = 0
    for axis in AXES:
        index = index * sizes[axis] + lax.axis_index(axis)
    return index


def dot(left, right):
    return lax.dot_general(left, right, (((1,), (0,)), ((), ())), preferred_element_type=F32)


def dot_nt(left, right):
    return lax.dot_general(left, right, (((1,), (1,)), ((), ())), preferred_element_type=F32)


def dot_tn(left, right):
    return lax.dot_general(left, right, (((0,), (0,)), ((), ())), preferred_element_type=F32)


def shape(dims, dtype):
    return jax.ShapeDtypeStruct(tuple(dims), dtype)


def run(kernel, grid, in_specs, out_specs, out_shape, args, flops=0):
    outs = jax.tree.leaves(out_shape)
    size = sum(math.prod(a.shape) * a.dtype.itemsize for a in list(args) + outs)
    return pl.pallas_call(
        kernel,
        grid=grid,
        in_specs=in_specs,
        out_specs=out_specs,
        out_shape=out_shape,
        compiler_params=pltpu.CompilerParams(
            vmem_limit_bytes=VMEM_LIMIT, dimension_semantics=("arbitrary",) * len(grid)
        ),
        cost_estimate=pl.CostEstimate(
            flops=WEIGHT * int(flops), bytes_accessed=WEIGHT * int(size), transcendentals=0
        ),
    )(*args)


def whole(array):
    return pl.BlockSpec(array.shape, lambda *_, n=len(array.shape): (0,) * n)


def inverse_rms(value):
    return lax.rsqrt(jnp.mean(value * value, axis=-1, keepdims=True) + EPS)


def norm_input_gradient(normed, inverse, e):
    return inverse * (e - normed * jnp.mean(e * normed, axis=-1, keepdims=True))


def reorder(values, places, inverse, copies=0):
    count = places.shape[0]
    width = values[0].shape[-1]
    cut = width // count
    if cut % 128:
        at = jnp.argsort(places) if inverse else places
        moved = [jnp.take(v.reshape(v.shape[:-1] + (count, cut)), at, axis=-2).reshape(v.shape) for v in values]
        if copies:
            side = jnp.concatenate(moved, axis=-1)
            return jnp.broadcast_to(side[None], (copies,) + side.shape)
        return moved
    if copies:
        outs = [shape((copies, values[0].shape[0], width * len(values)), values[0].dtype)]
    else:
        outs = [shape(v.shape, v.dtype) for v in values]

    def kernel(places_ref, *refs):
        for n, source in enumerate(refs[: len(values)]):
            for i in range(count):
                place = places_ref[i] * cut
                if copies:
                    value = source[:, pl.ds(pl.multiple_of(place, 128), cut)]
                    for copy in range(copies):
                        refs[-1][copy, :, n * width + i * cut : n * width + (i + 1) * cut] = value
                else:
                    moving = pl.ds(pl.multiple_of(place, 128), cut)
                    still = pl.ds(i * cut, cut)
                    target = refs[len(values) + n]
                    target[:, moving if inverse else still] = source[:, still if inverse else moving]

    size = sum(math.prod(a.shape) * a.dtype.itemsize for a in list(values) + outs)
    result = pl.pallas_call(
        kernel,
        grid_spec=pltpu.PrefetchScalarGridSpec(
            num_scalar_prefetch=1,
            grid=(1,),
            in_specs=[whole(v) for v in values],
            out_specs=[whole(o) for o in outs],
        ),
        out_shape=outs,
        compiler_params=pltpu.CompilerParams(vmem_limit_bytes=VMEM_LIMIT),
        cost_estimate=pl.CostEstimate(flops=0, bytes_accessed=WEIGHT * size, transcendentals=0),
    )(places, *values)
    return result[0] if copies else result


def pack_attention(w_qkv, w_out):
    owned, columns = w_qkv.shape
    q_cols, kv_cols = QUERY_HEADS * HEAD_SIZE, KEY_VALUE_HEADS * HEAD_SIZE
    q_width = q_cols // TEAM_SIZE

    def kernel(w_ref, w_out_ref, out_ref):
        for r in range(TEAM_SIZE):
            out_ref[r, :, :q_width] = w_ref[:, r * q_width : (r + 1) * q_width]
            for part in range(2):
                at = q_cols + part * kv_cols + r * HEAD_SIZE
                to = q_width + part * HEAD_SIZE
                out_ref[r, :, to : to + HEAD_SIZE] = w_ref[:, at : at + HEAD_SIZE]
            out_ref[r, :, columns // TEAM_SIZE :] = w_out_ref[:, r * q_width : (r + 1) * q_width]

    out = shape((TEAM_SIZE, owned, columns // TEAM_SIZE + q_width), BF16)
    return run(kernel, (1,), [whole(w_qkv), whole(w_out)], whole(out), out, [w_qkv, w_out])


def pack_chunks(w_gate_up, w_down, chunk):
    owned = w_down.shape[0]
    per = w_down.shape[1] // TEAM_SIZE

    def kernel(gate_up_ref, down_ref, target):
        for j in range(CHUNKS):
            to = 3 * chunk * j
            for r in range(TEAM_SIZE):
                at = slice(r * per + j * chunk, r * per + (j + 1) * chunk)
                target[r, :, to : to + chunk] = gate_up_ref[:, 0, at]
                target[r, :, to + chunk : to + 2 * chunk] = gate_up_ref[:, 1, at]
                target[r, :, to + 2 * chunk : to + 3 * chunk] = down_ref[:, at]

    out = shape((TEAM_SIZE, owned, 3 * chunk * CHUNKS), BF16)
    args = [w_gate_up, w_down]
    return run(kernel, (1,), [whole(a) for a in args], whole(out), out, args)


def unpack_chunks(back, w_gate_up, gain, chunk):
    owned = back.shape[1]
    per = CHUNKS * chunk

    def kernel(back_ref, w_ref, gain_ref, gate_up_ref, down_ref, out_ref):
        r = pl.program_id(0)
        total = jnp.zeros((owned, 1), F32)
        for j in range(CHUNKS):
            at, to = 3 * chunk * j, slice(j * chunk, (j + 1) * chunk)
            for part in range(2):
                value = back_ref[0, :, at + part * chunk : at + (part + 1) * chunk].astype(F32)
                gate_up_ref[:, part, to] = value
                total = total + jnp.sum(value * w_ref[:, part, to].astype(F32), axis=1, keepdims=True)
            down_ref[:, to] = back_ref[0, :, at + 2 * chunk : at + 3 * chunk].astype(F32)
        total = total / gain_ref[...]

        @pl.when(r == 0)
        def _():
            out_ref[...] = total

        @pl.when(r > 0)
        def _():
            out_ref[...] += total

    outs = [
        shape((owned, 2, TEAM_SIZE * per), F32),
        shape((owned, TEAM_SIZE * per), F32),
        shape((owned, 1), F32),
    ]
    wide = pl.BlockSpec((owned, 2, per), lambda r: (0, 0, r))
    return run(
        kernel,
        (TEAM_SIZE,),
        [pl.BlockSpec((1, owned, 3 * per), lambda r: (r, 0, 0)), wide, whole(gain)],
        [wide, pl.BlockSpec((owned, per), lambda r: (0, r)), whole(gain)],
        outs,
        [back, w_gate_up, gain],
    )


def unpack_attention(back, w_qkv, gain):
    owned, columns = w_qkv.shape
    q_cols, kv_cols = QUERY_HEADS * HEAD_SIZE, KEY_VALUE_HEADS * HEAD_SIZE
    q_width = q_cols // TEAM_SIZE

    def kernel(back_ref, w_ref, gain_ref, qkv_ref, out_weight_ref, out_ref):
        total = jnp.zeros((owned, 1), F32)
        for r in range(TEAM_SIZE):
            spans = [(0, r * q_width, q_width)]
            for part in range(2):
                spans.append((q_width + part * HEAD_SIZE, q_cols + part * kv_cols + r * HEAD_SIZE, HEAD_SIZE))
            for at, to, n in spans:
                value = back_ref[r, :, at : at + n].astype(F32)
                qkv_ref[:, to : to + n] = value
                total = total + jnp.sum(value * w_ref[:, to : to + n].astype(F32), axis=1, keepdims=True)
            out_weight_ref[:, r * q_width : (r + 1) * q_width] = back_ref[
                r, :, q_width + 2 * HEAD_SIZE :
            ].astype(F32)
        out_ref[...] = total / gain_ref[...]

    outs = [shape((owned, columns), F32), shape((owned, q_cols), F32), shape((owned, 1), F32)]
    args = [back, w_qkv, gain]
    return run(kernel, (1,), [whole(a) for a in args], [whole(o) for o in outs], outs, args)


def either(step, steps, refs, body):
    per = steps // 2

    @pl.when(step < per)
    def _():
        body(*[r[0] for r in refs])

    @pl.when(step >= per)
    def _():
        body(*[r[1] for r in refs])


def half_specs(side, width, steps):
    halves, column = side
    per = steps // 2
    rows = halves[0].shape[0]
    return [
        pl.BlockSpec((rows // per, width), lambda i: (jnp.minimum(i, per - 1), column)),
        pl.BlockSpec((rows // per, width), lambda i: (jnp.maximum(i - per, 0), column)),
    ]


def turned(value, cosine, sine):
    return value * cosine + pltpu.roll(value, HEAD_SIZE // 2, 1) * sine


def project(x_side, blocks, g_attn, g_q, g_k, cosine, sine, q_width):
    count = len(blocks)
    tokens, width = 2 * x_side[0][0].shape[0], count * blocks[0].shape[0]
    columns = q_width + 2 * HEAD_SIZE
    steps = 4
    rows = tokens // steps

    def kernel(x0, x1, *refs):
        w_refs = refs[:count]
        g_attn_ref, g_q_ref, g_k_ref, cos_ref, sin_ref, normed_ref, raw_ref, qkv_ref = refs[count:]

        def body(x_ref):
            x = x_ref[...].astype(F32)
            normed_ref[...] = (x * inverse_rms(x) * g_attn_ref[...]).astype(BF16)

        either(pl.program_id(0), steps, [(x0, x1)], body)
        per = width // count
        total = dot(normed_ref[:, :per], w_refs[0][...])
        for b in range(1, count):
            total = total + dot(normed_ref[:, b * per : (b + 1) * per], w_refs[b][...])
        raw_ref[...] = total[:, : q_width + HEAD_SIZE]
        cos, sin = cos_ref[...], sin_ref[...]
        for at in range(0, q_width + HEAD_SIZE, HEAD_SIZE):
            head = total[:, at : at + HEAD_SIZE]
            gain = g_q_ref[...] if at < q_width else g_k_ref[...]
            qkv_ref[:, at : at + HEAD_SIZE] = turned(head * inverse_rms(head) * gain, cos, sin).astype(BF16)
        qkv_ref[:, q_width + HEAD_SIZE :] = total[:, q_width + HEAD_SIZE :].astype(BF16)

    row = lambda n: pl.BlockSpec((rows, n), lambda i: (i, 0))
    outs = [
        shape((tokens, width), BF16),
        shape((tokens, q_width + HEAD_SIZE), F32),
        shape((tokens, columns), BF16),
    ]
    gains = [g_attn, g_q, g_k]
    return run(
        kernel,
        (steps,),
        half_specs(x_side, width, steps)
        + [pl.BlockSpec((w.shape[0], columns), lambda i: (0, 0)) for w in blocks]
        + [whole(g) for g in gains]
        + [row(HEAD_SIZE), row(HEAD_SIZE)],
        [row(o.shape[1]) for o in outs],
        outs,
        [*x_side[0], *blocks, *gains, cosine, sine],
        flops=2 * tokens * width * columns,
    )


def masked(q, k, allowed, scale):
    return jnp.where(allowed, dot_nt(q, k) * scale, -1e9)


def attention_specs(qkv, kv, kv_block, q_width, quarter, keys):
    parts = kv.shape[0]
    return [
        pl.BlockSpec((2, 1, quarter, q_width), lambda s: (0, s, 0, 0)),
        pl.BlockSpec((parts, 2, 1, quarter, 2 * HEAD_SIZE), lambda s: (0, 0, s, 0, kv_block)),
        pl.BlockSpec((1, 2 * quarter, 2), lambda s: (s, 0, 0)),
        pl.BlockSpec((1, 2, keys), lambda s: (s, 0, 0)),
    ]


def allowed_pairs(q_info, k_info):
    doc_q, index_q = q_info[:, 0:1], q_info[:, 1:2]
    doc_k, index_k = k_info[0:1, :], k_info[1:2, :]
    return (doc_q == doc_k) & (index_k <= index_q)


def attend(qkv, kv, kv_block, q_info, k_info, q_width):
    quarter = qkv.shape[2]
    keys = kv.shape[0] * 2 * quarter
    heads = q_width // HEAD_SIZE
    scale = HEAD_SIZE ** (-0.5)

    def kernel(q_ref, kv_ref, q_info_ref, k_info_ref, out_ref, lse_ref):
        allowed = allowed_pairs(q_info_ref[0], k_info_ref[0])
        pairs = kv_ref[...].reshape(keys, 2 * HEAD_SIZE)
        for h in range(heads):
            at = slice(h * HEAD_SIZE, (h + 1) * HEAD_SIZE)
            q = q_ref[:, 0, :, at].reshape(2 * quarter, HEAD_SIZE)
            scores = masked(q, pairs[:, :HEAD_SIZE], allowed, scale)
            peak = jnp.max(scores, axis=-1, keepdims=True)
            weights = jnp.exp(scores - peak)
            total = jnp.sum(weights, axis=-1, keepdims=True)
            probs = (weights * (1.0 / total)).astype(BF16)
            lse_ref[0, :, h : h + 1] = peak + jnp.log(total)
            attended = dot(probs, pairs[:, HEAD_SIZE:]).astype(BF16)
            out_ref[:, 0, :, at] = attended.reshape(2, quarter, HEAD_SIZE)

    outs = [shape((2, 2, quarter, q_width), BF16), shape((2, 2 * quarter, heads), F32)]
    return run(
        kernel,
        (2,),
        attention_specs(qkv, kv, kv_block, q_width, quarter, keys),
        [
            pl.BlockSpec((2, 1, quarter, q_width), lambda s: (0, s, 0, 0)),
            pl.BlockSpec((1, 2 * quarter, heads), lambda s: (s, 0, 0)),
        ],
        outs,
        [qkv, kv, q_info, k_info],
        flops=4 * 2 * heads * 2 * quarter * keys * HEAD_SIZE,
    )


def attend_back(qkv, kv, kv_block, q_info, k_info, q_width, lse, d_attended):
    quarter = qkv.shape[2]
    parts = kv.shape[0]
    keys = parts * 2 * quarter
    heads = q_width // HEAD_SIZE
    scale = HEAD_SIZE ** (-0.5)

    def kernel(q_ref, kv_ref, q_info_ref, k_info_ref, lse_ref, da_ref, dq_ref, dk_ref, dv_ref):
        allowed = allowed_pairs(q_info_ref[0], k_info_ref[0])
        pairs = kv_ref[...].reshape(keys, 2 * HEAD_SIZE)
        k, v = pairs[:, :HEAD_SIZE], pairs[:, HEAD_SIZE:]
        d_k = d_v = None
        for h in range(heads):
            at = slice(h * HEAD_SIZE, (h + 1) * HEAD_SIZE)
            q = q_ref[:, 0, :, at].reshape(2 * quarter, HEAD_SIZE)
            da = da_ref[:, 0, :, at].reshape(2 * quarter, HEAD_SIZE)
            probs = jnp.exp(masked(q, k, allowed, scale) - lse_ref[0, :, h : h + 1])
            d_probs = dot_nt(da, v)
            row_dot = jnp.sum(probs * d_probs, axis=-1, keepdims=True)
            d_raw = (probs * (d_probs - row_dot) * scale).astype(BF16)
            dq_ref[:, 0, :, at] = dot(d_raw, k).astype(BF16).reshape(2, quarter, HEAD_SIZE)
            k_term, v_term = dot_tn(d_raw, q), dot_tn(probs.astype(BF16), da)
            d_k = k_term if d_k is None else d_k + k_term
            d_v = v_term if d_v is None else d_v + v_term
        dk_ref[...] = d_k.astype(BF16).reshape(parts, 2, 1, quarter, HEAD_SIZE)
        dv_ref[...] = d_v.astype(BF16).reshape(parts, 2, 1, quarter, HEAD_SIZE)

    part = pl.BlockSpec((parts, 2, 1, quarter, HEAD_SIZE), lambda s: (0, 0, s, 0, 0))
    query = pl.BlockSpec((2, 1, quarter, q_width), lambda s: (0, s, 0, 0))
    part_shape = shape((parts, 2, 2, quarter, HEAD_SIZE), BF16)
    return run(
        kernel,
        (2,),
        attention_specs(qkv, kv, kv_block, q_width, quarter, keys)
        + [pl.BlockSpec((1, 2 * quarter, heads), lambda s: (s, 0, 0)), query],
        [query, part, part],
        [shape((2, 2, quarter, q_width), BF16), part_shape, part_shape],
        [qkv, kv, q_info, k_info, lse, d_attended],
        flops=10 * 2 * heads * 2 * quarter * keys * HEAD_SIZE,
    )


def project_back(raw, d_q, d_k, d_v, g_q, g_k, cosine, sine, q_width):
    tokens = raw.shape[0]
    steps = 4
    rows = tokens // steps

    def kernel(raw_ref, dq_ref, dk_ref, dv_ref, g_q_ref, g_k_ref, cos_ref, sin_ref, out_ref, gain_ref):
        cos, sin = cos_ref[...], sin_ref[...]
        gains = [jnp.zeros((1, HEAD_SIZE), F32), jnp.zeros((1, HEAD_SIZE), F32)]
        for at in range(0, q_width + HEAD_SIZE, HEAD_SIZE):
            is_key = int(at >= q_width)
            incoming = (dk_ref[...] if is_key else dq_ref[:, at : at + HEAD_SIZE]).astype(F32)
            back = turned(incoming, cos, -sin)
            head = raw_ref[:, at : at + HEAD_SIZE]
            inverse = inverse_rms(head)
            normed = head * inverse
            gains[is_key] = gains[is_key] + jnp.sum(back * normed, axis=0, keepdims=True)
            gain = g_k_ref[...] if is_key else g_q_ref[...]
            out_ref[:, at : at + HEAD_SIZE] = norm_input_gradient(normed, inverse, back * gain).astype(BF16)
        out_ref[:, q_width + HEAD_SIZE :] = dv_ref[...]

        @pl.when(pl.program_id(0) == 0)
        def _():
            gain_ref[...] = jnp.zeros_like(gain_ref)

        gain_ref[0:1, :] += gains[0]
        gain_ref[1:2, :] += gains[1]

    row = lambda n: pl.BlockSpec((rows, n), lambda i: (i, 0))
    outs = [shape((tokens, q_width + 2 * HEAD_SIZE), BF16), shape((8, HEAD_SIZE), F32)]
    args = [raw, d_q, d_k, d_v, g_q, g_k, cosine, sine]
    in_specs = [row(a.shape[1]) for a in args[:4]] + [whole(g_q), whole(g_k), row(HEAD_SIZE), row(HEAD_SIZE)]
    return run(kernel, (steps,), in_specs, [row(outs[0].shape[1]), whole(outs[1])], outs, args)


def back_rows(which, pairs, received=None):
    tokens = pairs[0][0].shape[0]
    half = tokens // 2
    steps = BACK_STEPS
    rows = half // steps
    count = len(pairs[0][1])
    per = pairs[0][1][0].shape[0]
    width = count * per
    left = [p[0] for p in pairs]
    blocks = [b for p in pairs for b in p[1]]

    def kernel(*refs):
        left_refs, w_refs = refs[: len(left)], refs[len(left) : len(left) + len(blocks)]
        out_ref = refs[-1]
        for b in range(count):
            at = slice(b * per, (b + 1) * per)
            total = None
            for i, l in enumerate(left_refs):
                term = dot_nt(l[...], w_refs[i * count + b][...])
                total = term if total is None else total + term
            if received is not None:
                total = total + refs[-2][:, at].astype(F32)
            out_ref[:, at] = total.astype(BF16)

    out = shape((half, width), BF16)
    out_spec = pl.BlockSpec((rows, width), lambda i: (i, 0))
    in_specs = [pl.BlockSpec((rows, p[0].shape[1]), lambda i: (which * steps + i, 0)) for p in pairs]
    for _, group, column, n in pairs:
        in_specs += [pl.BlockSpec((per, n), lambda i, column=column: (0, column)) for _ in group]
    args = left + blocks
    if received is not None:
        in_specs.append(out_spec)
        args = args + [received]
    flops = sum(2 * half * width * p[3] for p in pairs)
    return run(kernel, (steps,), in_specs, out_spec, out, args, flops=flops)


def feed_forward(nm, dy, blocks, chunk):
    count = len(blocks)
    per = blocks[0].shape[0]
    tokens, width = 2 * nm[0][0].shape[0], count * per
    steps = FORWARD_STEPS
    rows = tokens // steps

    def kernel(nm0, nm1, dy0, dy1, *refs):
        w_refs, (hidden_ref, d_ref) = refs[:count], refs[count:]

        def body(nm_ref, dy_ref):
            both = d_hidden = None
            for b in range(count):
                at = slice(b * per, (b + 1) * per)
                one = dot(nm_ref[:, at], w_refs[b][:, : 2 * chunk])
                two = dot(dy_ref[:, at], w_refs[b][:, 2 * chunk : 3 * chunk])
                both = one if both is None else both + one
                d_hidden = two if d_hidden is None else d_hidden + two
            gate, upward = both[:, :chunk], both[:, chunk:]
            sigma = 1.0 / (1.0 + jnp.exp(-gate))
            silu = gate * sigma
            hidden_ref[...] = (silu * upward).astype(BF16)
            d_ref[:, :chunk] = (d_hidden * upward * (sigma * (1.0 + gate * (1.0 - sigma)))).astype(BF16)
            d_ref[:, chunk:] = (d_hidden * silu).astype(BF16)

        either(pl.program_id(0), steps, [(nm0, nm1), (dy0, dy1)], body)

    row = lambda n: pl.BlockSpec((rows, n), lambda i: (i, 0))
    outs = [shape((tokens, chunk), BF16), shape((tokens, 2 * chunk), BF16)]
    w_specs = [pl.BlockSpec((per, 3 * chunk), lambda i: (0, 0)) for _ in blocks]
    return run(
        kernel,
        (steps,),
        half_specs(nm, width, steps) + half_specs(dy, width, steps) + w_specs,
        [row(chunk), row(2 * chunk)],
        outs,
        [*nm[0], *dy[0], *blocks],
        flops=2 * tokens * width * 3 * chunk,
    )


def weight_terms(layout, width, n, pairs, received=None):
    tile = width // layout.groups
    cuts = [p[1].shape[1] for p in pairs]
    columns = sum(cuts)
    tokens = pairs[0][1].shape[0]
    left = [(a, p[0][1]) for p in pairs for a in p[0][0]]

    def kernel(*refs):
        refs = list(refs)
        l_refs = [[refs.pop(0) for _ in p[0][0]] for p in pairs]
        d_refs = [refs.pop(0) for _ in pairs]
        in_refs = [refs.pop(0) for _ in (received or ())]
        column = 0
        for sources, d_ref, cut in zip(l_refs, d_refs, cuts):
            total, at = None, 0
            for source in sources:
                count = source.shape[0]
                term = dot_tn(source[...], d_ref[at : at + count, :])
                total = term if total is None else total + term
                at += count
            span = slice(column, column + cut)
            column += cut
            for r in in_refs:
                total = total + r[:, span].astype(F32)
            if received is None:
                refs[0][:, span] = total.astype(BF16)
                continue
            for k, out_ref in enumerate(refs):

                @pl.when(pl.program_id(0) == k)
                def _(out_ref=out_ref, total=total, span=span):
                    out_ref[:, span] = total.astype(BF16)

    in_specs = [
        pl.BlockSpec((a.shape[0], tile), lambda k, column=column: (0, column * layout.groups + n * layout.zh + k))
        for a, column in left
    ]
    in_specs += [whole(p[1]) for p in pairs]
    args = [a for a, _ in left] + [p[1] for p in pairs]
    row = pl.BlockSpec((tile, columns), lambda k: (k, 0))
    if received is None:
        outs, out_specs = shape((layout.zh * tile, columns), BF16), row
    else:
        args += received
        in_specs += [row] * len(received)
        outs = [shape((tile, columns), BF16)] * layout.zh
        out_specs = [whole(o) for o in outs]
    return run(
        kernel, (layout.zh,), in_specs, out_specs, outs, args, flops=2 * tokens * layout.zh * tile * columns
    )


def one_copy(value, width, column=0):
    if len(value.shape) == 2:
        return whole(value)
    return pl.BlockSpec((1, value.shape[1], width), lambda *_: (0, 0, column))


def rows_of(ref):
    return ref[...].reshape(ref.shape[-2:])


def middle_step(parts, x, gain):
    rows, width = x.shape[-2], gain.shape[1]

    def kernel(parts_ref, x_ref, gain_ref, middle_ref, nm_ref):
        middle = rows_of(x_ref).astype(F32)
        for i in range(4):
            middle = middle + parts_ref[i].astype(F32)
        middle_ref[...] = middle
        nm = (middle * inverse_rms(middle) * gain_ref[...]).astype(BF16)
        for i in range(4):
            nm_ref[i] = nm

    outs = [shape((rows, width), F32), shape((4, rows, width), BF16)]
    args = [parts, x, gain]
    return run(kernel, (1,), [whole(parts), one_copy(x, width), whole(gain)], [whole(o) for o in outs], outs, args)


def norm_back_step(parts, base, passed, passed_column, gain, copies):
    rows, width = base.shape[-2], gain.shape[1]

    def kernel(parts_ref, base_ref, passed_ref, gain_ref, *out_refs):
        total = parts_ref[0].astype(F32)
        for i in range(1, 4):
            total = total + parts_ref[i].astype(F32)
        value = rows_of(base_ref).astype(F32)
        inverse = inverse_rms(value)
        result = rows_of(passed_ref).astype(F32) + norm_input_gradient(
            value * inverse, inverse, total * gain_ref[...]
        )
        rounded = result.astype(BF16)
        if copies == 1:
            out_refs[0][...] = rounded
            return
        out_refs[0][...] = result
        for i in range(copies):
            out_refs[1][i] = rounded

    outs = [shape((rows, width), F32), shape((copies, rows, width), BF16)]
    if copies == 1:
        outs = [shape((rows, width), BF16)]
    args = [parts, base, passed, gain]
    return run(kernel, (1,), [whole(parts), one_copy(base, width), one_copy(passed, width, passed_column), whole(gain)], [whole(o) for o in outs], outs, args)


def plain_sum(parts, base):
    def kernel(parts_ref, base_ref, out_ref):
        total = base_ref[...]
        for i in range(4):
            total = total + parts_ref[i].astype(F32)
        out_ref[...] = total.astype(BF16)

    out = shape(base.shape, BF16)
    return run(kernel, (1,), [whole(parts), whole(base)], whole(out), out, [parts, base])


def attended_gradient(d_branch, blocks, column, n):
    count = len(blocks)
    per = blocks[0].shape[0]
    tokens, width = 2 * d_branch[0][0].shape[0], count * per
    steps = 4

    def kernel(d0, d1, *refs):
        w_refs, out_ref = refs[:count], refs[count]

        def body(d_ref):
            total = dot(d_ref[:, :per], w_refs[0][...])
            for b in range(1, count):
                total = total + dot(d_ref[:, b * per : (b + 1) * per], w_refs[b][...])
            out_ref[...] = total.astype(BF16)

        either(pl.program_id(0), steps, [(d0, d1)], body)

    out = shape((tokens, n), BF16)
    return run(
        kernel,
        (steps,),
        half_specs(d_branch, width, steps) + [pl.BlockSpec((per, n), lambda i: (0, column)) for _ in blocks],
        pl.BlockSpec((tokens // steps, n), lambda i: (i, 0)),
        out,
        [*d_branch[0], *blocks],
        flops=2 * tokens * width * n,
    )


def layer(
    sizes,
    tokens,
    doc_ids,
    w_qkv_rows,
    w_out_rows,
    w_gate_up_rows,
    w_down_rows,
    attn_gain,
    q_gain,
    k_gain,
    mlp_gain,
    out_grad,
):
    layout = Layout(sizes)
    rows = tokens.shape[1]
    width = tokens.shape[2]
    owned = w_qkv_rows.shape[0]
    devices = width // owned
    q_width = QUERY_HEADS // TEAM_SIZE * HEAD_SIZE
    chunk = w_down_rows.shape[1] // TEAM_SIZE // CHUNKS
    small = q_gain.shape[0]
    places = layout.order()

    def arrived(value):
        return value.reshape(TEAM_SIZE * owned, -1)

    def gathered(near, far):
        columns = [near] + far
        return [columns[k][n] for n in range(layout.near) for k in range(layout.zh)]

    def with_near(block):
        return [block] + layout.near_blocks(block)

    copies = reorder([tokens[0], out_grad[0]], places, False, 4)
    part_attn = arrived(exchange(pack_attention(w_qkv_rows, w_out_rows)))
    send_mlp = pack_chunks(w_gate_up_rows, w_down_rows, chunk)
    mine = jnp.concatenate([attn_gain, mlp_gain, q_gain, k_gain, doc_ids.reshape(-1).astype(BF16)])[None]
    table = jnp.zeros((devices, mine.shape[1]), BF16)
    table = lax.dynamic_update_slice(table, mine, (device_index(sizes), 0))
    table = all_sum(table, sizes, ("c", "xl", "zl"))
    part_attn, copies, send_mlp, table = hold(part_attn, copies, send_mlp, table)

    attn_near, attn_far = with_near(part_attn), layout.far_blocks(part_attn)
    rest = arrived(exchange(send_mlp))
    table = all_sum(table, sizes, ("y", "xh", "zh"))
    attn_near, attn_far, rest, table, copies = hold(attn_near, attn_far, rest, table, copies)
    parts = [rest[:, j * 3 * chunk : (j + 1) * 3 * chunk] for j in range(CHUNKS)]

    near, far = {}, {}
    w_attn = gathered(attn_near, [with_near(b) for b in attn_far])
    near[0], far[0] = with_near(parts[0]), layout.far_blocks(parts[0])
    token_half = spread(copies)

    table = table.astype(F32)
    natural = jnp.stack([table[:, :owned].reshape(width), table[:, owned : 2 * owned].reshape(width)])
    count = places.shape[0]
    g_attn, g_mlp = jnp.split(
        jnp.take(natural.reshape(2, count, -1), places, axis=1).reshape(2, width), 2, axis=0
    )
    g_q = table[:, 2 * owned : 2 * owned + small].reshape(1, -1)
    g_k = table[:, 2 * owned + small : 2 * owned + 2 * small].reshape(1, -1)
    docs = table[:, 2 * owned + 2 * small :].astype(jnp.int32)
    docs = docs.reshape(sizes["zh"], 2, sizes["y"], sizes["xh"], 2, 2, rows)
    docs = lax.dynamic_slice(
        docs, (lax.axis_index("zh"), 0, lax.axis_index("y"), 0, 0, 0, 0), (1, 2, 1) + docs.shape[3:]
    )[0, :, 0]
    docs = jnp.moveaxis(jnp.roll(docs, -lax.axis_index("c"), axis=3), 3, 2)
    place = (
        jnp.arange(sizes["xh"])[:, None, None] * 4
        + jnp.arange(2)[None, None, :] * 2
        + (lax.axis_index("c") ^ jnp.arange(2))[None, :, None]
    )
    index = (place[..., None] * rows + jnp.arange(rows)).astype(jnp.int32)
    index = jnp.broadcast_to(index[None], docs.shape)
    k_info = jnp.stack([docs.reshape(2, -1), index.reshape(2, -1)], axis=1)
    q_info = lax.dynamic_slice(
        jnp.stack([docs, index], axis=-1), (0, lax.axis_index("xh"), 0, 0, 0, 0), (2, 1, 2, 2, rows, 2)
    ).reshape(2, -1, 2)
    doc_start = jnp.sum((k_info[:, 0, None, :] < q_info[:, :, 0, None]).astype(jnp.int32), axis=2)
    position = (q_info[:, :, 1] - doc_start).astype(F32)
    position = jnp.moveaxis(position.reshape(2, 2, 2 * rows), 1, 0).reshape(-1, 1)
    half_head = HEAD_SIZE // 2
    freqs = jnp.exp(jnp.arange(half_head).astype(F32) * (-math.log(THETA) / half_head))
    angle = position * freqs
    cosine, sine = jnp.cos(angle), jnp.sin(angle)
    cosine = jnp.concatenate([cosine, cosine], axis=1)
    sine = jnp.concatenate([-sine, sine], axis=1)
    token_half, w_attn, cosine, sine, g_attn, g_mlp, k_info, q_info, near[0], far[0], parts = hold(
        token_half, w_attn, cosine, sine, g_attn, g_mlp, k_info, q_info, near[0], far[0], parts
    )

    near[1], far[1] = with_near(parts[1]), layout.far_blocks(parts[1])
    weights = [gathered(near[0], [with_near(b) for b in far[0]])]
    team = [token_half, other_core(token_half)]
    x_side, dy = (team, 0), (team, 1)
    normed_in, raw, qkv = project(x_side, w_attn, g_attn, g_q, g_k, cosine, sine, q_width)
    qkv4 = qkv.reshape(2, 2, 2 * rows, -1)
    if sizes["xh"] == 1:
        kv, kv_block = qkv4[None], 1
    else:
        kv, kv_block = lax.all_gather(qkv4[..., q_width:], "xh", axis=0, tiled=False), 0
    attended, lse = attend(qkv4, kv, kv_block, q_info, k_info, q_width)
    attended = attended.reshape(-1, q_width)
    out_column = (q_width + 2 * HEAD_SIZE) // q_width
    out_pair = [(attended, w_attn, out_column, q_width)]
    received = other_core(back_rows(1, out_pair))
    branch = among_four(back_rows(0, out_pair, received).reshape(4, rows, width))
    middle, nm_copies = middle_step(branch, copies, g_mlp)
    nm_copies, weights[0], near[1], far[1], parts[2] = hold(nm_copies, weights[0], near[1], far[1], parts[2])

    near[2], far[2] = with_near(parts[2]), layout.far_blocks(parts[2])
    weights.append(gathered(near[1], [with_near(b) for b in far[1]]))
    nm_half = spread(nm_copies)
    nm_half, weights[1], near[2], far[2] = hold(nm_half, weights[1], near[2], far[2])

    def near_send(*pairs):
        return [weight_terms(layout, width, n, pairs) for n in range(1, layout.near)]

    def to_near(terms):
        return [layout.to_near(t, n + 1) for n, t in enumerate(terms)]

    def own_terms(received, *pairs):
        return weight_terms(layout, width, 0, pairs, received=received)

    def to_far(sums):
        return [layout.to_far(sums[k], k) for k in range(1, layout.zh)]

    def far_total(own, received):
        total = own.astype(F32)
        for r in received:
            total = total + r.astype(F32)
        return total.astype(BF16).reshape(TEAM_SIZE, owned, -1)

    weights.append(gathered(near[2], [with_near(b) for b in far[2]]))
    nm = ([nm_half, other_core(nm_half)], 0)
    hidden, d_gate_up, mlp, going, arriving, sums, arrived_far = [], [], [], {}, {}, {}, {}

    def chunk_step(j):
        h, d = feed_forward(nm, dy, weights[j], chunk)
        hidden.append(h)
        d_gate_up.append(d)
        mlp.append([(nm, d), (dy, h)])

    chunk_step(0)
    chunk_step(1)
    going[0] = near_send(*mlp[0])
    weights[2], going[0], d_gate_up[1] = hold(weights[2], going[0], d_gate_up[1])

    arriving[0] = to_near(going[0])
    chunk_step(2)
    mid_pairs = [(d_gate_up[j], weights[j], 0, 2 * chunk) for j in range(CHUNKS)]
    out_pairs = [(hidden[j], weights[j], 2, chunk) for j in range(CHUNKS)]
    received = other_core(back_rows(1, mid_pairs))
    terms = among_four(back_rows(0, mid_pairs, received).reshape(4, rows, width))
    going[1] = near_send(*mlp[1])
    d_middle, d_copies = norm_back_step(terms, middle, copies, 1, g_mlp, 4)
    d_copies, going[1], arriving[0] = hold(d_copies, going[1], arriving[0])

    sums[0] = own_terms(arriving[0], *mlp[0])
    arrived_far[0] = to_far(sums[0])
    arriving[1] = to_near(going[1])
    d_half = spread(d_copies)
    going[2] = near_send(*mlp[2])
    received = other_core(back_rows(1, out_pairs))
    out_total = back_rows(0, out_pairs, received)
    d_half, arriving[1], arrived_far[0], going[2], out_total = hold(
        d_half, arriving[1], arrived_far[0], going[2], out_total
    )

    sums[1] = own_terms(arriving[1], *mlp[1])
    arrived_far[1] = to_far(sums[1])
    arriving[2] = to_near(going[2])
    out_total = among_four(out_total.reshape(4, rows, width))
    d_branch = ([d_half, other_core(d_half)], 0)
    d_attended = attended_gradient(d_branch, w_attn, out_column, q_width)
    d_attended = d_attended.reshape(2, 2, 2 * rows, q_width)
    d_q, d_k, d_v = attend_back(qkv4, kv, kv_block, q_info, k_info, q_width, lse, d_attended)
    if sizes["xh"] > 1:
        d_k = lax.psum_scatter(d_k, "xh", scatter_dimension=0, tiled=True)
        d_v = lax.psum_scatter(d_v, "xh", scatter_dimension=0, tiled=True)
    d_projected, head_gains = project_back(
        raw,
        d_q.reshape(-1, q_width),
        d_k.reshape(-1, HEAD_SIZE),
        d_v.reshape(-1, HEAD_SIZE),
        g_q,
        g_k,
        cosine,
        sine,
        q_width,
    )
    in_pair = [(d_projected, w_attn, 0, q_width + 2 * HEAD_SIZE)]
    received = other_core(back_rows(1, in_pair))
    terms = back_rows(0, in_pair, received)
    attention = [(([normed_in], 0), d_projected), (d_branch, attended)]
    going[3] = near_send(*attention)
    terms, arriving[2], arrived_far[1], out_total, going[3] = hold(
        terms, arriving[2], arrived_far[1], out_total, going[3]
    )

    arriving[3] = to_near(going[3])
    sums[2] = own_terms(arriving[2], *mlp[2])
    arrived_far[2] = to_far(sums[2])
    terms = among_four(terms.reshape(4, rows, width))
    output = plain_sum(out_total, middle)
    head_gains = all_sum(head_gains, sizes, ("c", "xl"))
    terms, arriving[3], arrived_far[2], head_gains = hold(terms, arriving[3], arrived_far[2], head_gains)

    sums[3] = own_terms(arriving[3], *attention)
    arrived_far[3] = to_far(sums[3])
    back = jnp.concatenate([far_total(sums[j][0], arrived_far[j]) for j in range(CHUNKS)], axis=2)
    back = exchange(back)
    (token_grad,) = norm_back_step(terms, copies, d_middle, 0, g_attn, 1)
    token_grad, output = reorder([token_grad, output], places, True)
    head_gains = all_sum(head_gains, sizes, ("zl", "y"))
    back, arrived_far[3], head_gains = hold(back, arrived_far[3], head_gains)

    last = exchange(far_total(sums[3][0], arrived_far[3]))
    head_gains = all_sum(head_gains, sizes, ("xh", "zh"))
    grad_gate_up, grad_down, grad_mlp_gain = unpack_chunks(
        back, w_gate_up_rows, mlp_gain.astype(F32).reshape(owned, 1), chunk
    )
    grad_qkv, grad_out, grad_attn_gain = unpack_attention(
        last, w_qkv_rows, attn_gain.astype(F32).reshape(owned, 1)
    )
    at = device_index(sizes) * small
    grad_q_gain = lax.dynamic_slice(head_gains[0], (at,), (small,))
    grad_k_gain = lax.dynamic_slice(head_gains[1], (at,), (small,))
    return (
        output[None],
        token_grad[None],
        grad_qkv,
        grad_out,
        grad_gate_up,
        grad_down,
        grad_attn_gain.reshape(owned),
        grad_q_gain,
        grad_k_gain,
        grad_mlp_gain.reshape(owned),
    )


def solution(mesh):
    dp, seq = mesh.shape["dp"], mesh.shape["seq"]
    fine = Mesh(mesh.devices.reshape(dp // 4, 2, 2, seq // 4, 2, 2), AXES)
    sizes = dict(fine.shape)
    dp_axes, seq_axes = ("zh", "zl", "y"), ("xh", "xl", "c")
    token, weight, vector = P(dp_axes, seq_axes, None), P(AXES, None), P(AXES)
    wide = P(AXES, None, None)

    def shards(*args):
        return layer(sizes, *args)

    return jax.shard_map(
        shards,
        mesh=fine,
        in_specs=(token, P(dp_axes, seq_axes), weight, weight, wide, weight, vector, vector, vector, vector, token),
        out_specs=(token, token, weight, weight, wide, weight, vector, vector, vector, vector),
        check_vma=False,
    )
```

time: 876 us -> 624 us (0.71)
  Pallas kernels: 0 us -> 152 us
  matrix products: 121 us -> 0 us
  other arithmetic: 119 us -> 14.7 us
  local copies, waits for them, and re-layouts: 133 us -> 38.9 us
  waiting for transfers between devices: 384 us -> 327 us
  starting transfers between devices: 109 us -> 82.6 us
    pallas_call x0 -> x34, Pallas kernels: none -> 152 us  [the longest x32 150 us: run(): pl.pallas_call(kernel, grid=grid, in_specs=in_specs, out_specs=out_specs,...]
    dot_general x40 -> x0, matrix products: 115 us -> none  [the longest x16 50.8 us: dot_nt(): lax.dot_general(left, right, (((1,), (1,)), ((), ())), preferred_element_...]
    ppermute x76 -> x37, waiting for transfers between devices: 346 us -> 250 us  [the longest x10 94.4 us: all_sum(): lax.ppermute(value, axis, [((i + k) % sizes[axis], i) for i in range(size...]
    all_to_all x0 -> x7, waiting for transfers between devices: none -> 75 us  [among_four(): return lax.all_to_all(value, ('zl', 'xl'), 0, 0, tiled=True)]
    ppermute x76 -> x37, starting transfers between devices: 70.1 us -> 32.1 us  [the longest x10 12.7 us: all_sum(): lax.ppermute(value, axis, [((i + k) % sizes[axis], i) for i in range(size...]
    all_to_all x10 -> x4, waiting for transfers between devices: 38 us -> 2.16 us  [exchange(): return lax.all_to_all(value, TEAM, 0, 0, tiled=True)]
    all_to_all x0 -> x7, starting transfers between devices: none -> 32.8 us  [among_four(): return lax.all_to_all(value, ('zl', 'xl'), 0, 0, tiled=True)]
    concatenate x24 -> x4, other arithmetic: 34.6 us -> 2.01 us  [the longest x1 1.58 us: layer(): jnp.concatenate([far_total(sums[j][0], arrived_far[j]) for j in range(CHU...]
  transfers between devices with their start and end apart: 86 -> 48, of which waited for: 37 -> 25; matrix products, arithmetic and copies ran while one was open for 28% -> 2% of each run, Pallas kernels for 0% -> 19%
where the time goes in v2:
time: 624 us; the launch traced here: 618 us
  waiting for transfers between devices  327 us (52%)
  Pallas kernels  152 us (24%)
  starting transfers between devices  82.6 us (13%)
  local copies, waits for them, and re-layouts  38.9 us (6%)
  other arithmetic  14.7 us (2%)
    pallas_call x32, Pallas kernels, run(): pl.pallas_call(kernel, grid=grid, in_specs=in_specs, out_specs=out_specs,...  150 us
    ppermute x10, waiting for transfers between devices, all_sum(): lax.ppermute(value, axis, [((i + k) % sizes[axis], i) for i in range(size...  94.4 us
    all_to_all x7, waiting for transfers between devices, among_four(): return lax.all_to_all(value, ('zl', 'xl'), 0, 0, tiled=True)  75 us
    ppermute x8, waiting for transfers between devices, near_blocks(): lax.ppermute(block, ('y', 'xh'), [(b, a) for a, b in self.shifted(n)])  61.5 us
    ppermute x4, waiting for transfers between devices, to_far(): lax.ppermute(value, 'zh', [(i, (i + k) % self.zh) for i in range(self.zh)])  55.1 us
    unnamed x194, local copies, waits for them, and re-layouts  32.8 us
    all_to_all x7, starting transfers between devices, among_four(): return lax.all_to_all(value, ('zl', 'xl'), 0, 0, tiled=True)  32.8 us
    ppermute x4, waiting for transfers between devices, far_blocks(): lax.ppermute(block, 'zh', [((i + k) % self.zh, i) for i in range(self.zh)])  25.3 us
  transfers between devices with their start and end apart: 48, of which 25 were waited for; matrix products, arithmetic and copies ran while one was open for 2% of the time, Pallas kernels for 19%

profile of v2, /device:TPU:0, one launch (start us, length us, event | category | flops | bytes accessed | tf_op | source)
XLA Modules:
  0.0 617.6 jit_solution(17350401650834618004)
XLA Ops:
  3.8 5.2 all-to-all-start
  12.6 8.6 %collective-permute-done.1 = bf16[32,264]{1,0:T(8,128)(2,1)S(1)} collective-permute-done((bf16[32,264]{1,0:T(8,128)(2,1)S(1)}, bf16[32,264]{1,0:T(8,128)(2,1)S(1)}, u32[]{:S(2)}, u32[]{:S(2)}) %collective-permute-start.1) | collective-permute-done | bytes 16928 | tf_op jit(solution)/shard_map/ppermute | solution.py:96
  41.8 15.7 %collective-permute-done.5 = bf16[32,264]{1,0:T(8,128)(2,1)S(1)} collective-permute-done((bf16[32,264]{1,0:T(8,128)(2,1)S(1)}, bf16[32,264]{1,0:T(8,128)(2,1)S(1)}, u32[]{:S(2)}, u32[]{:S(2)}) %collective-permute-start.5) | collective-permute-done | bytes 16928 | tf_op jit(solution)/shard_map/ppermute | solution.py:96
  60.1 20.6 %collective-permute-done.6 = bf16[32,264]{1,0:T(8,128)(2,1)S(1)} collective-permute-done((bf16[32,264]{1,0:T(8,128)(2,1)S(1)}, bf16[32,264]{1,0:T(8,128)(2,1)S(1)}, u32[]{:S(2)}, u32[]{:S(2)}) %collective-permute-start.6) | collective-permute-done | bytes 16928 | tf_op jit(solution)/shard_map/ppermute | solution.py:96
  83.0 5.8 all-to-all-start.2
  99.4 28.5 %collective-permute-done.7.refs_3_.refs_4_ = bf16[512,768]{1,0:T(8,128)(2,1)} collective-permute-done((bf16[512,768]{1,0:T(8,128)(2,1)}, bf16[512,768]{1,0:T(8,128)(2,1)}, u32[]{:S(2)}, u32[]{:S(2)}) %collective-permute-start.7) | collective-permute-done | bytes 786464 | tf_op jit(solution)/shard_map/ppermute | solution.py:66
  127.9 22.7 %collective-permute-done.9.refs_1_.refs_4_ = bf16[512,768]{1,0:T(8,128)(2,1)} collective-permute-done((bf16[512,768]{1,0:T(8,128)(2,1)S(1)}, bf16[512,768]{1,0:T(8,128)(2,1)}, u32[]{:S(2)}, u32[]{:S(2)}) %collective-permute-start.9) | collective-permute-done | bytes 786464 | tf_op jit(solution)/shard_map/ppermute | solution.py:53
  154.7 7.0 %collective-permute-done.10.x1.dy1.refs_3_ = bf16[512,4096]{1,0:T(8,128)(2,1)} collective-permute-done((bf16[512,4096]{1,0:T(8,128)(2,1)}, bf16[512,4096]{1,0:T(8,128)(2,1)}, u32[]{:S(2)}, u32[]{:S(2)}) %collective-permute-start.10) | collective-permute-done | bytes 4194336 | tf_op jit(solution)/shard_map/ppermute | solution.py:85
  162.8 8.3 %shard_map.189 = (bf16[1024,2048]{1,0:T(8,128)(2,1)}, f32[1024,384]{1,0:T(8,128)}, bf16[1024,512]{1,0:T(8,128)(2,1)S(1)}) custom-call(bf16[512,4096]{1,0:T(8,128)(2,1)} %bitcast.13.x0.dy0.refs_2_, bf16[512,4096]{1,0:T(8,128)(2,1)} %collective-permute-done.10.x1.dy1.refs_3_, bf16[512,768]{1,0:T(8,128)(2,1)S(1)} %bitcast.92, ...), custom_call_target="tpu_custom_call" | custom-call | flops 214748364800 | bytes 1940787200 | tf_op jit(solution)/shard_map/pallas_call | solution.py:127
  192.5 40.2 %all-to-all-done.3.parts_ref = bf16[4,128,2048]{2,1,0:T(8,128)(2,1)S(1)} async-done(((bf16[4,128,2048]{2,1,0:T(8,128)(2,1)}), bf16[4,128,2048]{2,1,0:T(8,128)(2,1)S(1)}, u32[]{:S(2)}, u32[]{:S(2)}) %all-to-all-start.3) | async-done | bytes 2097184 | tf_op jit(solution)/shard_map/all_to_all | solution.py:77
  241.9 18.7 %collective-permute-done.15.refs_3_.refs_10_ = bf16[512,768]{1,0:T(8,128)(2,1)S(1)} collective-permute-done((bf16[512,768]{1,0:T(8,128)(2,1)}, bf16[512,768]{1,0:T(8,128)(2,1)S(1)}, u32[]{:S(2)}, u32[]{:S(2)}) %collective-permute-start.15) | collective-permute-done | bytes 786464 | tf_op jit(solution)/shard_map/ppermute | solution.py:66
  261.4 14.3 %collective-permute-done.16.refs_2_.refs_13_ = bf16[512,768]{1,0:T(8,128)(2,1)S(1)} collective-permute-done((bf16[512,768]{1,0:T(8,128)(2,1)}, bf16[512,768]{1,0:T(8,128)(2,1)S(1)}, u32[]{:S(2)}, u32[]{:S(2)}) %collective-permute-start.16) | collective-permute-done | bytes 786464 | tf_op jit(solution)/shard_map/ppermute | solution.py:66
  287.9 7.6 %shard_map.194 = (bf16[1024,256]{1,0:T(8,128)(2,1)S(1)}, bf16[1024,512]{1,0:T(8,128)(2,1)S(1)}) custom-call(bf16[512,2048]{1,0:T(8,128)(2,1)} %bitcast.80, bf16[512,2048]{1,0:T(8,128)(2,1)} %copy-done.93, bf16[512,4096]{1,0:T(8,128)(2,1)} %bitcast.13.x0.dy0.refs_2_, bf16[512,4096]{1,0:T(8,128)(2,1)} %collective-permute-done.10.x1.dy1.refs_3_, ...), custom_call_target="tpu_custom_call" | custom-call | flops 322122547200 | bytes 1730150400 | tf_op jit(solution)/shard_map/pallas_call | solution.py:127
  295.5 8.1 %shard_map.196 = (bf16[1024,256]{1,0:T(8,128)(2,1)S(1)}, bf16[1024,512]{1,0:T(8,128)(2,1)S(1)}) custom-call(bf16[512,2048]{1,0:T(8,128)(2,1)} %bitcast.81, bf16[512,2048]{1,0:T(8,128)(2,1)} %copy-done.93, bf16[512,4096]{1,0:T(8,128)(2,1)} %bitcast.13.x0.dy0.refs_2_, bf16[512,4096]{1,0:T(8,128)(2,1)} %collective-permute-done.10.x1.dy1.refs_3_, ...), custom_call_target="tpu_custom_call" | custom-call | flops 322122547200 | bytes 1730150400 | tf_op jit(solution)/shard_map/pallas_call | solution.py:127
  309.4 7.4 %shard_map.197 = (bf16[1024,256]{1,0:T(8,128)(2,1)S(1)}, bf16[1024,512]{1,0:T(8,128)(2,1)S(1)}) custom-call(bf16[512,2048]{1,0:T(8,128)(2,1)} %bitcast.82, bf16[512,2048]{1,0:T(8,128)(2,1)} %copy-done.93, bf16[512,4096]{1,0:T(8,128)(2,1)} %bitcast.13.x0.dy0.refs_2_, bf16[512,4096]{1,0:T(8,128)(2,1)} %collective-permute-done.10.x1.dy1.refs_3_, ...), custom_call_target="tpu_custom_call" | custom-call | flops 322122547200 | bytes 1730150400 | tf_op jit(solution)/shard_map/pallas_call | solution.py:127
  317.7 7.8 %shard_map.198 = bf16[512,2048]{1,0:T(8,128)(2,1)} custom-call(bf16[1024,512]{1,0:T(8,128)(2,1)} %copy-done.71, bf16[1024,512]{1,0:T(8,128)(2,1)} %copy-done.68, bf16[1024,512]{1,0:T(8,128)(2,1)} %copy-done.65, bf16[512,768]{1,0:T(8,128)(2,1)S(1)} %copy-done.20, bf16[512,768]{1,0:T(8,128)(2,1)} %collective-permute-done.9.refs_1_.refs_4_, ...), custom_call_target="tpu_custom_call" | custom-call | flops 322122547200 | bytes 1468006400 | tf_op jit(solution)/shard_map/pallas_call | solution.py:127
  337.0 7.9 %shard_map.199 = bf16[512,2048]{1,0:T(8,128)(2,1)} custom-call(bf16[1024,512]{1,0:T(8,128)(2,1)} %copy-done.71, bf16[1024,512]{1,0:T(8,128)(2,1)} %copy-done.68, bf16[1024,512]{1,0:T(8,128)(2,1)} %copy-done.65, bf16[512,768]{1,0:T(8,128)(2,1)S(1)} %copy-done.20, bf16[512,768]{1,0:T(8,128)(2,1)} %collective-permute-done.9.refs_1_.refs_4_, ...), custom_call_target="tpu_custom_call" | custom-call | flops 322122547200 | bytes 1677721600 | tf_op jit(solution)/shard_map/pallas_call | solution.py:127
  356.6 18.9 %all-to-all-done.5.parts_ref = bf16[4,128,2048]{2,1,0:T(8,128)(2,1)} async-done(((bf16[4,128,2048]{2,1,0:T(8,128)(2,1)}), bf16[4,128,2048]{2,1,0:T(8,128)(2,1)}, u32[]{:S(2)}, u32[]{:S(2)}) %all-to-all-start.5) | async-done | bytes 2097184 | tf_op jit(solution)/shard_map/all_to_all | solution.py:77
  385.8 6.4 %shard_map.202 = (bf16[512,768]{1,0:T(8,128)(2,1)S(1)}, bf16[512,768]{1,0:T(8,128)(2,1)}) custom-call(bf16[512,2048]{1,0:T(8,128)(2,1)} %bitcast.83, bf16[512,2048]{1,0:T(8,128)(2,1)} %copy-done.93, bf16[512,4096]{1,0:T(8,128)(2,1)} %bitcast.13.x0.dy0.refs_2_, bf16[512,4096]{1,0:T(8,128)(2,1)} %collective-permute-done.10.x1.dy1.refs_3_, ...), custom_call_target="tpu_custom_call" | custom-call | flops 161061273600 | bytes 1730150400 | tf_op jit(solution)/shard_map/pallas_call | solution.py:127
  394.4 5.3 shard_map.205
  399.7 30.3 %collective-permute-done.23 = bf16[512,768]{1,0:T(8,128)(2,1)} collective-permute-done((bf16[512,768]{1,0:T(8,128)(2,1)}, bf16[512,768]{1,0:T(8,128)(2,1)}, u32[]{:S(2)}, u32[]{:S(2)}) %collective-permute-start.23) | collective-permute-done | bytes 786464 | tf_op jit(solution)/shard_map/ppermute | solution.py:73
  432.6 6.3 %shard_map.211 = (bf16[512,768]{1,0:T(8,128)(2,1)S(1)}, bf16[512,768]{1,0:T(8,128)(2,1)}) custom-call(bf16[512,2048]{1,0:T(8,128)(2,1)} %bitcast.84, bf16[512,2048]{1,0:T(8,128)(2,1)} %copy-done.93, bf16[512,4096]{1,0:T(8,128)(2,1)} %bitcast.13.x0.dy0.refs_2_, bf16[512,4096]{1,0:T(8,128)(2,1)} %collective-permute-done.10.x1.dy1.refs_3_, ...), custom_call_target="tpu_custom_call" | custom-call | flops 161061273600 | bytes 1730150400 | tf_op jit(solution)/shard_map/pallas_call | solution.py:127
  439.8 5.3 all-to-all-start.7
  450.8 5.6 shard_map.207
  472.0 5.4 collective-permute-done.28
  477.4 10.3 %all-to-all-done.7.parts_ref = bf16[4,128,2048]{2,1,0:T(8,128)(2,1)} async-done(((bf16[4,128,2048]{2,1,0:T(8,128)(2,1)}), bf16[4,128,2048]{2,1,0:T(8,128)(2,1)}, u32[]{:S(2)}, u32[]{:S(2)}) %all-to-all-start.7) | async-done | bytes 2097184 | tf_op jit(solution)/shard_map/all_to_all | solution.py:77
  494.2 5.5 shard_map.213
  505.1 8.7 %collective-permute-done.32 = f32[8,128]{1,0:T(8,128)S(1)} collective-permute-done((f32[8,128]{1,0:T(8,128)S(1)}, f32[8,128]{1,0:T(8,128)S(1)}, u32[]{:S(2)}, u32[]{:S(2)}) %collective-permute-start.32) | collective-permute-done | bytes 4128 | tf_op jit(solution)/shard_map/ppermute | solution.py:96
  516.7 19.3 %collective-permute-done.30 = bf16[512,768]{1,0:T(8,128)(2,1)S(1)} collective-permute-done((bf16[512,768]{1,0:T(8,128)(2,1)S(1)}, bf16[512,768]{1,0:T(8,128)(2,1)S(1)}, u32[]{:S(2)}, u32[]{:S(2)}) %collective-permute-start.30) | collective-permute-done | bytes 786464 | tf_op jit(solution)/shard_map/ppermute | solution.py:73
  545.9 5.4 shard_map.217
  553.3 36.7 %collective-permute-done.34 = f32[8,128]{1,0:T(8,128)S(1)} collective-permute-done((f32[8,128]{1,0:T(8,128)S(1)}, f32[8,128]{1,0:T(8,128)S(1)}, u32[]{:S(2)}, u32[]{:S(2)}) %collective-permute-start.34) | collective-permute-done | bytes 4128 | tf_op jit(solution)/shard_map/ppermute | solution.py:96
  605.9 7.7 %shard_map.219 = (f32[64,2,6144]{2,1,0:T(2,128)}, f32[64,6144]{1,0:T(8,128)}, f32[64,1]{1,0:T(8,128)S(1)}) custom-call(bf16[8,64,2304]{2,1,0:T(8,128)(2,1)} %all-to-all-done.9.back_ref, bf16[64,2,6144]{2,1,0:T(2,128)(2,1)S(1)} %copy-done.2, f32[64,1]{1,0:T(8,128)S(1)} %copy.38.gain_ref), custom_call_target="tpu_custom_call" | custom-call | bytes 865126400 | tf_op jit(solution)/shard_map/pallas_call | solution.py:127
  (359 shorter events, 204.2 us)
Async XLA Ops:
  3.8 28.9 %all-to-all-start = ((bf16[8,64,768]{2,1,0:T(8,128)(2,1)}), bf16[8,64,768]{2,1,0:T(8,128)(2,1)S(1)}, u32[]{:S(2)}, u32[]{:S(2)}) async-start(bf16[8,64,768]{2,1,0:T(8,128)(2,1)} %shard_map.186), calls=%async_computation | async-start | bytes 1572864 | tf_op jit(solution)/shard_map/all_to_all | solution.py:89
  32.7 50.3 %all-to-all-start.1 = ((bf16[8,64,2304]{2,1,0:T(8,128)(2,1)}), bf16[8,64,2304]{2,1,0:T(8,128)(2,1)}, u32[]{:S(2)}, u32[]{:S(2)}) async-start(bf16[8,64,2304]{2,1,0:T(8,128)(2,1)} %shard_map.188), calls=%async_computation.1 | async-start | bytes 4718592 | tf_op jit(solution)/shard_map/all_to_all | solution.py:89
  37.1 43.7 %collective-permute-start.3 = (bf16[512,768]{1,0:T(8,128)(2,1)S(1)}, bf16[512,768]{1,0:T(8,128)(2,1)S(1)}, u32[]{:S(2)}, u32[]{:S(2)}) collective-permute-start(bf16[512,768]{1,0:T(8,128)(2,1)S(1)} %bitcast.90), channel_id=1, source_target_pairs={{4,0},{0,4},{5,1},{1,5},{6,2},{2,6},{7,3},{3,7},{12,8},{8,12},{13,... | collective-permute-start | bytes 2359304 | tf_op jit(solution)/shard_map/ppermute | solution.py:66
  38.7 42.1 %collective-permute-start.4 = (bf16[512,768]{1,0:T(8,128)(2,1)S(1)}, bf16[512,768]{1,0:T(8,128)(2,1)}, u32[]{:S(2)}, u32[]{:S(2)}) collective-permute-start(bf16[512,768]{1,0:T(8,128)(2,1)S(1)} %bitcast.91), channel_id=1, source_target_pairs={{16,0},{0,16},{17,1},{1,17},{18,2},{2,18},{19,3},{3,19},{20,4},{4,... | collective-permute-start | bytes 2359304 | tf_op jit(solution)/shard_map/ppermute | solution.py:53
  57.4 23.3 %collective-permute-start.6 = (bf16[32,264]{1,0:T(8,128)(2,1)S(1)}, bf16[32,264]{1,0:T(8,128)(2,1)S(1)}, u32[]{:S(2)}, u32[]{:S(2)}) collective-permute-start(bf16[32,264]{1,0:T(8,128)(2,1)S(1)} %add.258), channel_id=1, source_target_pairs={{16,0},{0,16},{17,1},{1,17},{18,2},{2,18},{19,3},{3,19},{20,4},{4,... | collective-permute-start | bytes 50696 | tf_op jit(solution)/shard_map/ppermute | solution.py:96
  83.0 71.2 %all-to-all-start.2 = ((bf16[4,128,4096]{2,1,0:T(8,128)(2,1)}), bf16[4,128,4096]{2,1,0:T(8,128)(2,1)}, u32[]{:S(2)}, u32[]{:S(2)}) async-start(bf16[4,128,4096]{2,1,0:T(8,128)(2,1)} %copy-done), calls=%async_computation.2 | async-start | bytes 8388608 | tf_op jit(solution)/shard_map/all_to_all | solution.py:77
  92.1 35.9 %collective-permute-start.8 = (bf16[512,768]{1,0:T(8,128)(2,1)S(1)}, bf16[512,768]{1,0:T(8,128)(2,1)}, u32[]{:S(2)}, u32[]{:S(2)}) collective-permute-start(bf16[512,768]{1,0:T(8,128)(2,1)S(1)} %get-tuple-element.152.refs_0_.refs_3_), channel_id=1, source_target_pairs={{4,0},{0,4},{5,1},{1,5},{6,2},{2,6},{7,3},{3,7},{12,8},{8,12},{13,... | collective-permute-start | bytes 2359304 | tf_op jit(solution)/shard_map/ppermute | solution.py:66
  93.6 57.1 %collective-permute-start.9 = (bf16[512,768]{1,0:T(8,128)(2,1)S(1)}, bf16[512,768]{1,0:T(8,128)(2,1)}, u32[]{:S(2)}, u32[]{:S(2)}) collective-permute-start(bf16[512,768]{1,0:T(8,128)(2,1)S(1)} %get-tuple-element.152.refs_0_.refs_3_), channel_id=1, source_target_pairs={{16,0},{0,16},{17,1},{1,17},{18,2},{2,18},{19,3},{3,19},{20,4},{4,... | collective-permute-start | bytes 2359304 | tf_op jit(solution)/shard_map/ppermute | solution.py:53
  94.9 33.0 %collective-permute-start.7 = (bf16[512,768]{1,0:T(8,128)(2,1)}, bf16[512,768]{1,0:T(8,128)(2,1)}, u32[]{:S(2)}, u32[]{:S(2)}) collective-permute-start(bf16[512,768]{1,0:T(8,128)(2,1)} %collective-permute-done.4.refs_1_.refs_2_), channel_id=1, source_target_pairs={{4,0},{0,4},{5,1},{1,5},{6,2},{2,6},{7,3},{3,7},{12,8},{8,12},{13,... | collective-permute-start | bytes 2359304 | tf_op jit(solution)/shard_map/ppermute | solution.py:66
  186.8 45.9 %all-to-all-start.3 = ((bf16[4,128,2048]{2,1,0:T(8,128)(2,1)}), bf16[4,128,2048]{2,1,0:T(8,128)(2,1)S(1)}, u32[]{:S(2)}, u32[]{:S(2)}) async-start(bf16[4,128,2048]{2,1,0:T(8,128)(2,1)} %bitcast.89), calls=%async_computation.3 | async-start | bytes 4194304 | tf_op jit(solution)/shard_map/all_to_all | solution.py:77
  190.4 45.3 %collective-permute-start.12 = (bf16[512,768]{1,0:T(8,128)(2,1)}, bf16[512,768]{1,0:T(8,128)(2,1)}, u32[]{:S(2)}, u32[]{:S(2)}) collective-permute-start(bf16[512,768]{1,0:T(8,128)(2,1)} %collective-permute-done.9.refs_1_.refs_4_), channel_id=1, source_target_pairs={{4,0},{0,4},{5,1},{1,5},{6,2},{2,6},{7,3},{3,7},{12,8},{8,12},{13,... | collective-permute-start | bytes 2359304 | tf_op jit(solution)/shard_map/ppermute | solution.py:66
  192.0 43.7 %collective-permute-start.13 = (bf16[512,768]{1,0:T(8,128)(2,1)}, bf16[512,768]{1,0:T(8,128)(2,1)}, u32[]{:S(2)}, u32[]{:S(2)}) collective-permute-start(bf16[512,768]{1,0:T(8,128)(2,1)} %get-tuple-element.161.refs_0_.refs_7_), channel_id=1, source_target_pairs={{4,0},{0,4},{5,1},{1,5},{6,2},{2,6},{7,3},{3,7},{12,8},{8,12},{13,... | collective-permute-start | bytes 2359304 | tf_op jit(solution)/shard_map/ppermute | solution.py:66
  192.5 43.2 %collective-permute-start.14 = (bf16[512,768]{1,0:T(8,128)(2,1)}, bf16[512,768]{1,0:T(8,128)(2,1)}, u32[]{:S(2)}, u32[]{:S(2)}) collective-permute-start(bf16[512,768]{1,0:T(8,128)(2,1)} %get-tuple-element.161.refs_0_.refs_7_), channel_id=1, source_target_pairs={{16,0},{0,16},{17,1},{1,17},{18,2},{2,18},{19,3},{3,19},{20,4},{4,... | collective-permute-start | bytes 2359304 | tf_op jit(solution)/shard_map/ppermute | solution.py:53
  235.7 45.5 %all-to-all-start.4 = ((bf16[4,128,2048]{2,1,0:T(8,128)(2,1)}), bf16[4,128,2048]{2,1,0:T(8,128)(2,1)S(1)}, u32[]{:S(2)}, u32[]{:S(2)}) async-start(bf16[4,128,2048]{2,1,0:T(8,128)(2,1)} %copy-done.7), calls=%async_computation.4 | async-start | bytes 4194304 | tf_op jit(solution)/shard_map/all_to_all | solution.py:77
  241.3 34.3 %collective-permute-start.16 = (bf16[512,768]{1,0:T(8,128)(2,1)}, bf16[512,768]{1,0:T(8,128)(2,1)S(1)}, u32[]{:S(2)}, u32[]{:S(2)}) collective-permute-start(bf16[512,768]{1,0:T(8,128)(2,1)} %get-tuple-element.167.refs_0_.refs_11_), channel_id=1, source_target_pairs={{4,0},{0,4},{5,1},{1,5},{6,2},{2,6},{7,3},{3,7},{12,8},{8,12},{13,... | collective-permute-start | bytes 2359304 | tf_op jit(solution)/shard_map/ppermute | solution.py:66
  241.9 37.3 %collective-permute-start.17 = (bf16[512,768]{1,0:T(8,128)(2,1)}, bf16[512,768]{1,0:T(8,128)(2,1)}, u32[]{:S(2)}, u32[]{:S(2)}) collective-permute-start(bf16[512,768]{1,0:T(8,128)(2,1)} %get-tuple-element.167.refs_0_.refs_11_), channel_id=1, source_target_pairs={{16,0},{0,16},{17,1},{1,17},{18,2},{2,18},{19,3},{3,19},{20,4},{4,... | collective-permute-start | bytes 2359304 | tf_op jit(solution)/shard_map/ppermute | solution.py:53
  281.2 28.1 %collective-permute-start.19 = (bf16[512,768]{1,0:T(8,128)(2,1)}, bf16[512,768]{1,0:T(8,128)(2,1)}, u32[]{:S(2)}, u32[]{:S(2)}) collective-permute-start(bf16[512,768]{1,0:T(8,128)(2,1)} %collective-permute-done.17.refs_1_.refs_12_), channel_id=1, source_target_pairs={{4,0},{0,4},{5,1},{1,5},{6,2},{2,6},{7,3},{3,7},{12,8},{8,12},{13,... | collective-permute-start | bytes 2359304 | tf_op jit(solution)/shard_map/ppermute | solution.py:66
  325.6 53.9 %collective-permute-start.21 = (bf16[1024,768]{1,0:T(8,128)(2,1)}, bf16[1024,768]{1,0:T(8,128)(2,1)}, u32[]{:S(2)}, u32[]{:S(2)}) collective-permute-start(bf16[1024,768]{1,0:T(8,128)(2,1)} %shard_map.195), channel_id=1, source_target_pairs={{0,4},{4,0},{1,5},{5,1},{2,6},{6,2},{3,7},{7,3},{8,12},{12,8},{9,1... | collective-permute-start | bytes 4718600 | tf_op jit(solution)/shard_map/ppermute | solution.py:70
  332.2 62.2 %collective-permute-start.24 = (bf16[512,2048]{1,0:T(8,128)(2,1)}, bf16[512,2048]{1,0:T(8,128)(2,1)}, u32[]{:S(2)}, u32[]{:S(2)}) collective-permute-start(bf16[512,2048]{1,0:T(8,128)(2,1)} %shard_map.204), channel_id=1, source_target_pairs={{0,1},{1,0},{2,3},{3,2},{4,5},{5,4},{6,7},{7,6},{8,9},{9,8},{10,11... | collective-permute-start | bytes 6291464 | tf_op jit(solution)/shard_map/ppermute | solution.py:85
  344.9 30.6 %all-to-all-start.5 = ((bf16[4,128,2048]{2,1,0:T(8,128)(2,1)}), bf16[4,128,2048]{2,1,0:T(8,128)(2,1)}, u32[]{:S(2)}, u32[]{:S(2)}) async-start(bf16[4,128,2048]{2,1,0:T(8,128)(2,1)} %bitcast.122), calls=%async_computation.5 | async-start | bytes 4194304 | tf_op jit(solution)/shard_map/all_to_all | solution.py:77
  379.5 50.5 %all-to-all-start.6 = ((bf16[4,128,2048]{2,1,0:T(8,128)(2,1)}), bf16[4,128,2048]{2,1,0:T(8,128)(2,1)}, u32[]{:S(2)}, u32[]{:S(2)}) async-start(bf16[4,128,2048]{2,1,0:T(8,128)(2,1)} %get-tuple-element.176), calls=%async_computation.6 | async-start | bytes 4194304 | tf_op jit(solution)/shard_map/all_to_all | solution.py:77
  384.1 45.9 %collective-permute-start.22 = (bf16[1024,768]{1,0:T(8,128)(2,1)}, bf16[1024,768]{1,0:T(8,128)(2,1)}, u32[]{:S(2)}, u32[]{:S(2)}) collective-permute-start(bf16[1024,768]{1,0:T(8,128)(2,1)} %copy-done.45), channel_id=1, source_target_pairs={{0,4},{4,0},{1,5},{5,1},{2,6},{6,2},{3,7},{7,3},{8,12},{12,8},{9,1... | collective-permute-start | bytes 4718600 | tf_op jit(solution)/shard_map/ppermute | solution.py:70
  393.1 36.9 %collective-permute-start.23 = (bf16[512,768]{1,0:T(8,128)(2,1)}, bf16[512,768]{1,0:T(8,128)(2,1)}, u32[]{:S(2)}, u32[]{:S(2)}) collective-permute-start(bf16[512,768]{1,0:T(8,128)(2,1)} %get-tuple-element.179), channel_id=1, source_target_pairs={{0,16},{16,0},{1,17},{17,1},{2,18},{18,2},{3,19},{19,3},{4,20},{20... | collective-permute-start | bytes 2359304 | tf_op jit(solution)/shard_map/ppermute | solution.py:73
  430.0 47.4 %collective-permute-start.27 = (bf16[1024,768]{1,0:T(8,128)(2,1)}, bf16[1024,768]{1,0:T(8,128)(2,1)}, u32[]{:S(2)}, u32[]{:S(2)}) collective-permute-start(bf16[1024,768]{1,0:T(8,128)(2,1)} %copy-done.43), channel_id=1, source_target_pairs={{0,4},{4,0},{1,5},{5,1},{2,6},{6,2},{3,7},{7,3},{8,12},{12,8},{9,1... | collective-permute-start | bytes 4718600 | tf_op jit(solution)/shard_map/ppermute | solution.py:70
  439.7 37.7 %collective-permute-start.28 = (bf16[512,768]{1,0:T(8,128)(2,1)}, bf16[512,768]{1,0:T(8,128)(2,1)}, u32[]{:S(2)}, u32[]{:S(2)}) collective-permute-start(bf16[512,768]{1,0:T(8,128)(2,1)} %get-tuple-element.188), channel_id=1, source_target_pairs={{0,16},{16,0},{1,17},{17,1},{2,18},{18,2},{3,19},{19,3},{4,20},{20... | collective-permute-start | bytes 2359304 | tf_op jit(solution)/shard_map/ppermute | solution.py:73
  439.8 48.0 %all-to-all-start.7 = ((bf16[4,128,2048]{2,1,0:T(8,128)(2,1)}), bf16[4,128,2048]{2,1,0:T(8,128)(2,1)}, u32[]{:S(2)}, u32[]{:S(2)}) async-start(bf16[4,128,2048]{2,1,0:T(8,128)(2,1)} %bitcast.120), calls=%async_computation.7 | async-start | bytes 4194304 | tf_op jit(solution)/shard_map/all_to_all | solution.py:77
  487.8 49.1 %all-to-all-start.8 = ((bf16[4,128,2048]{2,1,0:T(8,128)(2,1)}), bf16[4,128,2048]{2,1,0:T(8,128)(2,1)}, u32[]{:S(2)}, u32[]{:S(2)}) async-start(bf16[4,128,2048]{2,1,0:T(8,128)(2,1)} %bitcast.121), calls=%async_computation.8 | async-start | bytes 4194304 | tf_op jit(solution)/shard_map/all_to_all | solution.py:77
  492.4 44.6 %collective-permute-start.29 = (bf16[1024,768]{1,0:T(8,128)(2,1)}, bf16[1024,768]{1,0:T(8,128)(2,1)}, u32[]{:S(2)}, u32[]{:S(2)}) collective-permute-start(bf16[1024,768]{1,0:T(8,128)(2,1)} %copy-done.44), channel_id=1, source_target_pairs={{0,4},{4,0},{1,5},{5,1},{2,6},{6,2},{3,7},{7,3},{8,12},{12,8},{9,1... | collective-permute-start | bytes 4718600 | tf_op jit(solution)/shard_map/ppermute | solution.py:70
  499.7 36.4 %collective-permute-start.30 = (bf16[512,768]{1,0:T(8,128)(2,1)S(1)}, bf16[512,768]{1,0:T(8,128)(2,1)S(1)}, u32[]{:S(2)}, u32[]{:S(2)}) collective-permute-start(bf16[512,768]{1,0:T(8,128)(2,1)S(1)} %get-tuple-element.194), channel_id=1, source_target_pairs={{0,16},{16,0},{1,17},{17,1},{2,18},{18,2},{3,19},{19,3},{4,20},{20... | collective-permute-start | bytes 2359304 | tf_op jit(solution)/shard_map/ppermute | solution.py:73
  540.1 53.6 %all-to-all-start.9 = ((bf16[8,64,2304]{2,1,0:T(8,128)(2,1)}), bf16[8,64,2304]{2,1,0:T(8,128)(2,1)}, u32[]{:S(2)}, u32[]{:S(2)}) async-start(bf16[8,64,2304]{2,1,0:T(8,128)(2,1)} %pad_maximum_fusion), calls=%async_computation.9 | async-start | bytes 4718592 | tf_op jit(solution)/shard_map/all_to_all | solution.py:89
  551.3 42.4 %collective-permute-start.33 = (bf16[512,768]{1,0:T(8,128)(2,1)S(1)}, bf16[512,768]{1,0:T(8,128)(2,1)}, u32[]{:S(2)}, u32[]{:S(2)}) collective-permute-start(bf16[512,768]{1,0:T(8,128)(2,1)S(1)} %get-tuple-element.209), channel_id=1, source_target_pairs={{0,16},{16,0},{1,17},{17,1},{2,18},{18,2},{3,19},{19,3},{4,20},{20... | collective-permute-start | bytes 2359304 | tf_op jit(solution)/shard_map/ppermute | solution.py:73
  551.4 38.7 %collective-permute-start.34 = (f32[8,128]{1,0:T(8,128)S(1)}, f32[8,128]{1,0:T(8,128)S(1)}, u32[]{:S(2)}, u32[]{:S(2)}) collective-permute-start(f32[8,128]{1,0:T(8,128)S(1)} %copy-done.86), channel_id=1, source_target_pairs={{8,0},{0,8},{9,1},{1,9},{10,2},{2,10},{11,3},{3,11},{12,4},{4,12},... | collective-permute-start | bytes 12296 | tf_op jit(solution)/shard_map/ppermute | solution.py:96
  (112 other events, 1257.7 us)

commit v3 on v2

--- a/solution.py
+++ b/solution.py
@@ -16,12 +16,11 @@
 F32 = jnp.float32
 BF16 = jnp.bfloat16
 SWAP = [(0, 1), (1, 0)]
-DIAGONAL = [(0, 3), (1, 2), (2, 1), (3, 0)]
 TEAM = ("zl", "xl", "c")
 TEAM_SIZE = 8
 AXES = ("zh", "zl", "y", "xh", "xl", "c")
 CHUNKS = 3
-VMEM_LIMIT = 48 << 20
+VMEM_LIMIT = 32 << 20
 WEIGHT = 100
 FORWARD_STEPS = 4
 BACK_STEPS = 2
@@ -85,6 +84,14 @@
     return lax.ppermute(value, "c", SWAP)
 
 
+def other_x(value):
+    return lax.ppermute(value, "xl", SWAP)
+
+
+def other_z(value):
+    return lax.ppermute(value, "zl", SWAP)
+
+
 def exchange(value):
     return lax.all_to_all(value, TEAM, 0, 0, tiled=True)
 
@@ -115,6 +122,10 @@
 
 def dot_tn(left, right):
     return lax.dot_general(left, right, (((0,), (0,)), ((), ())), preferred_element_type=F32)
+
+
+def joined(values, axis=0):
+    return values[0] if len(values) == 1 else jnp.concatenate(values, axis=axis)
 
 
 def shape(dims, dtype):
@@ -159,30 +170,24 @@
         at = jnp.argsort(places) if inverse else places
         moved = [jnp.take(v.reshape(v.shape[:-1] + (count, cut)), at, axis=-2).reshape(v.shape) for v in values]
         if copies:
-            side = jnp.concatenate(moved, axis=-1)
-            return jnp.broadcast_to(side[None], (copies,) + side.shape)
+            moved = [jnp.broadcast_to(v[None], (copies,) + v.shape) for v in moved]
         return moved
-    if copies:
-        outs = [shape((copies, values[0].shape[0], width * len(values)), values[0].dtype)]
-    else:
-        outs = [shape(v.shape, v.dtype) for v in values]
+    outs = [shape(((copies,) if copies else ()) + v.shape, v.dtype) for v in values]
 
     def kernel(places_ref, *refs):
-        for n, source in enumerate(refs[: len(values)]):
+        for source, target in zip(refs[: len(values)], refs[len(values) :]):
             for i in range(count):
-                place = places_ref[i] * cut
+                moving = pl.ds(pl.multiple_of(places_ref[i] * cut, 128), cut)
+                still = pl.ds(i * cut, cut)
                 if copies:
-                    value = source[:, pl.ds(pl.multiple_of(place, 128), cut)]
+                    value = source[:, moving]
                     for copy in range(copies):
-                        refs[-1][copy, :, n * width + i * cut : n * width + (i + 1) * cut] = value
+                        target[copy, :, still] = value
                 else:
-                    moving = pl.ds(pl.multiple_of(place, 128), cut)
-                    still = pl.ds(i * cut, cut)
-                    target = refs[len(values) + n]
                     target[:, moving if inverse else still] = source[:, still if inverse else moving]
 
     size = sum(math.prod(a.shape) * a.dtype.itemsize for a in list(values) + outs)
-    result = pl.pallas_call(
+    return pl.pallas_call(
         kernel,
         grid_spec=pltpu.PrefetchScalarGridSpec(
             num_scalar_prefetch=1,
@@ -194,7 +199,6 @@
         compiler_params=pltpu.CompilerParams(vmem_limit_bytes=VMEM_LIMIT),
         cost_estimate=pl.CostEstimate(flops=0, bytes_accessed=WEIGHT * size, transcendentals=0),
     )(places, *values)
-    return result[0] if copies else result
 
 
 def pack_attention(w_qkv, w_out):
@@ -219,29 +223,31 @@
     owned = w_down.shape[0]
     per = w_down.shape[1] // TEAM_SIZE
 
-    def kernel(gate_up_ref, down_ref, target):
+    def kernel(gate_up_ref, down_ref, *targets):
         for j in range(CHUNKS):
-            to = 3 * chunk * j
+            target = targets[min(j, 1)]
+            to = 3 * chunk * max(j - 1, 0)
             for r in range(TEAM_SIZE):
                 at = slice(r * per + j * chunk, r * per + (j + 1) * chunk)
                 target[r, :, to : to + chunk] = gate_up_ref[:, 0, at]
                 target[r, :, to + chunk : to + 2 * chunk] = gate_up_ref[:, 1, at]
                 target[r, :, to + 2 * chunk : to + 3 * chunk] = down_ref[:, at]
 
-    out = shape((TEAM_SIZE, owned, 3 * chunk * CHUNKS), BF16)
+    outs = [shape((TEAM_SIZE, owned, 3 * chunk * n), BF16) for n in (1, CHUNKS - 1)]
     args = [w_gate_up, w_down]
-    return run(kernel, (1,), [whole(a) for a in args], whole(out), out, args)
-
-
-def unpack_chunks(back, w_gate_up, gain, chunk):
-    owned = back.shape[1]
+    return run(kernel, (1,), [whole(a) for a in args], [whole(o) for o in outs], outs, args)
+
+
+def unpack_chunks(first, rest, w_gate_up, gain, chunk):
+    owned = first.shape[1]
     per = CHUNKS * chunk
 
-    def kernel(back_ref, w_ref, gain_ref, gate_up_ref, down_ref, out_ref):
+    def kernel(first_ref, rest_ref, w_ref, gain_ref, gate_up_ref, down_ref, out_ref):
         r = pl.program_id(0)
         total = jnp.zeros((owned, 1), F32)
         for j in range(CHUNKS):
-            at, to = 3 * chunk * j, slice(j * chunk, (j + 1) * chunk)
+            back_ref = rest_ref if j else first_ref
+            at, to = 3 * chunk * max(j - 1, 0), slice(j * chunk, (j + 1) * chunk)
             for part in range(2):
                 value = back_ref[0, :, at + part * chunk : at + (part + 1) * chunk].astype(F32)
                 gate_up_ref[:, part, to] = value
@@ -266,10 +272,10 @@
     return run(
         kernel,
         (TEAM_SIZE,),
-        [pl.BlockSpec((1, owned, 3 * per), lambda r: (r, 0, 0)), wide, whole(gain)],
+        [pl.BlockSpec((1,) + b.shape[1:], lambda r: (r, 0, 0)) for b in (first, rest)] + [wide, whole(gain)],
         [wide, pl.BlockSpec((owned, per), lambda r: (0, r)), whole(gain)],
         outs,
-        [back, w_gate_up, gain],
+        [first, rest, w_gate_up, gain],
     )
 
 
@@ -340,10 +346,7 @@
             normed_ref[...] = (x * inverse_rms(x) * g_attn_ref[...]).astype(BF16)
 
         either(pl.program_id(0), steps, [(x0, x1)], body)
-        per = width // count
-        total = dot(normed_ref[:, :per], w_refs[0][...])
-        for b in range(1, count):
-            total = total + dot(normed_ref[:, b * per : (b + 1) * per], w_refs[b][...])
+        total = dot(normed_ref[...], joined([w[...] for w in w_refs]))
         raw_ref[...] = total[:, : q_width + HEAD_SIZE]
         cos, sin = cos_ref[...], sin_ref[...]
         for at in range(0, q_width + HEAD_SIZE, HEAD_SIZE):
@@ -505,11 +508,12 @@
     return run(kernel, (steps,), in_specs, [row(outs[0].shape[1]), whole(outs[1])], outs, args)
 
 
-def back_rows(which, pairs, received=None):
+def back_rows(which, pairs, received=None, place=None):
     tokens = pairs[0][0].shape[0]
     half = tokens // 2
     steps = BACK_STEPS
     rows = half // steps
+    block = half // 4
     count = len(pairs[0][1])
     per = pairs[0][1][0].shape[0]
     width = count * per
@@ -517,17 +521,23 @@
     blocks = [b for p in pairs for b in p[1]]
 
     def kernel(*refs):
+        if place is not None:
+            place_ref, refs = refs[0], refs[1:]
         left_refs, w_refs = refs[: len(left)], refs[len(left) : len(left) + len(blocks)]
         out_ref = refs[-1]
         for b in range(count):
             at = slice(b * per, (b + 1) * per)
-            total = None
-            for i, l in enumerate(left_refs):
-                term = dot_nt(l[...], w_refs[i * count + b][...])
-                total = term if total is None else total + term
+            lefts = joined([l[...] for l in left_refs], 1)
+            total = dot_nt(lefts, joined([w_refs[i * count + b][...] for i in range(len(left))], 1))
             if received is not None:
                 total = total + refs[-2][:, at].astype(F32)
-            out_ref[:, at] = total.astype(BF16)
+            total = total.astype(BF16)
+            if place is None:
+                out_ref[:, at] = total
+                continue
+            for i in range(rows // block):
+                to = (pl.program_id(0) * (rows // block) + i) ^ place_ref[0]
+                out_ref[to, :, at] = total[i * block : (i + 1) * block]
 
     out = shape((half, width), BF16)
     out_spec = pl.BlockSpec((rows, width), lambda i: (i, 0))
@@ -538,6 +548,10 @@
     if received is not None:
         in_specs.append(out_spec)
         args = args + [received]
+    if place is not None:
+        in_specs, args = [scalars()] + in_specs, [place] + args
+        out = shape((4, block, width), BF16)
+        out_spec = whole(out)
     flops = sum(2 * half * width * p[3] for p in pairs)
     return run(kernel, (steps,), in_specs, out_spec, out, args, flops=flops)
 
@@ -553,13 +567,8 @@
         w_refs, (hidden_ref, d_ref) = refs[:count], refs[count:]
 
         def body(nm_ref, dy_ref):
-            both = d_hidden = None
-            for b in range(count):
-                at = slice(b * per, (b + 1) * per)
-                one = dot(nm_ref[:, at], w_refs[b][:, : 2 * chunk])
-                two = dot(dy_ref[:, at], w_refs[b][:, 2 * chunk : 3 * chunk])
-                both = one if both is None else both + one
-                d_hidden = two if d_hidden is None else d_hidden + two
+            both = dot(nm_ref[...], joined([w[:, : 2 * chunk] for w in w_refs]))
+            d_hidden = dot(dy_ref[...], joined([w[:, 2 * chunk : 3 * chunk] for w in w_refs]))
             gate, upward = both[:, :chunk], both[:, chunk:]
             sigma = 1.0 / (1.0 + jnp.exp(-gate))
             silu = gate * sigma
@@ -597,12 +606,7 @@
         in_refs = [refs.pop(0) for _ in (received or ())]
         column = 0
         for sources, d_ref, cut in zip(l_refs, d_refs, cuts):
-            total, at = None, 0
-            for source in sources:
-                count = source.shape[0]
-                term = dot_tn(source[...], d_ref[at : at + count, :])
-                total = term if total is None else total + term
-                at += count
+            total = dot_tn(joined([source[...] for source in sources]), d_ref[...])
             span = slice(column, column + cut)
             column += cut
             for r in in_refs:
@@ -635,6 +639,23 @@
     )
 
 
+def scalars():
+    return pl.BlockSpec(memory_space=pltpu.SMEM)
+
+
+def assemble(own, x, z, both, place):
+    rows, width = own.shape
+
+    def kernel(place_ref, *refs):
+        for i, ref in enumerate(refs[:4]):
+            refs[4][place_ref[0] ^ i] = ref[...]
+
+    out = shape((4, rows, width), BF16)
+    args = [place, own, x, z, both]
+    result = run(kernel, (1,), [scalars()] + [whole(a) for a in args[1:]], whole(out), out, args)
+    return result.reshape(4 * rows, width)
+
+
 def one_copy(value, width, column=0):
     if len(value.shape) == 2:
         return whole(value)
@@ -662,12 +683,12 @@
     return run(kernel, (1,), [whole(parts), one_copy(x, width), whole(gain)], [whole(o) for o in outs], outs, args)
 
 
-def norm_back_step(parts, base, passed, passed_column, gain, copies):
+def norm_back_step(parts, base, passed, gain, copies):
     rows, width = base.shape[-2], gain.shape[1]
 
     def kernel(parts_ref, base_ref, passed_ref, gain_ref, *out_refs):
         total = parts_ref[0].astype(F32)
-        for i in range(1, 4):
+        for i in range(1, parts.shape[0]):
             total = total + parts_ref[i].astype(F32)
         value = rows_of(base_ref).astype(F32)
         inverse = inverse_rms(value)
@@ -686,18 +707,19 @@
     if copies == 1:
         outs = [shape((rows, width), BF16)]
     args = [parts, base, passed, gain]
-    return run(kernel, (1,), [whole(parts), one_copy(base, width), one_copy(passed, width, passed_column), whole(gain)], [whole(o) for o in outs], outs, args)
-
-
-def plain_sum(parts, base):
-    def kernel(parts_ref, base_ref, out_ref):
-        total = base_ref[...]
-        for i in range(4):
-            total = total + parts_ref[i].astype(F32)
-        out_ref[...] = total.astype(BF16)
+    return run(kernel, (1,), [whole(parts), one_copy(base, width), one_copy(passed, width), whole(gain)], [whole(o) for o in outs], outs, args)
+
+
+def plain_sum(base, *parts):
+    def kernel(*refs):
+        total = refs[0][...].astype(F32)
+        for ref in refs[1:-1]:
+            total = total + ref[...].astype(F32)
+        refs[-1][...] = total.astype(BF16)
 
     out = shape(base.shape, BF16)
-    return run(kernel, (1,), [whole(parts), whole(base)], whole(out), out, [parts, base])
+    args = [base, *parts]
+    return run(kernel, (1,), [whole(a) for a in args], whole(out), out, args)
 
 
 def attended_gradient(d_branch, blocks, column, n):
@@ -710,10 +732,7 @@
         w_refs, out_ref = refs[:count], refs[count]
 
         def body(d_ref):
-            total = dot(d_ref[:, :per], w_refs[0][...])
-            for b in range(1, count):
-                total = total + dot(d_ref[:, b * per : (b + 1) * per], w_refs[b][...])
-            out_ref[...] = total.astype(BF16)
+            out_ref[...] = dot(d_ref[...], joined([w[...] for w in w_refs])).astype(BF16)
 
         either(pl.program_id(0), steps, [(d0, d1)], body)
 
@@ -763,25 +782,33 @@
     def with_near(block):
         return [block] + layout.near_blocks(block)
 
-    copies = reorder([tokens[0], out_grad[0]], places, False, 4)
-    part_attn = arrived(exchange(pack_attention(w_qkv_rows, w_out_rows)))
-    send_mlp = pack_chunks(w_gate_up_rows, w_down_rows, chunk)
     mine = jnp.concatenate([attn_gain, mlp_gain, q_gain, k_gain, doc_ids.reshape(-1).astype(BF16)])[None]
     table = jnp.zeros((devices, mine.shape[1]), BF16)
     table = lax.dynamic_update_slice(table, mine, (device_index(sizes), 0))
-    table = all_sum(table, sizes, ("c", "xl", "zl"))
-    part_attn, copies, send_mlp, table = hold(part_attn, copies, send_mlp, table)
+    table = all_sum(table, sizes, ("c",))
+    part_attn = arrived(exchange(pack_attention(w_qkv_rows, w_out_rows)))
+    send_first, send_rest = pack_chunks(w_gate_up_rows, w_down_rows, chunk)
+    x_own, dy_own = reorder([tokens[0], out_grad[0]], places, False)
+    corner = (lax.axis_index("zl") * 2 + lax.axis_index("xl")).astype(jnp.int32).reshape(1)
+    table, send_first, x_own = hold(table, send_first, x_own)
+    table = all_sum(table, sizes, ("xl", "zl"))
+    part_attn, x_own, send_first, table, dy_own = hold(part_attn, x_own, send_first, table, dy_own)
 
     attn_near, attn_far = with_near(part_attn), layout.far_blocks(part_attn)
-    rest = arrived(exchange(send_mlp))
+    parts = [arrived(exchange(send_first))]
+    x_parts = [x_own, other_x(x_own), other_z(x_own)]
     table = all_sum(table, sizes, ("y", "xh", "zh"))
-    attn_near, attn_far, rest, table, copies = hold(attn_near, attn_far, rest, table, copies)
-    parts = [rest[:, j * 3 * chunk : (j + 1) * 3 * chunk] for j in range(CHUNKS)]
+    attn_near, attn_far, parts, table, x_parts, dy_own, send_rest = hold(
+        attn_near, attn_far, parts, table, x_parts, dy_own, send_rest
+    )
 
     near, far = {}, {}
+    x_parts.append(other_x(x_parts[2]))
     w_attn = gathered(attn_near, [with_near(b) for b in attn_far])
     near[0], far[0] = with_near(parts[0]), layout.far_blocks(parts[0])
-    token_half = spread(copies)
+    rest = arrived(exchange(send_rest))
+    parts += [rest[:, j * 3 * chunk : (j + 1) * 3 * chunk] for j in range(CHUNKS - 1)]
+    dy_parts = [dy_own, other_x(dy_own), other_z(dy_own)]
 
     table = table.astype(F32)
     natural = jnp.stack([table[:, :owned].reshape(width), table[:, owned : 2 * owned].reshape(width)])
@@ -817,14 +844,8 @@
     cosine, sine = jnp.cos(angle), jnp.sin(angle)
     cosine = jnp.concatenate([cosine, cosine], axis=1)
     sine = jnp.concatenate([-sine, sine], axis=1)
-    token_half, w_attn, cosine, sine, g_attn, g_mlp, k_info, q_info, near[0], far[0], parts = hold(
-        token_half, w_attn, cosine, sine, g_attn, g_mlp, k_info, q_info, near[0], far[0], parts
-    )
-
-    near[1], far[1] = with_near(parts[1]), layout.far_blocks(parts[1])
-    weights = [gathered(near[0], [with_near(b) for b in far[0]])]
-    team = [token_half, other_core(token_half)]
-    x_side, dy = (team, 0), (team, 1)
+    x_half = assemble(*x_parts, corner)
+    x_side = ([x_half, other_core(x_half)], 0)
     normed_in, raw, qkv = project(x_side, w_attn, g_attn, g_q, g_k, cosine, sine, q_width)
     qkv4 = qkv.reshape(2, 2, 2 * rows, -1)
     if sizes["xh"] == 1:
@@ -835,15 +856,26 @@
     attended = attended.reshape(-1, q_width)
     out_column = (q_width + 2 * HEAD_SIZE) // q_width
     out_pair = [(attended, w_attn, out_column, q_width)]
-    received = other_core(back_rows(1, out_pair))
-    branch = among_four(back_rows(0, out_pair, received).reshape(4, rows, width))
-    middle, nm_copies = middle_step(branch, copies, g_mlp)
-    nm_copies, weights[0], near[1], far[1], parts[2] = hold(nm_copies, weights[0], near[1], far[1], parts[2])
+    branch_other = back_rows(1, out_pair)
+    branch_other, dy_parts, near[0], far[0], parts = hold(branch_other, dy_parts, near[0], far[0], parts)
+
+    near[1], far[1] = with_near(parts[1]), layout.far_blocks(parts[1])
+    weights = [gathered(near[0], [with_near(b) for b in far[0]])]
+    dy_parts.append(other_x(dy_parts[2]))
+    branch = back_rows(0, out_pair, other_core(branch_other))
+    branch = among_four(branch.reshape(4, rows, width))
+    middle, nm_copies = middle_step(branch, x_own, g_mlp)
+    nm_copies, weights[0], near[1], far[1], parts[2], dy_parts = hold(
+        nm_copies, weights[0], near[1], far[1], parts[2], dy_parts
+    )
 
     near[2], far[2] = with_near(parts[2]), layout.far_blocks(parts[2])
     weights.append(gathered(near[1], [with_near(b) for b in far[1]]))
     nm_half = spread(nm_copies)
-    nm_half, weights[1], near[2], far[2] = hold(nm_half, weights[1], near[2], far[2])
+    dy_half = assemble(*dy_parts, corner)
+    dy_halves = [dy_half, other_core(dy_half)]
+    nm_half, dy_halves, weights[1], near[2], far[2] = hold(nm_half, dy_halves, weights[1], near[2], far[2])
+    dy = (dy_halves, 0)
 
     def near_send(*pairs):
         return [weight_terms(layout, width, n, pairs) for n in range(1, layout.near)]
@@ -883,26 +915,32 @@
     mid_pairs = [(d_gate_up[j], weights[j], 0, 2 * chunk) for j in range(CHUNKS)]
     out_pairs = [(hidden[j], weights[j], 2, chunk) for j in range(CHUNKS)]
     received = other_core(back_rows(1, mid_pairs))
-    terms = among_four(back_rows(0, mid_pairs, received).reshape(4, rows, width))
+    terms = back_rows(0, mid_pairs, received)
+    terms, hidden, d_gate_up = hold(terms, hidden, d_gate_up)
+    mlp = [[(nm, d), (dy, h)] for h, d in zip(hidden, d_gate_up)]
+    out_pairs = [(hidden[j], weights[j], 2, chunk) for j in range(CHUNKS)]
+    terms = among_four(terms.reshape(4, rows, width))
     going[1] = near_send(*mlp[1])
-    d_middle, d_copies = norm_back_step(terms, middle, copies, 1, g_mlp, 4)
-    d_copies, going[1], arriving[0] = hold(d_copies, going[1], arriving[0])
-
     sums[0] = own_terms(arriving[0], *mlp[0])
+    d_middle, d_copies = norm_back_step(terms, middle, dy_own, g_mlp, 4)
+    d_copies, going[1], sums[0], hidden, d_gate_up = hold(d_copies, going[1], sums[0], hidden, d_gate_up)
+    mlp = [[(nm, d), (dy, h)] for h, d in zip(hidden, d_gate_up)]
+    out_pairs = [(hidden[j], weights[j], 2, chunk) for j in range(CHUNKS)]
+
     arrived_far[0] = to_far(sums[0])
     arriving[1] = to_near(going[1])
     d_half = spread(d_copies)
     going[2] = near_send(*mlp[2])
     received = other_core(back_rows(1, out_pairs))
-    out_total = back_rows(0, out_pairs, received)
-    d_half, arriving[1], arrived_far[0], going[2], out_total = hold(
-        d_half, arriving[1], arrived_far[0], going[2], out_total
-    )
-
+    out_total = back_rows(0, out_pairs, received, corner)
     sums[1] = own_terms(arriving[1], *mlp[1])
+    d_half, sums[1], arrived_far[0], going[2], out_total = hold(
+        d_half, sums[1], arrived_far[0], going[2], out_total
+    )
+
     arrived_far[1] = to_far(sums[1])
     arriving[2] = to_near(going[2])
-    out_total = among_four(out_total.reshape(4, rows, width))
+    out_both = other_x(out_total[3])
     d_branch = ([d_half, other_core(d_half)], 0)
     d_attended = attended_gradient(d_branch, w_attn, out_column, q_width)
     d_attended = d_attended.reshape(2, 2, 2 * rows, q_width)
@@ -923,34 +961,40 @@
     )
     in_pair = [(d_projected, w_attn, 0, q_width + 2 * HEAD_SIZE)]
     received = other_core(back_rows(1, in_pair))
-    terms = back_rows(0, in_pair, received)
+    terms = back_rows(0, in_pair, received, corner)
     attention = [(([normed_in], 0), d_projected), (d_branch, attended)]
     going[3] = near_send(*attention)
-    terms, arriving[2], arrived_far[1], out_total, going[3] = hold(
-        terms, arriving[2], arrived_far[1], out_total, going[3]
+    terms, arriving[2] = hold(terms, arriving[2])
+    sums[2] = own_terms(arriving[2], *mlp[2])
+    out_z = plain_sum(out_total[2], out_both)
+    terms, sums[2], arrived_far[1], out_total, out_z, going[3] = hold(
+        terms, sums[2], arrived_far[1], out_total, out_z, going[3]
     )
 
     arriving[3] = to_near(going[3])
-    sums[2] = own_terms(arriving[2], *mlp[2])
     arrived_far[2] = to_far(sums[2])
-    terms = among_four(terms.reshape(4, rows, width))
-    output = plain_sum(out_total, middle)
+    in_both = other_x(terms[3])
+    output = plain_sum(middle, out_total[0], other_x(out_total[1]), other_z(out_z))
+    sums[3] = own_terms(arriving[3], *attention)
     head_gains = all_sum(head_gains, sizes, ("c", "xl"))
-    terms, arriving[3], arrived_far[2], head_gains = hold(terms, arriving[3], arrived_far[2], head_gains)
-
-    sums[3] = own_terms(arriving[3], *attention)
+    in_z = plain_sum(terms[2], in_both)
+    back_first = exchange(far_total(sums[0][0], arrived_far[0]))
+    terms, in_z, sums[3], arrived_far[2], head_gains, output, back_first = hold(
+        terms, in_z, sums[3], arrived_far[2], head_gains, output, back_first
+    )
+
     arrived_far[3] = to_far(sums[3])
-    back = jnp.concatenate([far_total(sums[j][0], arrived_far[j]) for j in range(CHUNKS)], axis=2)
+    back = jnp.concatenate([far_total(sums[j][0], arrived_far[j]) for j in range(1, CHUNKS)], axis=2)
     back = exchange(back)
-    (token_grad,) = norm_back_step(terms, copies, d_middle, 0, g_attn, 1)
+    terms = jnp.stack([terms[0], other_x(terms[1]), other_z(in_z)])
+    (token_grad,) = norm_back_step(terms, x_own, d_middle, g_attn, 1)
     token_grad, output = reorder([token_grad, output], places, True)
-    head_gains = all_sum(head_gains, sizes, ("zl", "y"))
-    back, arrived_far[3], head_gains = hold(back, arrived_far[3], head_gains)
+    head_gains = all_sum(head_gains, sizes, ("zl", "y", "xh", "zh"))
+    back, arrived_far[3], head_gains, token_grad = hold(back, arrived_far[3], head_gains, token_grad)
 
     last = exchange(far_total(sums[3][0], arrived_far[3]))
-    head_gains = all_sum(head_gains, sizes, ("xh", "zh"))
     grad_gate_up, grad_down, grad_mlp_gain = unpack_chunks(
-        back, w_gate_up_rows, mlp_gain.astype(F32).reshape(owned, 1), chunk
+        back_first, back, w_gate_up_rows, mlp_gain.astype(F32).reshape(owned, 1), chunk
     )
     grad_qkv, grad_out, grad_attn_gain = unpack_attention(
         last, w_qkv_rows, attn_gain.astype(F32).reshape(owned, 1)

time: 624 us -> 583 us (0.934)
  waiting for transfers between devices: 327 us -> 256 us
  local copies, waits for them, and re-layouts: 38.9 us -> 68 us
  Pallas kernels: 152 us -> 134 us
  starting transfers between devices: 82.6 us -> 99.5 us
    ppermute x4, waiting for transfers between devices: 55.1 us -> 6.24 us  [to_far(): lax.ppermute(value, 'zh', [(i, (i + k) % self.zh) for i in range(self.zh)])]
    ppermute x0 -> x12, waiting for transfers between devices: none -> 43.7 us  [the longest x8 35.2 us: other_x(): return lax.ppermute(value, 'xl', SWAP)]
    all_to_all x7 -> x4, waiting for transfers between devices: 75 us -> 37.1 us  [among_four(): return lax.all_to_all(value, ('zl', 'xl'), 0, 0, tiled=True)]
    ppermute x4, waiting for transfers between devices: 0.01 us -> 31.7 us  [to_near(): return lax.ppermute(value, ('y', 'xh'), self.shifted(n))]
    unnamed x194 -> x285, local copies, waits for them, and re-layouts: 32.8 us -> 57.7 us
    ppermute x4, waiting for transfers between devices: 25.3 us -> 1.32 us  [far_blocks(): lax.ppermute(block, 'zh', [((i + k) % self.zh, i) for i in range(self.zh)])]
    ppermute x8, waiting for transfers between devices: 61.5 us -> 41.3 us  [near_blocks(): lax.ppermute(block, ('y', 'xh'), [(b, a) for a, b in self.shifted(n)])]
    ppermute x0 -> x12, starting transfers between devices: none -> 20 us  [the longest x8 13.5 us: other_x(): return lax.ppermute(value, 'xl', SWAP)]
  transfers between devices with their start and end apart: 48 -> 60, of which waited for: 25 -> 27; matrix products, arithmetic and copies ran while one was open for 2% -> 3% of each run, Pallas kernels for 19% -> 19%
where the time goes in v3:
time: 583 us; the launch traced here: 575 us
  waiting for transfers between devices  256 us (44%)
  Pallas kernels  134 us (23%)
  starting transfers between devices  99.5 us (17%)
  local copies, waits for them, and re-layouts  68 us (12%)
  other arithmetic  14.8 us (3%)
    pallas_call x36, Pallas kernels, run(): pl.pallas_call(kernel, grid=grid, in_specs=in_specs, out_specs=out_specs,...  131 us
    ppermute x10, waiting for transfers between devices, all_sum(): lax.ppermute(value, axis, [((i + k) % sizes[axis], i) for i in range(size...  78.5 us
    unnamed x285, local copies, waits for them, and re-layouts  57.7 us
    ppermute x8, waiting for transfers between devices, near_blocks(): lax.ppermute(block, ('y', 'xh'), [(b, a) for a, b in self.shifted(n)])  41.3 us
    all_to_all x4, waiting for transfers between devices, among_four(): return lax.all_to_all(value, ('zl', 'xl'), 0, 0, tiled=True)  37.1 us
    ppermute x8, waiting for transfers between devices, other_x(): return lax.ppermute(value, 'xl', SWAP)  35.2 us
    ppermute x4, waiting for transfers between devices, to_near(): return lax.ppermute(value, ('y', 'xh'), self.shifted(n))  31.7 us
    all_to_all x6, starting transfers between devices, exchange(): return lax.all_to_all(value, TEAM, 0, 0, tiled=True)  27.1 us
  transfers between devices with their start and end apart: 60, of which 27 were waited for; matrix products, arithmetic and copies ran while one was open for 3% of the time, Pallas kernels for 19%

profile of v3, /device:TPU:0, one launch (start us, length us, event | category | flops | bytes accessed | tf_op | source)
XLA Modules:
  0.0 575.2 jit_solution(4452797371118106868)
XLA Ops:
  3.8 5.2 all-to-all-start
  25.7 4.2 all-to-all-start.1
  38.2 12.2 %collective-permute-done.5 = bf16[32,264]{1,0:T(8,128)(2,1)S(1)} collective-permute-done((bf16[32,264]{1,0:T(8,128)(2,1)S(1)}, bf16[32,264]{1,0:T(8,128)(2,1)S(1)}, u32[]{:S(2)}, u32[]{:S(2)}) %collective-permute-start.5) | collective-permute-done | bytes 16928 | tf_op jit(solution)/shard_map/ppermute | solution.py:103
  53.0 16.5 %collective-permute-done.6 = bf16[32,264]{1,0:T(8,128)(2,1)S(1)} collective-permute-done((bf16[32,264]{1,0:T(8,128)(2,1)S(1)}, bf16[32,264]{1,0:T(8,128)(2,1)S(1)}, u32[]{:S(2)}, u32[]{:S(2)}) %collective-permute-start.6) | collective-permute-done | bytes 16928 | tf_op jit(solution)/shard_map/ppermute | solution.py:103
  77.4 7.1 %collective-permute-done.9.refs_3_ = bf16[128,2048]{1,0:T(8,128)(2,1)S(1)} collective-permute-done((bf16[128,2048]{1,0:T(8,128)(2,1)S(1)}, bf16[128,2048]{1,0:T(8,128)(2,1)S(1)}, u32[]{:S(2)}, u32[]{:S(2)}) %collective-permute-start.9) | collective-permute-done | bytes 524320 | tf_op jit(solution)/shard_map/ppermute | solution.py:88
  91.5 5.6 all-to-all-start.2
  102.2 7.3 %collective-permute-done.11.refs_3_.refs_4_.refs_5_ = bf16[512,768]{1,0:T(8,128)(2,1)} collective-permute-done((bf16[512,768]{1,0:T(8,128)(2,1)}, bf16[512,768]{1,0:T(8,128)(2,1)}, u32[]{:S(2)}, u32[]{:S(2)}) %collective-permute-start.11) | collective-permute-done | bytes 786464 | tf_op jit(solution)/shard_map/ppermute | solution.py:65
  112.7 7.0 %shard_map.190 = (bf16[1024,2048]{1,0:T(8,128)(2,1)S(1)}, f32[1024,384]{1,0:T(8,128)S(1)}, bf16[1024,512]{1,0:T(8,128)(2,1)S(1)}) custom-call(bf16[512,2048]{1,0:T(8,128)(2,1)S(1)} %bitcast.117, bf16[512,2048]{1,0:T(8,128)(2,1)} %collective-permute-done.10.x1, bf16[512,768]{1,0:T(8,128)(2,1)S(1)} %bitcast.122, ...), custom_call_target="tpu_custom_call" | custom-call | flops 214748364800 | bytes 1521356800 | tf_op jit(solution)/shard_map/pallas_call | solution.py:138
  131.0 8.5 %collective-permute-done.13.refs_2_ = bf16[128,2048]{1,0:T(8,128)(2,1)} collective-permute-done((bf16[128,2048]{1,0:T(8,128)(2,1)}, bf16[128,2048]{1,0:T(8,128)(2,1)}, u32[]{:S(2)}, u32[]{:S(2)}) %collective-permute-start.13) | collective-permute-done | bytes 524320 | tf_op jit(solution)/shard_map/ppermute | solution.py:92
  156.0 37.1 %all-to-all-done.3.parts_ref = bf16[4,128,2048]{2,1,0:T(8,128)(2,1)S(1)} async-done(((bf16[4,128,2048]{2,1,0:T(8,128)(2,1)}), bf16[4,128,2048]{2,1,0:T(8,128)(2,1)S(1)}, u32[]{:S(2)}, u32[]{:S(2)}) %all-to-all-start.3) | async-done | bytes 2097184 | tf_op jit(solution)/shard_map/all_to_all | solution.py:76
  205.6 18.4 %collective-permute-done.22.refs_3_.refs_10_.refs_11_ = bf16[512,768]{1,0:T(8,128)(2,1)S(1)} collective-permute-done((bf16[512,768]{1,0:T(8,128)(2,1)}, bf16[512,768]{1,0:T(8,128)(2,1)S(1)}, u32[]{:S(2)}, u32[]{:S(2)}) %collective-permute-start.22) | collective-permute-done | bytes 786464 | tf_op jit(solution)/shard_map/ppermute | solution.py:65
  224.9 15.6 %collective-permute-done.23.refs_2_.refs_13_.refs_14_ = bf16[512,768]{1,0:T(8,128)(2,1)S(1)} collective-permute-done((bf16[512,768]{1,0:T(8,128)(2,1)S(1)}, bf16[512,768]{1,0:T(8,128)(2,1)S(1)}, u32[]{:S(2)}, u32[]{:S(2)}) %collective-permute-start.23) | collective-permute-done | bytes 786464 | tf_op jit(solution)/shard_map/ppermute | solution.py:65
  253.4 6.2 %shard_map.198 = (bf16[1024,256]{1,0:T(8,128)(2,1)S(1)}, bf16[1024,512]{1,0:T(8,128)(2,1)S(1)}) custom-call(bf16[512,2048]{1,0:T(8,128)(2,1)S(1)} %bitcast.97, bf16[512,2048]{1,0:T(8,128)(2,1)S(1)} %collective-permute-done.25.nm1.refs_1_, bf16[512,2048]{1,0:T(8,128)(2,1)S(1)} %bitcast.107, bf16[512,2048]{1,0:T(8,128)(2,1)S(1)} %copy-done.68, ...), custom_call_target="tpu_custom_call" | custom-call | flops 322122547200 | bytes 1310720000 | tf_op jit(solution)/shard_map/pallas_call | solution.py:138
  259.6 6.5 %shard_map.196 = (bf16[1024,256]{1,0:T(8,128)(2,1)S(1)}, bf16[1024,512]{1,0:T(8,128)(2,1)S(1)}) custom-call(bf16[512,2048]{1,0:T(8,128)(2,1)S(1)} %bitcast.98, bf16[512,2048]{1,0:T(8,128)(2,1)S(1)} %collective-permute-done.25.nm1.refs_1_, bf16[512,2048]{1,0:T(8,128)(2,1)S(1)} %bitcast.108, bf16[512,2048]{1,0:T(8,128)(2,1)S(1)} %copy-done.68, ...), custom_call_target="tpu_custom_call" | custom-call | flops 322122547200 | bytes 1310720000 | tf_op jit(solution)/shard_map/pallas_call | solution.py:138
  269.5 5.3 shard_map.199
  274.8 6.2 %shard_map.200 = bf16[512,2048]{1,0:T(8,128)(2,1)S(1)} custom-call(bf16[1024,512]{1,0:T(8,128)(2,1)S(1)} %get-tuple-element.224.refs_4_.refs_0_, bf16[1024,512]{1,0:T(8,128)(2,1)S(1)} %get-tuple-element.232.refs_1_.refs_4_, bf16[1024,512]{1,0:T(8,128)(2,1)S(1)} %get-tuple-element.238.refs_2_.refs_4_, bf16[512,768]{1,0:T(8,128)(2,1)} %bitcast.13.refs_0_.refs_3_.refs_4_, ...), custom_call_target="tpu_custom_call" | custom-call | flops 322122547200 | bytes 1468006400 | tf_op jit(solution)/shard_map/pallas_call | solution.py:138
  286.5 5.7 shard_map.201
  293.6 4.4 all-to-all-start.5
  308.5 9.8 %collective-permute-done.28.refs_6_ = bf16[1024,768]{1,0:T(8,128)(2,1)} collective-permute-done((bf16[1024,768]{1,0:T(8,128)(2,1)}, bf16[1024,768]{1,0:T(8,128)(2,1)}, u32[]{:S(2)}, u32[]{:S(2)}) %collective-permute-start.28) | collective-permute-done | bytes 1572896 | tf_op jit(solution)/shard_map/ppermute | solution.py:69
  319.9 5.8 %shard_map.204 = (bf16[512,768]{1,0:T(8,128)(2,1)S(1)}, bf16[512,768]{1,0:T(8,128)(2,1)}) custom-call(bf16[512,2048]{1,0:T(8,128)(2,1)S(1)} %bitcast.102, bf16[512,2048]{1,0:T(8,128)(2,1)S(1)} %copy-done.73, bf16[512,2048]{1,0:T(8,128)(2,1)S(1)} %bitcast.112, bf16[512,2048]{1,0:T(8,128)(2,1)S(1)} %copy-done.69, bf16[1024,512]{1,0:T(8,128)(2,1)S(1)} %copy-done.119, ...), custom_call_target="tpu_custom_call" | custom-call | flops 161061273600 | bytes 1310720000 | tf_op jit(solution)/shard_map/pallas_call | solution.py:138
  332.8 4.6 shard_map.207
  338.1 4.6 all-to-all-start.6
  353.1 21.4 %collective-permute-done.29.refs_6_ = bf16[1024,768]{1,0:T(8,128)(2,1)} collective-permute-done((bf16[1024,768]{1,0:T(8,128)(2,1)}, bf16[1024,768]{1,0:T(8,128)(2,1)}, u32[]{:S(2)}, u32[]{:S(2)}) %collective-permute-start.29) | collective-permute-done | bytes 1572896 | tf_op jit(solution)/shard_map/ppermute | solution.py:69
  374.5 5.9 %shard_map.205 = (bf16[512,768]{1,0:T(8,128)(2,1)S(1)}, bf16[512,768]{1,0:T(8,128)(2,1)}) custom-call(bf16[512,2048]{1,0:T(8,128)(2,1)S(1)} %bitcast.104, bf16[512,2048]{1,0:T(8,128)(2,1)S(1)} %copy-done.74, bf16[512,2048]{1,0:T(8,128)(2,1)S(1)} %bitcast.114, bf16[512,2048]{1,0:T(8,128)(2,1)S(1)} %copy-done.70, bf16[1024,512]{1,0:T(8,128)(2,1)S(1)} %copy-done.116, ...), custom_call_target="tpu_custom_call" | custom-call | flops 161061273600 | bytes 1310720000 | tf_op jit(solution)/shard_map/pallas_call | solution.py:138
  390.7 12.0 %collective-permute-done.36.refs_1_ = bf16[128,2048]{1,0:T(8,128)(2,1)S(1)} collective-permute-done((bf16[128,2048]{1,0:T(8,128)(2,1)S(1)}, bf16[128,2048]{1,0:T(8,128)(2,1)S(1)}, u32[]{:S(2)}, u32[]{:S(2)}) %collective-permute-start.36) | collective-permute-done | bytes 524320 | tf_op jit(solution)/shard_map/ppermute | solution.py:88
  407.8 5.5 shard_map.210
  428.3 5.3 shard_map.214
  452.4 16.0 %collective-permute-done.37.refs_1_ = bf16[128,2048]{1,0:T(8,128)(2,1)S(1)} collective-permute-done((bf16[128,2048]{1,0:T(8,128)(2,1)}, bf16[128,2048]{1,0:T(8,128)(2,1)S(1)}, u32[]{:S(2)}, u32[]{:S(2)}) %collective-permute-start.37) | collective-permute-done | bytes 524320 | tf_op jit(solution)/shard_map/ppermute | solution.py:88
  473.0 5.0 shard_map.218
  479.8 6.2 %collective-permute-done.39 = bf16[512,768]{1,0:T(8,128)(2,1)} collective-permute-done((bf16[512,768]{1,0:T(8,128)(2,1)}, bf16[512,768]{1,0:T(8,128)(2,1)}, u32[]{:S(2)}, u32[]{:S(2)}) %collective-permute-start.39) | collective-permute-done | bytes 786464 | tf_op jit(solution)/shard_map/ppermute | solution.py:72
  500.1 40.4 %collective-permute-done.47 = f32[8,128]{1,0:T(8,128)S(1)} collective-permute-done((f32[8,128]{1,0:T(8,128)S(1)}, f32[8,128]{1,0:T(8,128)S(1)}, u32[]{:S(2)}, u32[]{:S(2)}) %collective-permute-start.47) | collective-permute-done | bytes 4128 | tf_op jit(solution)/shard_map/ppermute | solution.py:103
  559.4 7.3 %shard_map.223 = (f32[64,2,6144]{2,1,0:T(2,128)}, f32[64,6144]{1,0:T(8,128)}, f32[64,1]{1,0:T(8,128)S(1)}) custom-call(bf16[8,64,768]{2,1,0:T(8,128)(2,1)} %all-to-all-done.7.first_ref, bf16[8,64,1536]{2,1,0:T(8,128)(2,1)S(1)} %all-to-all-done.8.rest_ref, bf16[64,2,6144]{2,1,0:T(2,128)(2,1)S(1)} %copy-done.1, f32[64,1]{1,0:T(8,128)S(1)} %copy.38.gain_ref), custom_call_target="tpu_custom_call" | custom-call | bytes 865126400 | tf_op jit(solution)/shard_map/pallas_call | solution.py:138
  (482 shorter events, 243.9 us)
Async XLA Ops:
  25.7 45.5 %all-to-all-start.1 = ((bf16[8,64,768]{2,1,0:T(8,128)(2,1)}), bf16[8,64,768]{2,1,0:T(8,128)(2,1)}, u32[]{:S(2)}, u32[]{:S(2)}) async-start(bf16[8,64,768]{2,1,0:T(8,128)(2,1)} %get-tuple-element.156), calls=%async_computation.1 | async-start | bytes 1572864 | tf_op jit(solution)/shard_map/all_to_all | solution.py:96
  30.0 40.3 %collective-permute-start.3 = (bf16[512,768]{1,0:T(8,128)(2,1)S(1)}, bf16[512,768]{1,0:T(8,128)(2,1)S(1)}, u32[]{:S(2)}, u32[]{:S(2)}) collective-permute-start(bf16[512,768]{1,0:T(8,128)(2,1)S(1)} %bitcast.120), channel_id=1, source_target_pairs={{4,0},{0,4},{5,1},{1,5},{6,2},{2,6},{7,3},{3,7},{12,8},{8,12},{13,... | collective-permute-start | bytes 2359304 | tf_op jit(solution)/shard_map/ppermute | solution.py:65
  31.6 39.7 %collective-permute-start.4 = (bf16[512,768]{1,0:T(8,128)(2,1)S(1)}, bf16[512,768]{1,0:T(8,128)(2,1)}, u32[]{:S(2)}, u32[]{:S(2)}) collective-permute-start(bf16[512,768]{1,0:T(8,128)(2,1)S(1)} %bitcast.121), channel_id=1, source_target_pairs={{16,0},{0,16},{17,1},{1,17},{18,2},{2,18},{19,3},{3,19},{20,4},{4,... | collective-permute-start | bytes 2359304 | tf_op jit(solution)/shard_map/ppermute | solution.py:52
  34.3 35.2 %collective-permute-start.7 = (bf16[128,2048]{1,0:T(8,128)(2,1)S(1)}, bf16[128,2048]{1,0:T(8,128)(2,1)S(1)}, u32[]{:S(2)}, u32[]{:S(2)}) collective-permute-start(bf16[128,2048]{1,0:T(8,128)(2,1)S(1)} %get-tuple-element.161.refs_0_.x_ref.base_ref), channel_id=1, source_target_pairs={{0,2},{2,0},{1,3},{3,1},{4,6},{6,4},{5,7},{7,5},{8,10},{10,8},{9,1... | collective-permute-start | bytes 1572872 | tf_op jit(solution)/shard_map/ppermute | solution.py:88
  36.2 34.1 %collective-permute-start.8 = (bf16[128,2048]{1,0:T(8,128)(2,1)S(1)}, bf16[128,2048]{1,0:T(8,128)(2,1)S(1)}, u32[]{:S(2)}, u32[]{:S(2)}) collective-permute-start(bf16[128,2048]{1,0:T(8,128)(2,1)S(1)} %get-tuple-element.161.refs_0_.x_ref.base_ref), channel_id=1, source_target_pairs={{0,8},{8,0},{1,9},{9,1},{2,10},{10,2},{3,11},{11,3},{4,12},{12,4},... | collective-permute-start | bytes 1572872 | tf_op jit(solution)/shard_map/ppermute | solution.py:92
  73.7 65.8 %collective-permute-start.14 = (bf16[512,768]{1,0:T(8,128)(2,1)}, bf16[512,768]{1,0:T(8,128)(2,1)}, u32[]{:S(2)}, u32[]{:S(2)}) collective-permute-start(bf16[512,768]{1,0:T(8,128)(2,1)} %bitcast.13.refs_0_.refs_3_.refs_4_), channel_id=1, source_target_pairs={{4,0},{0,4},{5,1},{1,5},{6,2},{2,6},{7,3},{3,7},{12,8},{8,12},{13,... | collective-permute-start | bytes 2359304 | tf_op jit(solution)/shard_map/ppermute | solution.py:65
  74.8 64.7 %collective-permute-start.15 = (bf16[512,768]{1,0:T(8,128)(2,1)}, bf16[512,768]{1,0:T(8,128)(2,1)}, u32[]{:S(2)}, u32[]{:S(2)}) collective-permute-start(bf16[512,768]{1,0:T(8,128)(2,1)} %bitcast.13.refs_0_.refs_3_.refs_4_), channel_id=1, source_target_pairs={{16,0},{0,16},{17,1},{1,17},{18,2},{2,18},{19,3},{3,19},{20,4},{4,... | collective-permute-start | bytes 2359304 | tf_op jit(solution)/shard_map/ppermute | solution.py:52
  91.5 36.9 %all-to-all-start.2 = ((bf16[8,64,1536]{2,1,0:T(8,128)(2,1)}), bf16[8,64,1536]{2,1,0:T(8,128)(2,1)}, u32[]{:S(2)}, u32[]{:S(2)}) async-start(bf16[8,64,1536]{2,1,0:T(8,128)(2,1)} %copy-done.28), calls=%async_computation.2 | async-start | bytes 3145728 | tf_op jit(solution)/shard_map/all_to_all | solution.py:96
  147.1 46.1 %all-to-all-start.3 = ((bf16[4,128,2048]{2,1,0:T(8,128)(2,1)}), bf16[4,128,2048]{2,1,0:T(8,128)(2,1)S(1)}, u32[]{:S(2)}, u32[]{:S(2)}) async-start(bf16[4,128,2048]{2,1,0:T(8,128)(2,1)} %bitcast.118), calls=%async_computation.3 | async-start | bytes 4194304 | tf_op jit(solution)/shard_map/all_to_all | solution.py:76
  150.9 45.3 %collective-permute-start.17 = (bf16[512,768]{1,0:T(8,128)(2,1)}, bf16[512,768]{1,0:T(8,128)(2,1)}, u32[]{:S(2)}, u32[]{:S(2)}) collective-permute-start(bf16[512,768]{1,0:T(8,128)(2,1)} %collective-permute-done.15.refs_1_.refs_4_.refs_5_), channel_id=1, source_target_pairs={{4,0},{0,4},{5,1},{1,5},{6,2},{2,6},{7,3},{3,7},{12,8},{8,12},{13,... | collective-permute-start | bytes 2359304 | tf_op jit(solution)/shard_map/ppermute | solution.py:65
  151.3 44.9 %collective-permute-start.18 = (bf16[512,768]{1,0:T(8,128)(2,1)S(1)}, bf16[512,768]{1,0:T(8,128)(2,1)}, u32[]{:S(2)}, u32[]{:S(2)}) collective-permute-start(bf16[512,768]{1,0:T(8,128)(2,1)S(1)} %copy-done.41), channel_id=1, source_target_pairs={{4,0},{0,4},{5,1},{1,5},{6,2},{2,6},{7,3},{3,7},{12,8},{8,12},{13,... | collective-permute-start | bytes 2359304 | tf_op jit(solution)/shard_map/ppermute | solution.py:65
  153.0 43.2 %collective-permute-start.19 = (bf16[512,768]{1,0:T(8,128)(2,1)S(1)}, bf16[512,768]{1,0:T(8,128)(2,1)}, u32[]{:S(2)}, u32[]{:S(2)}) collective-permute-start(bf16[512,768]{1,0:T(8,128)(2,1)S(1)} %copy-done.41), channel_id=1, source_target_pairs={{16,0},{0,16},{17,1},{1,17},{18,2},{2,18},{19,3},{3,19},{20,4},{4,... | collective-permute-start | bytes 2359304 | tf_op jit(solution)/shard_map/ppermute | solution.py:52
  154.0 42.2 %collective-permute-start.20 = (bf16[128,2048]{1,0:T(8,128)(2,1)}, bf16[128,2048]{1,0:T(8,128)(2,1)}, u32[]{:S(2)}, u32[]{:S(2)}) collective-permute-start(bf16[128,2048]{1,0:T(8,128)(2,1)} %collective-permute-done.13.refs_2_), channel_id=1, source_target_pairs={{0,2},{2,0},{1,3},{3,1},{4,6},{6,4},{5,7},{7,5},{8,10},{10,8},{9,1... | collective-permute-start | bytes 1572872 | tf_op jit(solution)/shard_map/ppermute | solution.py:88
  196.2 48.7 %all-to-all-start.4 = ((bf16[4,128,2048]{2,1,0:T(8,128)(2,1)}), bf16[4,128,2048]{2,1,0:T(8,128)(2,1)S(1)}, u32[]{:S(2)}, u32[]{:S(2)}) async-start(bf16[4,128,2048]{2,1,0:T(8,128)(2,1)} %copy-done.19), calls=%async_computation.4 | async-start | bytes 4194304 | tf_op jit(solution)/shard_map/all_to_all | solution.py:76
  202.0 41.6 %collective-permute-start.21 = (bf16[512,2048]{1,0:T(8,128)(2,1)S(1)}, bf16[512,2048]{1,0:T(8,128)(2,1)S(1)}, u32[]{:S(2)}, u32[]{:S(2)}) collective-permute-start(bf16[512,2048]{1,0:T(8,128)(2,1)S(1)} %bitcast.106), channel_id=1, source_target_pairs={{0,1},{1,0},{2,3},{3,2},{4,5},{5,4},{6,7},{7,6},{8,9},{9,8},{10,11... | collective-permute-start | bytes 6291464 | tf_op jit(solution)/shard_map/ppermute | solution.py:84
  203.8 36.6 %collective-permute-start.23 = (bf16[512,768]{1,0:T(8,128)(2,1)S(1)}, bf16[512,768]{1,0:T(8,128)(2,1)S(1)}, u32[]{:S(2)}, u32[]{:S(2)}) collective-permute-start(bf16[512,768]{1,0:T(8,128)(2,1)S(1)} %copy-done.37), channel_id=1, source_target_pairs={{4,0},{0,4},{5,1},{1,5},{6,2},{2,6},{7,3},{3,7},{12,8},{8,12},{13,... | collective-permute-start | bytes 2359304 | tf_op jit(solution)/shard_map/ppermute | solution.py:65
  205.5 37.2 %collective-permute-start.24 = (bf16[512,768]{1,0:T(8,128)(2,1)S(1)}, bf16[512,768]{1,0:T(8,128)(2,1)S(1)}, u32[]{:S(2)}, u32[]{:S(2)}) collective-permute-start(bf16[512,768]{1,0:T(8,128)(2,1)S(1)} %copy-done.37), channel_id=1, source_target_pairs={{16,0},{0,16},{17,1},{1,17},{18,2},{2,18},{19,3},{3,19},{20,4},{4,... | collective-permute-start | bytes 2359304 | tf_op jit(solution)/shard_map/ppermute | solution.py:52
  281.3 37.0 %collective-permute-start.28 = (bf16[1024,768]{1,0:T(8,128)(2,1)}, bf16[1024,768]{1,0:T(8,128)(2,1)}, u32[]{:S(2)}, u32[]{:S(2)}) collective-permute-start(bf16[1024,768]{1,0:T(8,128)(2,1)} %shard_map.197), channel_id=1, source_target_pairs={{0,4},{4,0},{1,5},{5,1},{2,6},{6,2},{3,7},{7,3},{8,12},{12,8},{9,1... | collective-permute-start | bytes 4718600 | tf_op jit(solution)/shard_map/ppermute | solution.py:69
  337.3 44.0 %collective-permute-start.31 = (bf16[512,2048]{1,0:T(8,128)(2,1)}, bf16[512,2048]{1,0:T(8,128)(2,1)}, u32[]{:S(2)}, u32[]{:S(2)}) collective-permute-start(bf16[512,2048]{1,0:T(8,128)(2,1)} %shard_map.207), channel_id=1, source_target_pairs={{0,1},{1,0},{2,3},{3,2},{4,5},{5,4},{6,7},{7,6},{8,9},{9,8},{10,11... | collective-permute-start | bytes 6291464 | tf_op jit(solution)/shard_map/ppermute | solution.py:84
  337.3 37.1 %collective-permute-start.29 = (bf16[1024,768]{1,0:T(8,128)(2,1)}, bf16[1024,768]{1,0:T(8,128)(2,1)}, u32[]{:S(2)}, u32[]{:S(2)}) collective-permute-start(bf16[1024,768]{1,0:T(8,128)(2,1)} %shard_map.203), channel_id=1, source_target_pairs={{0,4},{4,0},{1,5},{5,1},{2,6},{6,2},{3,7},{7,3},{8,12},{12,8},{9,1... | collective-permute-start | bytes 4718600 | tf_op jit(solution)/shard_map/ppermute | solution.py:69
  337.8 48.9 %collective-permute-start.30 = (bf16[512,768]{1,0:T(8,128)(2,1)}, bf16[512,768]{1,0:T(8,128)(2,1)}, u32[]{:S(2)}, u32[]{:S(2)}) collective-permute-start(bf16[512,768]{1,0:T(8,128)(2,1)} %get-tuple-element.237), channel_id=1, source_target_pairs={{0,16},{16,0},{1,17},{17,1},{2,18},{18,2},{3,19},{19,3},{4,20},{20... | collective-permute-start | bytes 2359304 | tf_op jit(solution)/shard_map/ppermute | solution.py:72
  338.1 48.6 %all-to-all-start.6 = ((bf16[4,128,2048]{2,1,0:T(8,128)(2,1)}), bf16[4,128,2048]{2,1,0:T(8,128)(2,1)}, u32[]{:S(2)}, u32[]{:S(2)}) async-start(bf16[4,128,2048]{2,1,0:T(8,128)(2,1)} %copy-done.18), calls=%async_computation.6 | async-start | bytes 4194304 | tf_op jit(solution)/shard_map/all_to_all | solution.py:76
  390.3 37.5 %collective-permute-start.34 = (bf16[1024,768]{1,0:T(8,128)(2,1)}, bf16[1024,768]{1,0:T(8,128)(2,1)}, u32[]{:S(2)}, u32[]{:S(2)}) collective-permute-start(bf16[1024,768]{1,0:T(8,128)(2,1)} %shard_map.206), channel_id=1, source_target_pairs={{0,4},{4,0},{1,5},{5,1},{2,6},{6,2},{3,7},{7,3},{8,12},{12,8},{9,1... | collective-permute-start | bytes 4718600 | tf_op jit(solution)/shard_map/ppermute | solution.py:69
  390.7 43.1 %collective-permute-start.35 = (bf16[512,768]{1,0:T(8,128)(2,1)}, bf16[512,768]{1,0:T(8,128)(2,1)}, u32[]{:S(2)}, u32[]{:S(2)}) collective-permute-start(bf16[512,768]{1,0:T(8,128)(2,1)} %get-tuple-element.251), channel_id=1, source_target_pairs={{0,16},{16,0},{1,17},{17,1},{2,18},{18,2},{3,19},{19,3},{4,20},{20... | collective-permute-start | bytes 2359304 | tf_op jit(solution)/shard_map/ppermute | solution.py:72
  433.7 37.0 %collective-permute-start.38 = (bf16[1024,768]{1,0:T(8,128)(2,1)}, bf16[1024,768]{1,0:T(8,128)(2,1)}, u32[]{:S(2)}, u32[]{:S(2)}) collective-permute-start(bf16[1024,768]{1,0:T(8,128)(2,1)} %shard_map.216), channel_id=1, source_target_pairs={{0,4},{4,0},{1,5},{5,1},{2,6},{6,2},{3,7},{7,3},{8,12},{12,8},{9,1... | collective-permute-start | bytes 4718600 | tf_op jit(solution)/shard_map/ppermute | solution.py:69
  443.3 36.5 %all-to-all-start.7 = ((bf16[8,64,768]{2,1,0:T(8,128)(2,1)}), bf16[8,64,768]{2,1,0:T(8,128)(2,1)}, u32[]{:S(2)}, u32[]{:S(2)}) async-start(bf16[8,64,768]{2,1,0:T(8,128)(2,1)} %bitcast.146), calls=%async_computation.7 | async-start | bytes 1572864 | tf_op jit(solution)/shard_map/all_to_all | solution.py:96
  448.1 37.9 %collective-permute-start.39 = (bf16[512,768]{1,0:T(8,128)(2,1)}, bf16[512,768]{1,0:T(8,128)(2,1)}, u32[]{:S(2)}, u32[]{:S(2)}) collective-permute-start(bf16[512,768]{1,0:T(8,128)(2,1)} %copy-done.98), channel_id=1, source_target_pairs={{0,16},{16,0},{1,17},{17,1},{2,18},{18,2},{3,19},{19,3},{4,20},{20... | collective-permute-start | bytes 2359304 | tf_op jit(solution)/shard_map/ppermute | solution.py:72
  488.7 63.7 %all-to-all-start.8 = ((bf16[8,64,1536]{2,1,0:T(8,128)(2,1)}), bf16[8,64,1536]{2,1,0:T(8,128)(2,1)S(1)}, u32[]{:S(2)}, u32[]{:S(2)}) async-start(bf16[8,64,1536]{2,1,0:T(8,128)(2,1)} %pad_maximum_fusion.1), calls=%async_computation.8 | async-start | bytes 3145728 | tf_op jit(solution)/shard_map/all_to_all | solution.py:96
  493.7 54.9 %collective-permute-start.44 = (bf16[128,2048]{1,0:T(8,128)(2,1)S(1)}, bf16[128,2048]{1,0:T(8,128)(2,1)S(1)}, u32[]{:S(2)}, u32[]{:S(2)}) collective-permute-start(bf16[128,2048]{1,0:T(8,128)(2,1)S(1)} %get-tuple-element.289), channel_id=1, source_target_pairs={{0,2},{2,0},{1,3},{3,1},{4,6},{6,4},{5,7},{7,5},{8,10},{10,8},{9,1... | collective-permute-start | bytes 1572872 | tf_op jit(solution)/shard_map/ppermute | solution.py:88
  495.6 52.9 %collective-permute-start.45 = (bf16[128,2048]{1,0:T(8,128)(2,1)S(1)}, bf16[128,2048]{1,0:T(8,128)(2,1)S(1)}, u32[]{:S(2)}, u32[]{:S(2)}) collective-permute-start(bf16[128,2048]{1,0:T(8,128)(2,1)S(1)} %shard_map.217), channel_id=1, source_target_pairs={{0,8},{8,0},{1,9},{9,1},{2,10},{10,2},{3,11},{11,3},{4,12},{12,4},... | collective-permute-start | bytes 1572872 | tf_op jit(solution)/shard_map/ppermute | solution.py:92
  497.1 55.2 %collective-permute-start.46 = (bf16[512,768]{1,0:T(8,128)(2,1)S(1)}, bf16[512,768]{1,0:T(8,128)(2,1)}, u32[]{:S(2)}, u32[]{:S(2)}) collective-permute-start(bf16[512,768]{1,0:T(8,128)(2,1)S(1)} %copy-done.100), channel_id=1, source_target_pairs={{0,16},{16,0},{1,17},{17,1},{2,18},{18,2},{3,19},{19,3},{4,20},{20... | collective-permute-start | bytes 2359304 | tf_op jit(solution)/shard_map/ppermute | solution.py:72
  499.5 40.9 %collective-permute-start.47 = (f32[8,128]{1,0:T(8,128)S(1)}, f32[8,128]{1,0:T(8,128)S(1)}, u32[]{:S(2)}, u32[]{:S(2)}) collective-permute-start(f32[8,128]{1,0:T(8,128)S(1)} %copy-done.133), channel_id=1, source_target_pairs={{8,0},{0,8},{9,1},{1,9},{10,2},{2,10},{11,3},{3,11},{12,4},{4,12},... | collective-permute-start | bytes 12296 | tf_op jit(solution)/shard_map/ppermute | solution.py:103
  (169 other events, 1594.3 us)

commit v4 on v3

--- a/solution.py
+++ b/solution.py
@@ -130,6 +130,12 @@
 
 def shape(dims, dtype):
     return jax.ShapeDtypeStruct(tuple(dims), dtype)
+
+
+def in_hbm(args):
+    return [
+        pltpu.with_memory_space_constraint(a, pltpu.HBM) if math.prod(a.shape) >= 1 << 16 else a for a in args
+    ]
 
 
 def run(kernel, grid, in_specs, out_specs, out_shape, args, flops=0):
@@ -216,7 +222,7 @@
             out_ref[r, :, columns // TEAM_SIZE :] = w_out_ref[:, r * q_width : (r + 1) * q_width]
 
     out = shape((TEAM_SIZE, owned, columns // TEAM_SIZE + q_width), BF16)
-    return run(kernel, (1,), [whole(w_qkv), whole(w_out)], whole(out), out, [w_qkv, w_out])
+    return run(kernel, (1,), [whole(w_qkv), whole(w_out)], whole(out), out, in_hbm([w_qkv, w_out]))
 
 
 def pack_chunks(w_gate_up, w_down, chunk):
@@ -246,8 +252,8 @@
         r = pl.program_id(0)
         total = jnp.zeros((owned, 1), F32)
         for j in range(CHUNKS):
-            back_ref = rest_ref if j else first_ref
-            at, to = 3 * chunk * max(j - 1, 0), slice(j * chunk, (j + 1) * chunk)
+            back_ref = rest_ref if j == CHUNKS - 1 else first_ref
+            at, to = 3 * chunk * (j % (CHUNKS - 1)), slice(j * chunk, (j + 1) * chunk)
             for part in range(2):
                 value = back_ref[0, :, at + part * chunk : at + (part + 1) * chunk].astype(F32)
                 gate_up_ref[:, part, to] = value
@@ -275,7 +281,7 @@
         [pl.BlockSpec((1,) + b.shape[1:], lambda r: (r, 0, 0)) for b in (first, rest)] + [wide, whole(gain)],
         [wide, pl.BlockSpec((owned, per), lambda r: (0, r)), whole(gain)],
         outs,
-        [first, rest, w_gate_up, gain],
+        in_hbm([first, rest, w_gate_up, gain]),
     )
 
 
@@ -587,7 +593,7 @@
         half_specs(nm, width, steps) + half_specs(dy, width, steps) + w_specs,
         [row(chunk), row(2 * chunk)],
         outs,
-        [*nm[0], *dy[0], *blocks],
+        in_hbm([*nm[0], *dy[0], *blocks]),
         flops=2 * tokens * width * 3 * chunk,
     )
 
@@ -652,7 +658,7 @@
 
     out = shape((4, rows, width), BF16)
     args = [place, own, x, z, both]
-    result = run(kernel, (1,), [scalars()] + [whole(a) for a in args[1:]], whole(out), out, args)
+    result = run(kernel, (1,), [scalars()] + [whole(a) for a in args[1:]], whole(out), out, in_hbm(args))
     return result.reshape(4 * rows, width)
 
 
@@ -844,6 +850,7 @@
     cosine, sine = jnp.cos(angle), jnp.sin(angle)
     cosine = jnp.concatenate([cosine, cosine], axis=1)
     sine = jnp.concatenate([-sine, sine], axis=1)
+    w_attn, x_parts = hold(w_attn, x_parts)
     x_half = assemble(*x_parts, corner)
     x_side = ([x_half, other_core(x_half)], 0)
     normed_in, raw, qkv = project(x_side, w_attn, g_attn, g_q, g_k, cosine, sine, q_width)
@@ -931,16 +938,11 @@
     arriving[1] = to_near(going[1])
     d_half = spread(d_copies)
     going[2] = near_send(*mlp[2])
-    received = other_core(back_rows(1, out_pairs))
-    out_total = back_rows(0, out_pairs, received, corner)
     sums[1] = own_terms(arriving[1], *mlp[1])
-    d_half, sums[1], arrived_far[0], going[2], out_total = hold(
-        d_half, sums[1], arrived_far[0], going[2], out_total
-    )
+    d_half, sums[1], arrived_far[0], going[2] = hold(d_half, sums[1], arrived_far[0], going[2])
 
     arrived_far[1] = to_far(sums[1])
     arriving[2] = to_near(going[2])
-    out_both = other_x(out_total[3])
     d_branch = ([d_half, other_core(d_half)], 0)
     d_attended = attended_gradient(d_branch, w_attn, out_column, q_width)
     d_attended = d_attended.reshape(2, 2, 2 * rows, q_width)
@@ -966,33 +968,41 @@
     going[3] = near_send(*attention)
     terms, arriving[2] = hold(terms, arriving[2])
     sums[2] = own_terms(arriving[2], *mlp[2])
-    out_z = plain_sum(out_total[2], out_both)
-    terms, sums[2], arrived_far[1], out_total, out_z, going[3] = hold(
-        terms, sums[2], arrived_far[1], out_total, out_z, going[3]
-    )
+    head_gains = all_sum(head_gains, sizes, ("c",))
+    terms, sums[2], arrived_far[1], going[3], head_gains, hidden = hold(
+        terms, sums[2], arrived_far[1], going[3], head_gains, hidden
+    )
+    out_pairs = [(hidden[j], weights[j], 2, chunk) for j in range(CHUNKS)]
 
     arriving[3] = to_near(going[3])
     arrived_far[2] = to_far(sums[2])
     in_both = other_x(terms[3])
+    received = other_core(back_rows(1, out_pairs))
+    out_total = back_rows(0, out_pairs, received, corner)
+    out_both = other_x(out_total[3])
+    sums[3] = own_terms(arriving[3], *attention)
+    head_gains = all_sum(head_gains, sizes, ("xl",))
+    in_z = plain_sum(terms[2], in_both)
+    back_first = [far_total(sums[j][0], arrived_far[j]) for j in range(CHUNKS - 1)]
+    back_first = exchange(jnp.concatenate(back_first, axis=2))
+    terms, in_z, sums[3], arrived_far[2], head_gains, out_total, out_both, back_first = hold(
+        terms, in_z, sums[3], arrived_far[2], head_gains, out_total, out_both, back_first
+    )
+
+    arrived_far[3] = to_far(sums[3])
+    back = exchange(far_total(sums[CHUNKS - 1][0], arrived_far[CHUNKS - 1]))
+    out_z = plain_sum(out_total[2], out_both)
     output = plain_sum(middle, out_total[0], other_x(out_total[1]), other_z(out_z))
-    sums[3] = own_terms(arriving[3], *attention)
-    head_gains = all_sum(head_gains, sizes, ("c", "xl"))
-    in_z = plain_sum(terms[2], in_both)
-    back_first = exchange(far_total(sums[0][0], arrived_far[0]))
-    terms, in_z, sums[3], arrived_far[2], head_gains, output, back_first = hold(
-        terms, in_z, sums[3], arrived_far[2], head_gains, output, back_first
-    )
-
-    arrived_far[3] = to_far(sums[3])
-    back = jnp.concatenate([far_total(sums[j][0], arrived_far[j]) for j in range(1, CHUNKS)], axis=2)
-    back = exchange(back)
     terms = jnp.stack([terms[0], other_x(terms[1]), other_z(in_z)])
     (token_grad,) = norm_back_step(terms, x_own, d_middle, g_attn, 1)
     token_grad, output = reorder([token_grad, output], places, True)
-    head_gains = all_sum(head_gains, sizes, ("zl", "y", "xh", "zh"))
-    back, arrived_far[3], head_gains, token_grad = hold(back, arrived_far[3], head_gains, token_grad)
+    head_gains = all_sum(head_gains, sizes, ("zl",))
+    back, arrived_far[3], head_gains, token_grad, output = hold(
+        back, arrived_far[3], head_gains, token_grad, output
+    )
 
     last = exchange(far_total(sums[3][0], arrived_far[3]))
+    head_gains = all_sum(head_gains, sizes, ("y", "xh", "zh"))
     grad_gate_up, grad_down, grad_mlp_gain = unpack_chunks(
         back_first, back, w_gate_up_rows, mlp_gain.astype(F32).reshape(owned, 1), chunk
     )

time: 583 us -> 566 us (0.971)
  local copies, waits for them, and re-layouts: 68 us -> 55 us
  Pallas kernels: 134 us -> 140 us
  waiting for transfers between devices: 256 us -> 250 us
    ppermute x4, waiting for transfers between devices: 31.7 us -> 49.8 us  [to_near(): return lax.ppermute(value, ('y', 'xh'), self.shifted(n))]
    ppermute x10, waiting for transfers between devices: 78.5 us -> 64.1 us  [all_sum(): lax.ppermute(value, axis, [((i + k) % sizes[axis], i) for i in range(size...]
    unnamed x285 -> x281, local copies, waits for them, and re-layouts: 57.7 us -> 44.9 us
    ppermute x4, waiting for transfers between devices: 6.24 us -> 0.01 us  [to_far(): lax.ppermute(value, 'zh', [(i, (i + k) % self.zh) for i in range(self.zh)])]
  transfers between devices with their start and end apart: 60 -> 60, of which waited for: 27 -> 25; matrix products, arithmetic and copies ran while one was open for 3% -> 4% of each run, Pallas kernels for 19% -> 20%
where the time goes in v4:
time: 566 us; the launch traced here: 559 us
  waiting for transfers between devices  250 us (44%)
  Pallas kernels  140 us (25%)
  starting transfers between devices  96.2 us (17%)
  local copies, waits for them, and re-layouts  55 us (10%)
  other arithmetic  14.8 us (3%)
    pallas_call x36, Pallas kernels, run(): pl.pallas_call(kernel, grid=grid, in_specs=in_specs, out_specs=out_specs,...  137 us
    ppermute x10, waiting for transfers between devices, all_sum(): lax.ppermute(value, axis, [((i + k) % sizes[axis], i) for i in range(size...  64.1 us
    ppermute x4, waiting for transfers between devices, to_near(): return lax.ppermute(value, ('y', 'xh'), self.shifted(n))  49.8 us
    unnamed x281, local copies, waits for them, and re-layouts  44.9 us
    all_to_all x4, waiting for transfers between devices, among_four(): return lax.all_to_all(value, ('zl', 'xl'), 0, 0, tiled=True)  42.5 us
    ppermute x8, waiting for transfers between devices, near_blocks(): lax.ppermute(block, ('y', 'xh'), [(b, a) for a, b in self.shifted(n)])  37.9 us
    ppermute x8, waiting for transfers between devices, other_x(): return lax.ppermute(value, 'xl', SWAP)  32.2 us
    all_to_all x6, starting transfers between devices, exchange(): return lax.all_to_all(value, TEAM, 0, 0, tiled=True)  26.7 us
  transfers between devices with their start and end apart: 60, of which 25 were waited for; matrix products, arithmetic and copies ran while one was open for 4% of the time, Pallas kernels for 20%

profile of v4, /device:TPU:0, one launch (start us, length us, event | category | flops | bytes accessed | tf_op | source)
XLA Modules:
  0.0 559.0 jit_solution(14151205597569853344)
XLA Ops:
  2.9 5.2 all-to-all-start
  8.9 4.4 shard_map.187
  37.4 12.2 %collective-permute-done.5 = bf16[32,264]{1,0:T(8,128)(2,1)S(1)} collective-permute-done((bf16[32,264]{1,0:T(8,128)(2,1)S(1)}, bf16[32,264]{1,0:T(8,128)(2,1)S(1)}, u32[]{:S(2)}, u32[]{:S(2)}) %collective-permute-start.5) | collective-permute-done | bytes 16928 | tf_op jit(solution)/shard_map/ppermute | solution.py:103
  52.2 16.5 %collective-permute-done.6 = bf16[32,264]{1,0:T(8,128)(2,1)S(1)} collective-permute-done((bf16[32,264]{1,0:T(8,128)(2,1)S(1)}, bf16[32,264]{1,0:T(8,128)(2,1)S(1)}, u32[]{:S(2)}, u32[]{:S(2)}) %collective-permute-start.6) | collective-permute-done | bytes 16928 | tf_op jit(solution)/shard_map/ppermute | solution.py:103
  70.3 5.0 all-to-all-start.2
  82.0 24.8 %collective-permute-done.10.refs_3_ = bf16[128,2048]{1,0:T(8,128)(2,1)S(1)} collective-permute-done((bf16[128,2048]{1,0:T(8,128)(2,1)}, bf16[128,2048]{1,0:T(8,128)(2,1)S(1)}, u32[]{:S(2)}, u32[]{:S(2)}) %collective-permute-start.10) | collective-permute-done | bytes 524320 | tf_op jit(solution)/shard_map/ppermute | solution.py:88
  122.6 6.8 %shard_map.190 = (bf16[1024,2048]{1,0:T(8,128)(2,1)S(1)}, f32[1024,384]{1,0:T(8,128)S(1)}, bf16[1024,512]{1,0:T(8,128)(2,1)S(1)}) custom-call(bf16[512,2048]{1,0:T(8,128)(2,1)S(1)} %bitcast.117, bf16[512,2048]{1,0:T(8,128)(2,1)} %collective-permute-done.11.x1, bf16[512,768]{1,0:T(8,128)(2,1)S(1)} %bitcast.122, bf16[512,768]{1,0:T(8,128)(2,1)S(1)} %copy-done.74, ...), custom_call_target="tpu_custom_call" | custom-call | flops 214748364800 | bytes 1521356800 | tf_op jit(solution)/shard_map/pallas_call | solution.py:144
  150.5 36.4 %all-to-all-done.3.parts_ref = bf16[4,128,2048]{2,1,0:T(8,128)(2,1)S(1)} async-done(((bf16[4,128,2048]{2,1,0:T(8,128)(2,1)}), bf16[4,128,2048]{2,1,0:T(8,128)(2,1)S(1)}, u32[]{:S(2)}, u32[]{:S(2)}) %all-to-all-start.3) | async-done | bytes 2097184 | tf_op jit(solution)/shard_map/all_to_all | solution.py:76
  198.9 17.6 %collective-permute-done.22.refs_3_.refs_10_.refs_11_ = bf16[512,768]{1,0:T(8,128)(2,1)S(1)} collective-permute-done((bf16[512,768]{1,0:T(8,128)(2,1)}, bf16[512,768]{1,0:T(8,128)(2,1)S(1)}, u32[]{:S(2)}, u32[]{:S(2)}) %collective-permute-start.22) | collective-permute-done | bytes 786464 | tf_op jit(solution)/shard_map/ppermute | solution.py:65
  216.5 16.4 %collective-permute-done.23.refs_2_.refs_13_.refs_14_ = bf16[512,768]{1,0:T(8,128)(2,1)S(1)} collective-permute-done((bf16[512,768]{1,0:T(8,128)(2,1)S(1)}, bf16[512,768]{1,0:T(8,128)(2,1)S(1)}, u32[]{:S(2)}, u32[]{:S(2)}) %collective-permute-start.23) | collective-permute-done | bytes 786464 | tf_op jit(solution)/shard_map/ppermute | solution.py:65
  240.9 7.7 %shard_map.198 = (bf16[1024,256]{1,0:T(8,128)(2,1)S(1)}, bf16[1024,512]{1,0:T(8,128)(2,1)S(1)}) custom-call(bf16[512,2048]{1,0:T(8,128)(2,1)} %bitcast.97, bf16[512,2048]{1,0:T(8,128)(2,1)} %copy-done.56, bf16[512,2048]{1,0:T(8,128)(2,1)} %bitcast.107, bf16[512,2048]{1,0:T(8,128)(2,1)} %collective-permute-done.21.dy1.refs_3_, ...), custom_call_target="tpu_custom_call" | custom-call | flops 322122547200 | bytes 1310720000 | tf_op jit(solution)/shard_map/pallas_call | solution.py:144
  248.7 8.4 %shard_map.196 = (bf16[1024,256]{1,0:T(8,128)(2,1)S(1)}, bf16[1024,512]{1,0:T(8,128)(2,1)S(1)}) custom-call(bf16[512,2048]{1,0:T(8,128)(2,1)} %bitcast.98, bf16[512,2048]{1,0:T(8,128)(2,1)} %copy-done.56, bf16[512,2048]{1,0:T(8,128)(2,1)} %bitcast.108, bf16[512,2048]{1,0:T(8,128)(2,1)} %collective-permute-done.21.dy1.refs_3_, ...), custom_call_target="tpu_custom_call" | custom-call | flops 322122547200 | bytes 1310720000 | tf_op jit(solution)/shard_map/pallas_call | solution.py:144
  257.1 4.5 shard_map.197
  261.7 7.9 %shard_map.199 = (bf16[1024,256]{1,0:T(8,128)(2,1)S(1)}, bf16[1024,512]{1,0:T(8,128)(2,1)S(1)}) custom-call(bf16[512,2048]{1,0:T(8,128)(2,1)} %bitcast.99, bf16[512,2048]{1,0:T(8,128)(2,1)} %copy-done.56, bf16[512,2048]{1,0:T(8,128)(2,1)} %bitcast.109, bf16[512,2048]{1,0:T(8,128)(2,1)} %collective-permute-done.21.dy1.refs_3_, ...), custom_call_target="tpu_custom_call" | custom-call | flops 322122547200 | bytes 1310720000 | tf_op jit(solution)/shard_map/pallas_call | solution.py:144
  269.7 6.2 %shard_map.200 = bf16[512,2048]{1,0:T(8,128)(2,1)S(1)} custom-call(bf16[1024,512]{1,0:T(8,128)(2,1)S(1)} %get-tuple-element.243.refs_4_.refs_0_, bf16[1024,512]{1,0:T(8,128)(2,1)S(1)} %get-tuple-element.251.refs_1_.refs_4_, bf16[1024,512]{1,0:T(8,128)(2,1)S(1)} %get-tuple-element.257.refs_2_.refs_4_, bf16[512,768]{1,0:T(8,128)(2,1)} %bitcast.13.refs_0_.refs_3_.refs_4_, ...), custom_call_target="tpu_custom_call" | custom-call | flops 322122547200 | bytes 1468006400 | tf_op jit(solution)/shard_map/pallas_call | solution.py:144
  280.2 5.8 %shard_map.201 = bf16[512,2048]{1,0:T(8,128)(2,1)S(1)} custom-call(bf16[1024,512]{1,0:T(8,128)(2,1)S(1)} %get-tuple-element.243.refs_4_.refs_0_, bf16[1024,512]{1,0:T(8,128)(2,1)S(1)} %get-tuple-element.251.refs_1_.refs_4_, bf16[1024,512]{1,0:T(8,128)(2,1)S(1)} %get-tuple-element.257.refs_2_.refs_4_, bf16[512,768]{1,0:T(8,128)(2,1)} %bitcast.13.refs_0_.refs_3_.refs_4_, ...), custom_call_target="tpu_custom_call" | custom-call | flops 322122547200 | bytes 1677721600 | tf_op jit(solution)/shard_map/pallas_call | solution.py:144
  287.3 4.6 all-to-all-start.5
  301.7 11.4 %collective-permute-done.28.refs_6_ = bf16[1024,768]{1,0:T(8,128)(2,1)} collective-permute-done((bf16[1024,768]{1,0:T(8,128)(2,1)}, bf16[1024,768]{1,0:T(8,128)(2,1)}, u32[]{:S(2)}, u32[]{:S(2)}) %collective-permute-start.28) | collective-permute-done | bytes 1572896 | tf_op jit(solution)/shard_map/ppermute | solution.py:69
  313.1 6.0 %shard_map.204 = (bf16[512,768]{1,0:T(8,128)(2,1)S(1)}, bf16[512,768]{1,0:T(8,128)(2,1)}) custom-call(bf16[512,2048]{1,0:T(8,128)(2,1)S(1)} %bitcast.102, bf16[512,2048]{1,0:T(8,128)(2,1)S(1)} %copy-done.58, bf16[512,2048]{1,0:T(8,128)(2,1)S(1)} %bitcast.112, bf16[512,2048]{1,0:T(8,128)(2,1)} %collective-permute-done.21.dy1.refs_3_, ...), custom_call_target="tpu_custom_call" | custom-call | flops 161061273600 | bytes 1310720000 | tf_op jit(solution)/shard_map/pallas_call | solution.py:144
  328.6 4.7 all-to-all-start.6
  343.7 17.4 %collective-permute-done.29.refs_6_ = bf16[1024,768]{1,0:T(8,128)(2,1)} collective-permute-done((bf16[1024,768]{1,0:T(8,128)(2,1)}, bf16[1024,768]{1,0:T(8,128)(2,1)}, u32[]{:S(2)}, u32[]{:S(2)}) %collective-permute-start.29) | collective-permute-done | bytes 1572896 | tf_op jit(solution)/shard_map/ppermute | solution.py:69
  361.1 5.1 shard_map.205
  368.0 5.3 all-to-all-done.6
  385.1 5.5 shard_map.208
  410.6 5.2 shard_map.212
  417.6 4.8 shard_map.216
  435.5 7.4 %collective-permute-done.36.refs_1_ = bf16[128,2048]{1,0:T(8,128)(2,1)S(1)} collective-permute-done((bf16[128,2048]{1,0:T(8,128)(2,1)}, bf16[128,2048]{1,0:T(8,128)(2,1)S(1)}, u32[]{:S(2)}, u32[]{:S(2)}) %collective-permute-start.36) | collective-permute-done | bytes 524320 | tf_op jit(solution)/shard_map/ppermute | solution.py:88
  454.2 17.1 %collective-permute-done.37.refs_5_ = bf16[1024,768]{1,0:T(8,128)(2,1)} collective-permute-done((bf16[1024,768]{1,0:T(8,128)(2,1)}, bf16[1024,768]{1,0:T(8,128)(2,1)}, u32[]{:S(2)}, u32[]{:S(2)}) %collective-permute-start.37) | collective-permute-done | bytes 1572896 | tf_op jit(solution)/shard_map/ppermute | solution.py:69
  471.3 5.0 shard_map.215
  492.1 28.1 %collective-permute-done.43 = f32[8,128]{1,0:T(8,128)S(1)} collective-permute-done((f32[8,128]{1,0:T(8,128)S(1)}, f32[8,128]{1,0:T(8,128)S(1)}, u32[]{:S(2)}, u32[]{:S(2)}) %collective-permute-start.43) | collective-permute-done | bytes 4128 | tf_op jit(solution)/shard_map/ppermute | solution.py:103
  524.8 10.0 %collective-permute-done.47.refs_3_ = bf16[128,2048]{1,0:T(8,128)(2,1)S(1)} collective-permute-done((bf16[128,2048]{1,0:T(8,128)(2,1)S(1)}, bf16[128,2048]{1,0:T(8,128)(2,1)S(1)}, u32[]{:S(2)}, u32[]{:S(2)}) %collective-permute-start.47) | collective-permute-done | bytes 524320 | tf_op jit(solution)/shard_map/ppermute | solution.py:92
  547.0 8.1 %shard_map.223 = (f32[64,2,6144]{2,1,0:T(2,128)}, f32[64,6144]{1,0:T(8,128)}, f32[64,1]{1,0:T(8,128)S(1)}) custom-call(bf16[8,64,1536]{2,1,0:T(8,128)(2,1)} %all-to-all-done.7.first_ref, bf16[8,64,768]{2,1,0:T(8,128)(2,1)} %all-to-all-done.8.rest_ref, bf16[64,2,6144]{2,1,0:T(2,128)(2,1)} %w_ref.5, f32[64,1]{1,0:T(8,128)S(1)} %copy.38.gain_ref), custom_call_target="tpu_custom_call" | custom-call | bytes 865126400 | tf_op jit(solution)/shard_map/pallas_call | solution.py:144
  (478 shorter events, 224.9 us)
Async XLA Ops:
  24.9 44.5 %all-to-all-start.1 = ((bf16[8,64,768]{2,1,0:T(8,128)(2,1)}), bf16[8,64,768]{2,1,0:T(8,128)(2,1)}, u32[]{:S(2)}, u32[]{:S(2)}) async-start(bf16[8,64,768]{2,1,0:T(8,128)(2,1)} %get-tuple-element.167), calls=%async_computation.1 | async-start | bytes 1572864 | tf_op jit(solution)/shard_map/all_to_all | solution.py:96
  29.2 40.2 %collective-permute-start.3 = (bf16[512,768]{1,0:T(8,128)(2,1)S(1)}, bf16[512,768]{1,0:T(8,128)(2,1)S(1)}, u32[]{:S(2)}, u32[]{:S(2)}) collective-permute-start(bf16[512,768]{1,0:T(8,128)(2,1)S(1)} %bitcast.120), channel_id=1, source_target_pairs={{4,0},{0,4},{5,1},{1,5},{6,2},{2,6},{7,3},{3,7},{12,8},{8,12},{13,... | collective-permute-start | bytes 2359304 | tf_op jit(solution)/shard_map/ppermute | solution.py:65
  30.8 38.7 %collective-permute-start.4 = (bf16[512,768]{1,0:T(8,128)(2,1)S(1)}, bf16[512,768]{1,0:T(8,128)(2,1)S(1)}, u32[]{:S(2)}, u32[]{:S(2)}) collective-permute-start(bf16[512,768]{1,0:T(8,128)(2,1)S(1)} %bitcast.121), channel_id=1, source_target_pairs={{16,0},{0,16},{17,1},{1,17},{18,2},{2,18},{19,3},{3,19},{20,4},{4,... | collective-permute-start | bytes 2359304 | tf_op jit(solution)/shard_map/ppermute | solution.py:52
  33.5 35.2 %collective-permute-start.7 = (bf16[128,2048]{1,0:T(8,128)(2,1)S(1)}, bf16[128,2048]{1,0:T(8,128)(2,1)}, u32[]{:S(2)}, u32[]{:S(2)}) collective-permute-start(bf16[128,2048]{1,0:T(8,128)(2,1)S(1)} %get-tuple-element.178.refs_0_.x_ref.base_ref), channel_id=1, source_target_pairs={{0,2},{2,0},{1,3},{3,1},{4,6},{6,4},{5,7},{7,5},{8,10},{10,8},{9,1... | collective-permute-start | bytes 1572872 | tf_op jit(solution)/shard_map/ppermute | solution.py:88
  35.4 34.0 %collective-permute-start.8 = (bf16[128,2048]{1,0:T(8,128)(2,1)S(1)}, bf16[128,2048]{1,0:T(8,128)(2,1)}, u32[]{:S(2)}, u32[]{:S(2)}) collective-permute-start(bf16[128,2048]{1,0:T(8,128)(2,1)S(1)} %get-tuple-element.178.refs_0_.x_ref.base_ref), channel_id=1, source_target_pairs={{0,8},{8,0},{1,9},{9,1},{2,10},{10,2},{3,11},{11,3},{4,12},{12,4},... | collective-permute-start | bytes 1572872 | tf_op jit(solution)/shard_map/ppermute | solution.py:92
  70.3 49.4 %all-to-all-start.2 = ((bf16[8,64,1536]{2,1,0:T(8,128)(2,1)}), bf16[8,64,1536]{2,1,0:T(8,128)(2,1)}, u32[]{:S(2)}, u32[]{:S(2)}) async-start(bf16[8,64,1536]{2,1,0:T(8,128)(2,1)} %get-tuple-element.193), calls=%async_computation.2 | async-start | bytes 3145728 | tf_op jit(solution)/shard_map/all_to_all | solution.py:96
  75.3 58.6 %collective-permute-start.14 = (bf16[512,768]{1,0:T(8,128)(2,1)}, bf16[512,768]{1,0:T(8,128)(2,1)}, u32[]{:S(2)}, u32[]{:S(2)}) collective-permute-start(bf16[512,768]{1,0:T(8,128)(2,1)} %bitcast.13.refs_0_.refs_3_.refs_4_), channel_id=1, source_target_pairs={{4,0},{0,4},{5,1},{1,5},{6,2},{2,6},{7,3},{3,7},{12,8},{8,12},{13,... | collective-permute-start | bytes 2359304 | tf_op jit(solution)/shard_map/ppermute | solution.py:65
  76.9 57.0 %collective-permute-start.15 = (bf16[512,768]{1,0:T(8,128)(2,1)}, bf16[512,768]{1,0:T(8,128)(2,1)}, u32[]{:S(2)}, u32[]{:S(2)}) collective-permute-start(bf16[512,768]{1,0:T(8,128)(2,1)} %bitcast.13.refs_0_.refs_3_.refs_4_), channel_id=1, source_target_pairs={{16,0},{0,16},{17,1},{1,17},{18,2},{2,18},{19,3},{3,19},{20,4},{4,... | collective-permute-start | bytes 2359304 | tf_op jit(solution)/shard_map/ppermute | solution.py:52
  81.9 52.0 %collective-permute-start.12 = (bf16[128,2048]{1,0:T(8,128)(2,1)}, bf16[128,2048]{1,0:T(8,128)(2,1)}, u32[]{:S(2)}, u32[]{:S(2)}) collective-permute-start(bf16[128,2048]{1,0:T(8,128)(2,1)} %get-tuple-element.205.refs_0_.passed_ref), channel_id=1, source_target_pairs={{0,2},{2,0},{1,3},{3,1},{4,6},{6,4},{5,7},{7,5},{8,10},{10,8},{9,1... | collective-permute-start | bytes 1572872 | tf_op jit(solution)/shard_map/ppermute | solution.py:88
  140.7 46.3 %all-to-all-start.3 = ((bf16[4,128,2048]{2,1,0:T(8,128)(2,1)}), bf16[4,128,2048]{2,1,0:T(8,128)(2,1)S(1)}, u32[]{:S(2)}, u32[]{:S(2)}) async-start(bf16[4,128,2048]{2,1,0:T(8,128)(2,1)} %bitcast.118), calls=%async_computation.3 | async-start | bytes 4194304 | tf_op jit(solution)/shard_map/all_to_all | solution.py:76
  144.7 45.3 %collective-permute-start.17 = (bf16[512,768]{1,0:T(8,128)(2,1)}, bf16[512,768]{1,0:T(8,128)(2,1)}, u32[]{:S(2)}, u32[]{:S(2)}) collective-permute-start(bf16[512,768]{1,0:T(8,128)(2,1)} %collective-permute-done.15.refs_1_.refs_4_.refs_5_), channel_id=1, source_target_pairs={{4,0},{0,4},{5,1},{1,5},{6,2},{2,6},{7,3},{3,7},{12,8},{8,12},{13,... | collective-permute-start | bytes 2359304 | tf_op jit(solution)/shard_map/ppermute | solution.py:65
  146.2 43.8 %collective-permute-start.18 = (bf16[512,768]{1,0:T(8,128)(2,1)}, bf16[512,768]{1,0:T(8,128)(2,1)}, u32[]{:S(2)}, u32[]{:S(2)}) collective-permute-start(bf16[512,768]{1,0:T(8,128)(2,1)} %get-tuple-element.225.refs_0_.refs_7_.refs_8_), channel_id=1, source_target_pairs={{4,0},{0,4},{5,1},{1,5},{6,2},{2,6},{7,3},{3,7},{12,8},{8,12},{13,... | collective-permute-start | bytes 2359304 | tf_op jit(solution)/shard_map/ppermute | solution.py:65
  146.7 43.3 %collective-permute-start.19 = (bf16[512,768]{1,0:T(8,128)(2,1)}, bf16[512,768]{1,0:T(8,128)(2,1)}, u32[]{:S(2)}, u32[]{:S(2)}) collective-permute-start(bf16[512,768]{1,0:T(8,128)(2,1)} %get-tuple-element.225.refs_0_.refs_7_.refs_8_), channel_id=1, source_target_pairs={{16,0},{0,16},{17,1},{1,17},{18,2},{2,18},{19,3},{3,19},{20,4},{4,... | collective-permute-start | bytes 2359304 | tf_op jit(solution)/shard_map/ppermute | solution.py:52
  148.5 41.5 %collective-permute-start.20 = (bf16[128,2048]{1,0:T(8,128)(2,1)}, bf16[128,2048]{1,0:T(8,128)(2,1)}, u32[]{:S(2)}, u32[]{:S(2)}) collective-permute-start(bf16[128,2048]{1,0:T(8,128)(2,1)} %collective-permute-done.13.refs_2_), channel_id=1, source_target_pairs={{0,2},{2,0},{1,3},{3,1},{4,6},{6,4},{5,7},{7,5},{8,10},{10,8},{9,1... | collective-permute-start | bytes 1572872 | tf_op jit(solution)/shard_map/ppermute | solution.py:88
  190.0 45.4 %all-to-all-start.4 = ((bf16[4,128,2048]{2,1,0:T(8,128)(2,1)}), bf16[4,128,2048]{2,1,0:T(8,128)(2,1)S(1)}, u32[]{:S(2)}, u32[]{:S(2)}) async-start(bf16[4,128,2048]{2,1,0:T(8,128)(2,1)} %copy-done.19), calls=%async_computation.4 | async-start | bytes 4194304 | tf_op jit(solution)/shard_map/all_to_all | solution.py:76
  195.8 38.9 %collective-permute-start.21 = (bf16[512,2048]{1,0:T(8,128)(2,1)S(1)}, bf16[512,2048]{1,0:T(8,128)(2,1)}, u32[]{:S(2)}, u32[]{:S(2)}) collective-permute-start(bf16[512,2048]{1,0:T(8,128)(2,1)S(1)} %bitcast.106), channel_id=1, source_target_pairs={{0,1},{1,0},{2,3},{3,2},{4,5},{5,4},{6,7},{7,6},{8,9},{9,8},{10,11... | collective-permute-start | bytes 6291464 | tf_op jit(solution)/shard_map/ppermute | solution.py:84
  197.4 35.4 %collective-permute-start.23 = (bf16[512,768]{1,0:T(8,128)(2,1)S(1)}, bf16[512,768]{1,0:T(8,128)(2,1)S(1)}, u32[]{:S(2)}, u32[]{:S(2)}) collective-permute-start(bf16[512,768]{1,0:T(8,128)(2,1)S(1)} %copy-done.34), channel_id=1, source_target_pairs={{4,0},{0,4},{5,1},{1,5},{6,2},{2,6},{7,3},{3,7},{12,8},{8,12},{13,... | collective-permute-start | bytes 2359304 | tf_op jit(solution)/shard_map/ppermute | solution.py:65
  197.9 35.3 %collective-permute-start.24 = (bf16[512,768]{1,0:T(8,128)(2,1)S(1)}, bf16[512,768]{1,0:T(8,128)(2,1)S(1)}, u32[]{:S(2)}, u32[]{:S(2)}) collective-permute-start(bf16[512,768]{1,0:T(8,128)(2,1)S(1)} %copy-done.34), channel_id=1, source_target_pairs={{16,0},{0,16},{17,1},{1,17},{18,2},{2,18},{19,3},{3,19},{20,4},{4,... | collective-permute-start | bytes 2359304 | tf_op jit(solution)/shard_map/ppermute | solution.py:52
  276.1 37.0 %collective-permute-start.28 = (bf16[1024,768]{1,0:T(8,128)(2,1)}, bf16[1024,768]{1,0:T(8,128)(2,1)}, u32[]{:S(2)}, u32[]{:S(2)}) collective-permute-start(bf16[1024,768]{1,0:T(8,128)(2,1)} %shard_map.197), channel_id=1, source_target_pairs={{0,4},{4,0},{1,5},{5,1},{2,6},{6,2},{3,7},{7,3},{8,12},{12,8},{9,1... | collective-permute-start | bytes 4718600 | tf_op jit(solution)/shard_map/ppermute | solution.py:69
  324.9 36.2 %collective-permute-start.29 = (bf16[1024,768]{1,0:T(8,128)(2,1)}, bf16[1024,768]{1,0:T(8,128)(2,1)}, u32[]{:S(2)}, u32[]{:S(2)}) collective-permute-start(bf16[1024,768]{1,0:T(8,128)(2,1)} %shard_map.203), channel_id=1, source_target_pairs={{0,4},{4,0},{1,5},{5,1},{2,6},{6,2},{3,7},{7,3},{8,12},{12,8},{9,1... | collective-permute-start | bytes 4718600 | tf_op jit(solution)/shard_map/ppermute | solution.py:69
  326.5 41.6 %collective-permute-start.30 = (bf16[512,768]{1,0:T(8,128)(2,1)}, bf16[512,768]{1,0:T(8,128)(2,1)}, u32[]{:S(2)}, u32[]{:S(2)}) collective-permute-start(bf16[512,768]{1,0:T(8,128)(2,1)} %get-tuple-element.256), channel_id=1, source_target_pairs={{0,16},{16,0},{1,17},{17,1},{2,18},{18,2},{3,19},{19,3},{4,20},{20... | collective-permute-start | bytes 2359304 | tf_op jit(solution)/shard_map/ppermute | solution.py:72
  328.6 44.7 %all-to-all-start.6 = ((bf16[4,128,2048]{2,1,0:T(8,128)(2,1)}), bf16[4,128,2048]{2,1,0:T(8,128)(2,1)}, u32[]{:S(2)}, u32[]{:S(2)}) async-start(bf16[4,128,2048]{2,1,0:T(8,128)(2,1)} %copy-done.20), calls=%async_computation.6 | async-start | bytes 4194304 | tf_op jit(solution)/shard_map/all_to_all | solution.py:76
  373.4 37.1 %collective-permute-start.33 = (bf16[1024,768]{1,0:T(8,128)(2,1)}, bf16[1024,768]{1,0:T(8,128)(2,1)}, u32[]{:S(2)}, u32[]{:S(2)}) collective-permute-start(bf16[1024,768]{1,0:T(8,128)(2,1)} %copy-done.65), channel_id=1, source_target_pairs={{0,4},{4,0},{1,5},{5,1},{2,6},{6,2},{3,7},{7,3},{8,12},{12,8},{9,1... | collective-permute-start | bytes 4718600 | tf_op jit(solution)/shard_map/ppermute | solution.py:69
  373.9 43.7 %collective-permute-start.34 = (bf16[512,768]{1,0:T(8,128)(2,1)}, bf16[512,768]{1,0:T(8,128)(2,1)}, u32[]{:S(2)}, u32[]{:S(2)}) collective-permute-start(bf16[512,768]{1,0:T(8,128)(2,1)} %copy-done.97), channel_id=1, source_target_pairs={{0,16},{16,0},{1,17},{17,1},{2,18},{18,2},{3,19},{19,3},{4,20},{20... | collective-permute-start | bytes 2359304 | tf_op jit(solution)/shard_map/ppermute | solution.py:72
  430.0 47.3 %all-to-all-start.7 = ((bf16[8,64,1536]{2,1,0:T(8,128)(2,1)}), bf16[8,64,1536]{2,1,0:T(8,128)(2,1)}, u32[]{:S(2)}, u32[]{:S(2)}) async-start(bf16[8,64,1536]{2,1,0:T(8,128)(2,1)} %pad_maximum_fusion), calls=%async_computation.7 | async-start | bytes 3145728 | tf_op jit(solution)/shard_map/all_to_all | solution.py:96
  434.3 37.0 %collective-permute-start.37 = (bf16[1024,768]{1,0:T(8,128)(2,1)}, bf16[1024,768]{1,0:T(8,128)(2,1)}, u32[]{:S(2)}, u32[]{:S(2)}) collective-permute-start(bf16[1024,768]{1,0:T(8,128)(2,1)} %copy-done.64), channel_id=1, source_target_pairs={{0,4},{4,0},{1,5},{5,1},{2,6},{6,2},{3,7},{7,3},{8,12},{12,8},{9,1... | collective-permute-start | bytes 4718600 | tf_op jit(solution)/shard_map/ppermute | solution.py:69
  434.9 42.4 %collective-permute-start.38 = (bf16[512,768]{1,0:T(8,128)(2,1)}, bf16[512,768]{1,0:T(8,128)(2,1)}, u32[]{:S(2)}, u32[]{:S(2)}) collective-permute-start(bf16[512,768]{1,0:T(8,128)(2,1)} %copy-done.96), channel_id=1, source_target_pairs={{0,16},{16,0},{1,17},{17,1},{2,18},{18,2},{3,19},{19,3},{4,20},{20... | collective-permute-start | bytes 2359304 | tf_op jit(solution)/shard_map/ppermute | solution.py:72
  479.5 57.6 %all-to-all-start.8 = ((bf16[8,64,768]{2,1,0:T(8,128)(2,1)}), bf16[8,64,768]{2,1,0:T(8,128)(2,1)}, u32[]{:S(2)}, u32[]{:S(2)}) async-start(bf16[8,64,768]{2,1,0:T(8,128)(2,1)} %bitcast.146), calls=%async_computation.8 | async-start | bytes 1572864 | tf_op jit(solution)/shard_map/all_to_all | solution.py:96
  485.3 37.5 %collective-permute-start.44 = (bf16[128,2048]{1,0:T(8,128)(2,1)S(1)}, bf16[128,2048]{1,0:T(8,128)(2,1)S(1)}, u32[]{:S(2)}, u32[]{:S(2)}) collective-permute-start(bf16[128,2048]{1,0:T(8,128)(2,1)S(1)} %get-tuple-element.314), channel_id=1, source_target_pairs={{0,2},{2,0},{1,3},{3,1},{4,6},{6,4},{5,7},{7,5},{8,10},{10,8},{9,1... | collective-permute-start | bytes 1572872 | tf_op jit(solution)/shard_map/ppermute | solution.py:88
  487.2 35.6 %collective-permute-start.45 = (bf16[128,2048]{1,0:T(8,128)(2,1)S(1)}, bf16[128,2048]{1,0:T(8,128)(2,1)S(1)}, u32[]{:S(2)}, u32[]{:S(2)}) collective-permute-start(bf16[128,2048]{1,0:T(8,128)(2,1)S(1)} %copy-done.47), channel_id=1, source_target_pairs={{0,8},{8,0},{1,9},{9,1},{2,10},{10,2},{3,11},{11,3},{4,12},{12,4},... | collective-permute-start | bytes 1572872 | tf_op jit(solution)/shard_map/ppermute | solution.py:92
  489.3 47.8 %collective-permute-start.42 = (bf16[512,768]{1,0:T(8,128)(2,1)}, bf16[512,768]{1,0:T(8,128)(2,1)}, u32[]{:S(2)}, u32[]{:S(2)}) collective-permute-start(bf16[512,768]{1,0:T(8,128)(2,1)} %copy-done.95), channel_id=1, source_target_pairs={{0,16},{16,0},{1,17},{17,1},{2,18},{18,2},{3,19},{19,3},{4,20},{20... | collective-permute-start | bytes 2359304 | tf_op jit(solution)/shard_map/ppermute | solution.py:72
  490.6 44.2 %collective-permute-start.47 = (bf16[128,2048]{1,0:T(8,128)(2,1)S(1)}, bf16[128,2048]{1,0:T(8,128)(2,1)S(1)}, u32[]{:S(2)}, u32[]{:S(2)}) collective-permute-start(bf16[128,2048]{1,0:T(8,128)(2,1)S(1)} %shard_map.219), channel_id=1, source_target_pairs={{0,8},{8,0},{1,9},{9,1},{2,10},{10,2},{3,11},{11,3},{4,12},{12,4},... | collective-permute-start | bytes 1572872 | tf_op jit(solution)/shard_map/ppermute | solution.py:92
  (167 other events, 1500.2 us)

commit v5 on v4

--- a/solution.py
+++ b/solution.py
@@ -562,39 +562,43 @@
     return run(kernel, (steps,), in_specs, out_spec, out, args, flops=flops)
 
 
-def feed_forward(nm, dy, blocks, chunk):
-    count = len(blocks)
-    per = blocks[0].shape[0]
+def feed_forward(nm, dy, groups, chunk):
+    count = len(groups[0])
+    per = groups[0][0].shape[0]
+    blocks = [w for group in groups for w in group]
     tokens, width = 2 * nm[0][0].shape[0], count * per
     steps = FORWARD_STEPS
     rows = tokens // steps
 
     def kernel(nm0, nm1, dy0, dy1, *refs):
-        w_refs, (hidden_ref, d_ref) = refs[:count], refs[count:]
+        all_refs, out_refs = refs[: len(blocks)], refs[len(blocks) :]
 
         def body(nm_ref, dy_ref):
-            both = dot(nm_ref[...], joined([w[:, : 2 * chunk] for w in w_refs]))
-            d_hidden = dot(dy_ref[...], joined([w[:, 2 * chunk : 3 * chunk] for w in w_refs]))
-            gate, upward = both[:, :chunk], both[:, chunk:]
-            sigma = 1.0 / (1.0 + jnp.exp(-gate))
-            silu = gate * sigma
-            hidden_ref[...] = (silu * upward).astype(BF16)
-            d_ref[:, :chunk] = (d_hidden * upward * (sigma * (1.0 + gate * (1.0 - sigma)))).astype(BF16)
-            d_ref[:, chunk:] = (d_hidden * silu).astype(BF16)
+            for g in range(len(groups)):
+                w_refs = all_refs[g * count : (g + 1) * count]
+                hidden_ref, d_ref = out_refs[2 * g : 2 * g + 2]
+                both = dot(nm_ref[...], joined([w[:, : 2 * chunk] for w in w_refs]))
+                d_hidden = dot(dy_ref[...], joined([w[:, 2 * chunk : 3 * chunk] for w in w_refs]))
+                gate, upward = both[:, :chunk], both[:, chunk:]
+                sigma = 1.0 / (1.0 + jnp.exp(-gate))
+                silu = gate * sigma
+                hidden_ref[...] = (silu * upward).astype(BF16)
+                d_ref[:, :chunk] = (d_hidden * upward * (sigma * (1.0 + gate * (1.0 - sigma)))).astype(BF16)
+                d_ref[:, chunk:] = (d_hidden * silu).astype(BF16)
 
         either(pl.program_id(0), steps, [(nm0, nm1), (dy0, dy1)], body)
 
     row = lambda n: pl.BlockSpec((rows, n), lambda i: (i, 0))
-    outs = [shape((tokens, chunk), BF16), shape((tokens, 2 * chunk), BF16)]
+    outs = [shape((tokens, chunk), BF16), shape((tokens, 2 * chunk), BF16)] * len(groups)
     w_specs = [pl.BlockSpec((per, 3 * chunk), lambda i: (0, 0)) for _ in blocks]
     return run(
         kernel,
         (steps,),
         half_specs(nm, width, steps) + half_specs(dy, width, steps) + w_specs,
-        [row(chunk), row(2 * chunk)],
+        [row(chunk), row(2 * chunk)] * len(groups),
         outs,
         in_hbm([*nm[0], *dy[0], *blocks]),
-        flops=2 * tokens * width * 3 * chunk,
+        flops=2 * tokens * width * 3 * chunk * len(groups),
     )
 
 
@@ -811,10 +815,8 @@
     near, far = {}, {}
     x_parts.append(other_x(x_parts[2]))
     w_attn = gathered(attn_near, [with_near(b) for b in attn_far])
-    near[0], far[0] = with_near(parts[0]), layout.far_blocks(parts[0])
-    rest = arrived(exchange(send_rest))
-    parts += [rest[:, j * 3 * chunk : (j + 1) * 3 * chunk] for j in range(CHUNKS - 1)]
-    dy_parts = [dy_own, other_x(dy_own), other_z(dy_own)]
+    far[0] = layout.far_blocks(parts[0])
+    dy_z = other_z(dy_own)
 
     table = table.astype(F32)
     natural = jnp.stack([table[:, :owned].reshape(width), table[:, owned : 2 * owned].reshape(width)])
@@ -852,6 +854,11 @@
     sine = jnp.concatenate([-sine, sine], axis=1)
     w_attn, x_parts = hold(w_attn, x_parts)
     x_half = assemble(*x_parts, corner)
+    x_half, send_rest, dy_late, late = hold(x_half, send_rest, dy_own, parts[0])
+    near[0] = with_near(late)
+    rest = arrived(exchange(send_rest))
+    parts += [rest[:, j * 3 * chunk : (j + 1) * 3 * chunk] for j in range(CHUNKS - 1)]
+    dy_parts = [dy_own, dy_own, dy_z]
     x_side = ([x_half, other_core(x_half)], 0)
     normed_in, raw, qkv = project(x_side, w_attn, g_attn, g_q, g_k, cosine, sine, q_width)
     qkv4 = qkv.reshape(2, 2, 2 * rows, -1)
@@ -868,7 +875,7 @@
 
     near[1], far[1] = with_near(parts[1]), layout.far_blocks(parts[1])
     weights = [gathered(near[0], [with_near(b) for b in far[0]])]
-    dy_parts.append(other_x(dy_parts[2]))
+    dy_parts = [dy_parts[0], other_x(dy_parts[0]), dy_parts[2], other_x(dy_parts[2])]
     branch = back_rows(0, out_pair, other_core(branch_other))
     branch = among_four(branch.reshape(4, rows, width))
     middle, nm_copies = middle_step(branch, x_own, g_mlp)
@@ -906,19 +913,19 @@
     nm = ([nm_half, other_core(nm_half)], 0)
     hidden, d_gate_up, mlp, going, arriving, sums, arrived_far = [], [], [], {}, {}, {}, {}
 
-    def chunk_step(j):
-        h, d = feed_forward(nm, dy, weights[j], chunk)
-        hidden.append(h)
-        d_gate_up.append(d)
-        mlp.append([(nm, d), (dy, h)])
-
-    chunk_step(0)
-    chunk_step(1)
+    def chunk_steps(*chunks):
+        results = feed_forward(nm, dy, [weights[j] for j in chunks], chunk)
+        for h, d in zip(results[::2], results[1::2]):
+            hidden.append(h)
+            d_gate_up.append(d)
+            mlp.append([(nm, d), (dy, h)])
+
+    chunk_steps(0, 1)
     going[0] = near_send(*mlp[0])
     weights[2], going[0], d_gate_up[1] = hold(weights[2], going[0], d_gate_up[1])
 
     arriving[0] = to_near(going[0])
-    chunk_step(2)
+    chunk_steps(2)
     mid_pairs = [(d_gate_up[j], weights[j], 0, 2 * chunk) for j in range(CHUNKS)]
     out_pairs = [(hidden[j], weights[j], 2, chunk) for j in range(CHUNKS)]
     received = other_core(back_rows(1, mid_pairs))

time: 566 us -> 566 us (level)
  local copies, waits for them, and re-layouts: 55 us -> 68.6 us
  waiting for transfers between devices: 250 us -> 243 us
  Pallas kernels: 140 us -> 134 us
    ppermute x8, waiting for transfers between devices: 32.2 us -> 18.2 us  [other_x(): return lax.ppermute(value, 'xl', SWAP)]
    unnamed x281 -> x291, local copies, waits for them, and re-layouts: 44.9 us -> 58.5 us
    all_to_all x6, waiting for transfers between devices: 0.02 us -> 5.98 us  [exchange(): return lax.all_to_all(value, TEAM, 0, 0, tiled=True)]
    pallas_call x36 -> x35, Pallas kernels: 137 us -> 131 us  [run(): pl.pallas_call(kernel, grid=grid, in_specs=in_specs, out_specs=out_specs,...]
  transfers between devices with their start and end apart: 60 -> 60, of which waited for: 25 -> 27; matrix products, arithmetic and copies ran while one was open for 4% -> 4% of each run, Pallas kernels for 20% -> 19%
where the time goes in v5:
time: 566 us; the launch traced here: 557 us
  waiting for transfers between devices  243 us (43%)
  Pallas kernels  134 us (24%)
  starting transfers between devices  93.6 us (17%)
  local copies, waits for them, and re-layouts  68.6 us (12%)
  other arithmetic  14.8 us (3%)
    pallas_call x35, Pallas kernels, run(): pl.pallas_call(kernel, grid=grid, in_specs=in_specs, out_specs=out_specs,...  131 us
    ppermute x10, waiting for transfers between devices, all_sum(): lax.ppermute(value, axis, [((i + k) % sizes[axis], i) for i in range(size...  63.1 us
    unnamed x291, local copies, waits for them, and re-layouts  58.5 us
    ppermute x4, waiting for transfers between devices, to_near(): return lax.ppermute(value, ('y', 'xh'), self.shifted(n))  51.6 us
    all_to_all x4, waiting for transfers between devices, among_four(): return lax.all_to_all(value, ('zl', 'xl'), 0, 0, tiled=True)  42.4 us
    ppermute x8, waiting for transfers between devices, near_blocks(): lax.ppermute(block, ('y', 'xh'), [(b, a) for a, b in self.shifted(n)])  37.7 us
    all_to_all x6, starting transfers between devices, exchange(): return lax.all_to_all(value, TEAM, 0, 0, tiled=True)  26.5 us
    ppermute x8, waiting for transfers between devices, other_x(): return lax.ppermute(value, 'xl', SWAP)  18.2 us
  transfers between devices with their start and end apart: 60, of which 27 were waited for; matrix products, arithmetic and copies ran while one was open for 4% of the time, Pallas kernels for 19%

profile of v5, /device:TPU:0, one launch (start us, length us, event | category | flops | bytes accessed | tf_op | source)
XLA Modules:
  0.0 557.0 jit_solution(3779417633208840867)
XLA Ops:
  2.9 5.2 all-to-all-start
  37.4 12.1 %collective-permute-done.5 = bf16[32,264]{1,0:T(8,128)(2,1)S(1)} collective-permute-done((bf16[32,264]{1,0:T(8,128)(2,1)S(1)}, bf16[32,264]{1,0:T(8,128)(2,1)S(1)}, u32[]{:S(2)}, u32[]{:S(2)}) %collective-permute-start.5) | collective-permute-done | bytes 16928 | tf_op jit(solution)/shard_map/ppermute | solution.py:103
  52.1 16.5 %collective-permute-done.6 = bf16[32,264]{1,0:T(8,128)(2,1)S(1)} collective-permute-done((bf16[32,264]{1,0:T(8,128)(2,1)S(1)}, bf16[32,264]{1,0:T(8,128)(2,1)S(1)}, u32[]{:S(2)}, u32[]{:S(2)}) %collective-permute-start.6) | collective-permute-done | bytes 16928 | tf_op jit(solution)/shard_map/ppermute | solution.py:103
  77.7 8.7 %collective-permute-done.10.refs_3_ = bf16[128,2048]{1,0:T(8,128)(2,1)} collective-permute-done((bf16[128,2048]{1,0:T(8,128)(2,1)}, bf16[128,2048]{1,0:T(8,128)(2,1)}, u32[]{:S(2)}, u32[]{:S(2)}) %collective-permute-start.10) | collective-permute-done | bytes 524320 | tf_op jit(solution)/shard_map/ppermute | solution.py:88
  97.2 4.8 all-to-all-start.2
  108.1 6.7 %shard_map.190 = (bf16[1024,2048]{1,0:T(8,128)(2,1)S(1)}, f32[1024,384]{1,0:T(8,128)S(1)}, bf16[1024,512]{1,0:T(8,128)(2,1)S(1)}) custom-call(bf16[512,2048]{1,0:T(8,128)(2,1)S(1)} %bitcast.115, bf16[512,2048]{1,0:T(8,128)(2,1)} %collective-permute-done.11.x1, bf16[512,768]{1,0:T(8,128)(2,1)S(1)} %bitcast.120, bf16[512,768]{1,0:T(8,128)(2,1)S(1)} %copy-done.77, ...), custom_call_target="tpu_custom_call" | custom-call | flops 214748364800 | bytes 1521356800 | tf_op jit(solution)/shard_map/pallas_call | solution.py:144
  122.0 6.0 %all-to-all-done.2 = bf16[8,64,1536]{2,1,0:T(8,128)(2,1)} async-done(((bf16[8,64,1536]{2,1,0:T(8,128)(2,1)}), bf16[8,64,1536]{2,1,0:T(8,128)(2,1)}, u32[]{:S(2)}, u32[]{:S(2)}) %all-to-all-start.2) | async-done | bytes 1572896 | tf_op jit(solution)/shard_map/all_to_all | solution.py:96
  145.8 37.7 %all-to-all-done.3.parts_ref = bf16[4,128,2048]{2,1,0:T(8,128)(2,1)S(1)} async-done(((bf16[4,128,2048]{2,1,0:T(8,128)(2,1)}), bf16[4,128,2048]{2,1,0:T(8,128)(2,1)S(1)}, u32[]{:S(2)}, u32[]{:S(2)}) %all-to-all-start.3) | async-done | bytes 2097184 | tf_op jit(solution)/shard_map/all_to_all | solution.py:76
  197.4 18.3 %collective-permute-done.22.refs_7_.refs_10_.refs_11_ = bf16[512,768]{1,0:T(8,128)(2,1)S(1)} collective-permute-done((bf16[512,768]{1,0:T(8,128)(2,1)}, bf16[512,768]{1,0:T(8,128)(2,1)S(1)}, u32[]{:S(2)}, u32[]{:S(2)}) %collective-permute-start.22) | collective-permute-done | bytes 786464 | tf_op jit(solution)/shard_map/ppermute | solution.py:65
  215.7 16.4 %collective-permute-done.23.refs_2_.refs_13_.refs_14_ = bf16[512,768]{1,0:T(8,128)(2,1)S(1)} collective-permute-done((bf16[512,768]{1,0:T(8,128)(2,1)S(1)}, bf16[512,768]{1,0:T(8,128)(2,1)S(1)}, u32[]{:S(2)}, u32[]{:S(2)}) %collective-permute-start.23) | collective-permute-done | bytes 786464 | tf_op jit(solution)/shard_map/ppermute | solution.py:65
  240.6 11.7 %shard_map.196 = (bf16[1024,256]{1,0:T(8,128)(2,1)S(1)}, bf16[1024,512]{1,0:T(8,128)(2,1)S(1)}, bf16[1024,256]{1,0:T(8,128)(2,1)S(1)}, bf16[1024,512]{1,0:T(8,128)(2,1)S(1)}) custom-call(bf16[512,2048]{1,0:T(8,128)(2,1)} %bitcast.97, bf16[512,2048]{1,0:T(8,128)(2,1)} %copy-done.58, bf16[512,2048]{1,0:T(8,128)(2,1)} %bitcast.106, ...), custom_call_target="tpu_custom_call" | custom-call | flops 644245094400 | bytes 1782579200 | tf_op jit(solution)/shard_map/pallas_call | solution.py:144
  260.9 8.1 %shard_map.198 = (bf16[1024,256]{1,0:T(8,128)(2,1)S(1)}, bf16[1024,512]{1,0:T(8,128)(2,1)S(1)}) custom-call(bf16[512,2048]{1,0:T(8,128)(2,1)} %bitcast.98, bf16[512,2048]{1,0:T(8,128)(2,1)} %copy-done.58, bf16[512,2048]{1,0:T(8,128)(2,1)} %bitcast.107, bf16[512,2048]{1,0:T(8,128)(2,1)} %collective-permute-done.21.dy1.refs_3_, ...), custom_call_target="tpu_custom_call" | custom-call | flops 322122547200 | bytes 1310720000 | tf_op jit(solution)/shard_map/pallas_call | solution.py:144
  269.1 6.2 %shard_map.199 = bf16[512,2048]{1,0:T(8,128)(2,1)S(1)} custom-call(bf16[1024,512]{1,0:T(8,128)(2,1)S(1)} %copy-done.120, bf16[1024,512]{1,0:T(8,128)(2,1)S(1)} %get-tuple-element.255.refs_1_.refs_4_, bf16[1024,512]{1,0:T(8,128)(2,1)S(1)} %get-tuple-element.261.refs_2_.refs_4_, bf16[512,768]{1,0:T(8,128)(2,1)} %bitcast.13.refs_0_.refs_3_.refs_4_, ...), custom_call_target="tpu_custom_call" | custom-call | flops 322122547200 | bytes 1468006400 | tf_op jit(solution)/shard_map/pallas_call | solution.py:144
  279.6 5.8 %shard_map.200 = bf16[512,2048]{1,0:T(8,128)(2,1)S(1)} custom-call(bf16[1024,512]{1,0:T(8,128)(2,1)S(1)} %copy-done.120, bf16[1024,512]{1,0:T(8,128)(2,1)S(1)} %get-tuple-element.255.refs_1_.refs_4_, bf16[1024,512]{1,0:T(8,128)(2,1)S(1)} %get-tuple-element.261.refs_2_.refs_4_, bf16[512,768]{1,0:T(8,128)(2,1)} %bitcast.13.refs_0_.refs_3_.refs_4_, ...), custom_call_target="tpu_custom_call" | custom-call | flops 322122547200 | bytes 1677721600 | tf_op jit(solution)/shard_map/pallas_call | solution.py:144
  286.6 4.6 all-to-all-start.5
  296.7 4.3 shard_map.202
  301.0 11.5 %collective-permute-done.28.refs_6_ = bf16[1024,768]{1,0:T(8,128)(2,1)} collective-permute-done((bf16[1024,768]{1,0:T(8,128)(2,1)}, bf16[1024,768]{1,0:T(8,128)(2,1)}, u32[]{:S(2)}, u32[]{:S(2)}) %collective-permute-start.28) | collective-permute-done | bytes 1572896 | tf_op jit(solution)/shard_map/ppermute | solution.py:69
  312.5 6.0 %shard_map.203 = (bf16[512,768]{1,0:T(8,128)(2,1)S(1)}, bf16[512,768]{1,0:T(8,128)(2,1)}) custom-call(bf16[512,2048]{1,0:T(8,128)(2,1)S(1)} %bitcast.101, bf16[512,2048]{1,0:T(8,128)(2,1)S(1)} %copy-done.60, bf16[512,2048]{1,0:T(8,128)(2,1)S(1)} %bitcast.110, bf16[512,2048]{1,0:T(8,128)(2,1)} %collective-permute-done.21.dy1.refs_3_, ...), custom_call_target="tpu_custom_call" | custom-call | flops 161061273600 | bytes 1310720000 | tf_op jit(solution)/shard_map/pallas_call | solution.py:144
  326.4 4.7 all-to-all-start.6
  341.4 19.1 %collective-permute-done.29.refs_6_ = bf16[1024,768]{1,0:T(8,128)(2,1)} collective-permute-done((bf16[1024,768]{1,0:T(8,128)(2,1)}, bf16[1024,768]{1,0:T(8,128)(2,1)}, u32[]{:S(2)}, u32[]{:S(2)}) %collective-permute-start.29) | collective-permute-done | bytes 1572896 | tf_op jit(solution)/shard_map/ppermute | solution.py:69
  360.5 5.1 shard_map.204
  382.6 5.5 shard_map.207
  404.1 4.5 collective-permute-done.33.refs_6_
  408.7 5.2 shard_map.211
  415.7 4.8 shard_map.215
  434.4 6.8 %collective-permute-done.36.refs_1_ = bf16[128,2048]{1,0:T(8,128)(2,1)S(1)} collective-permute-done((bf16[128,2048]{1,0:T(8,128)(2,1)}, bf16[128,2048]{1,0:T(8,128)(2,1)S(1)}, u32[]{:S(2)}, u32[]{:S(2)}) %collective-permute-start.36) | collective-permute-done | bytes 524320 | tf_op jit(solution)/shard_map/ppermute | solution.py:88
  452.5 16.5 %collective-permute-done.37.refs_5_ = bf16[1024,768]{1,0:T(8,128)(2,1)} collective-permute-done((bf16[1024,768]{1,0:T(8,128)(2,1)}, bf16[1024,768]{1,0:T(8,128)(2,1)}, u32[]{:S(2)}, u32[]{:S(2)}) %collective-permute-start.37) | collective-permute-done | bytes 1572896 | tf_op jit(solution)/shard_map/ppermute | solution.py:69
  469.0 5.0 shard_map.214
  477.2 4.3 all-to-all-start.8
  489.8 28.3 %collective-permute-done.43 = f32[8,128]{1,0:T(8,128)S(1)} collective-permute-done((f32[8,128]{1,0:T(8,128)S(1)}, f32[8,128]{1,0:T(8,128)S(1)}, u32[]{:S(2)}, u32[]{:S(2)}) %collective-permute-start.43) | collective-permute-done | bytes 4128 | tf_op jit(solution)/shard_map/ppermute | solution.py:103
  522.7 9.8 %collective-permute-done.47.refs_3_ = bf16[128,2048]{1,0:T(8,128)(2,1)S(1)} collective-permute-done((bf16[128,2048]{1,0:T(8,128)(2,1)S(1)}, bf16[128,2048]{1,0:T(8,128)(2,1)S(1)}, u32[]{:S(2)}, u32[]{:S(2)}) %collective-permute-start.47) | collective-permute-done | bytes 524320 | tf_op jit(solution)/shard_map/ppermute | solution.py:92
  544.9 8.1 %shard_map.222 = (f32[64,2,6144]{2,1,0:T(2,128)}, f32[64,6144]{1,0:T(8,128)}, f32[64,1]{1,0:T(8,128)S(1)}) custom-call(bf16[8,64,1536]{2,1,0:T(8,128)(2,1)} %all-to-all-done.7.first_ref, bf16[8,64,768]{2,1,0:T(8,128)(2,1)} %all-to-all-done.8.rest_ref, bf16[64,2,6144]{2,1,0:T(2,128)(2,1)} %w_ref.5, f32[64,1]{1,0:T(8,128)S(1)} %copy.38.gain_ref), custom_call_target="tpu_custom_call" | custom-call | bytes 865126400 | tf_op jit(solution)/shard_map/pallas_call | solution.py:144
  (487 shorter events, 236.3 us)
Async XLA Ops:
  24.9 45.4 %all-to-all-start.1 = ((bf16[8,64,768]{2,1,0:T(8,128)(2,1)}), bf16[8,64,768]{2,1,0:T(8,128)(2,1)}, u32[]{:S(2)}, u32[]{:S(2)}) async-start(bf16[8,64,768]{2,1,0:T(8,128)(2,1)} %get-tuple-element.169), calls=%async_computation.1 | async-start | bytes 1572864 | tf_op jit(solution)/shard_map/all_to_all | solution.py:96
  29.1 40.3 %collective-permute-start.3 = (bf16[512,768]{1,0:T(8,128)(2,1)S(1)}, bf16[512,768]{1,0:T(8,128)(2,1)S(1)}, u32[]{:S(2)}, u32[]{:S(2)}) collective-permute-start(bf16[512,768]{1,0:T(8,128)(2,1)S(1)} %bitcast.118), channel_id=1, source_target_pairs={{4,0},{0,4},{5,1},{1,5},{6,2},{2,6},{7,3},{3,7},{12,8},{8,12},{13,... | collective-permute-start | bytes 2359304 | tf_op jit(solution)/shard_map/ppermute | solution.py:65
  30.7 39.6 %collective-permute-start.4 = (bf16[512,768]{1,0:T(8,128)(2,1)S(1)}, bf16[512,768]{1,0:T(8,128)(2,1)S(1)}, u32[]{:S(2)}, u32[]{:S(2)}) collective-permute-start(bf16[512,768]{1,0:T(8,128)(2,1)S(1)} %bitcast.119), channel_id=1, source_target_pairs={{16,0},{0,16},{17,1},{1,17},{18,2},{2,18},{19,3},{3,19},{20,4},{4,... | collective-permute-start | bytes 2359304 | tf_op jit(solution)/shard_map/ppermute | solution.py:52
  33.5 35.2 %collective-permute-start.7 = (bf16[128,2048]{1,0:T(8,128)(2,1)S(1)}, bf16[128,2048]{1,0:T(8,128)(2,1)}, u32[]{:S(2)}, u32[]{:S(2)}) collective-permute-start(bf16[128,2048]{1,0:T(8,128)(2,1)S(1)} %get-tuple-element.180.refs_0_.x_ref.base_ref), channel_id=1, source_target_pairs={{0,2},{2,0},{1,3},{3,1},{4,6},{6,4},{5,7},{7,5},{8,10},{10,8},{9,1... | collective-permute-start | bytes 1572872 | tf_op jit(solution)/shard_map/ppermute | solution.py:88
  35.3 34.1 %collective-permute-start.8 = (bf16[128,2048]{1,0:T(8,128)(2,1)S(1)}, bf16[128,2048]{1,0:T(8,128)(2,1)}, u32[]{:S(2)}, u32[]{:S(2)}) collective-permute-start(bf16[128,2048]{1,0:T(8,128)(2,1)S(1)} %get-tuple-element.180.refs_0_.x_ref.base_ref), channel_id=1, source_target_pairs={{0,8},{8,0},{1,9},{9,1},{2,10},{10,2},{3,11},{11,3},{4,12},{12,4},... | collective-permute-start | bytes 1572872 | tf_op jit(solution)/shard_map/ppermute | solution.py:92
  74.5 56.4 %collective-permute-start.14 = (bf16[512,768]{1,0:T(8,128)(2,1)}, bf16[512,768]{1,0:T(8,128)(2,1)}, u32[]{:S(2)}, u32[]{:S(2)}) collective-permute-start(bf16[512,768]{1,0:T(8,128)(2,1)} %bitcast.13.refs_0_.refs_3_.refs_4_), channel_id=1, source_target_pairs={{16,0},{0,16},{17,1},{1,17},{18,2},{2,18},{19,3},{3,19},{20,4},{4,... | collective-permute-start | bytes 2359304 | tf_op jit(solution)/shard_map/ppermute | solution.py:52
  76.9 53.9 %collective-permute-start.12 = (bf16[128,2048]{1,0:T(8,128)(2,1)}, bf16[128,2048]{1,0:T(8,128)(2,1)}, u32[]{:S(2)}, u32[]{:S(2)}) collective-permute-start(bf16[128,2048]{1,0:T(8,128)(2,1)} %get-tuple-element.209.refs_0_.passed_ref), channel_id=1, source_target_pairs={{0,8},{8,0},{1,9},{9,1},{2,10},{10,2},{3,11},{11,3},{4,12},{12,4},... | collective-permute-start | bytes 1572872 | tf_op jit(solution)/shard_map/ppermute | solution.py:92
  137.5 46.1 %all-to-all-start.3 = ((bf16[4,128,2048]{2,1,0:T(8,128)(2,1)}), bf16[4,128,2048]{2,1,0:T(8,128)(2,1)S(1)}, u32[]{:S(2)}, u32[]{:S(2)}) async-start(bf16[4,128,2048]{2,1,0:T(8,128)(2,1)} %bitcast.116), calls=%async_computation.3 | async-start | bytes 4194304 | tf_op jit(solution)/shard_map/all_to_all | solution.py:76
  141.3 47.9 %collective-permute-start.16 = (bf16[512,768]{1,0:T(8,128)(2,1)}, bf16[512,768]{1,0:T(8,128)(2,1)}, u32[]{:S(2)}, u32[]{:S(2)}) collective-permute-start(bf16[512,768]{1,0:T(8,128)(2,1)} %collective-permute-done.14.refs_1_.refs_4_.refs_5_), channel_id=1, source_target_pairs={{4,0},{0,4},{5,1},{1,5},{6,2},{2,6},{7,3},{3,7},{12,8},{8,12},{13,... | collective-permute-start | bytes 2359304 | tf_op jit(solution)/shard_map/ppermute | solution.py:65
  141.7 47.5 %collective-permute-start.17 = (bf16[512,768]{1,0:T(8,128)(2,1)}, bf16[512,768]{1,0:T(8,128)(2,1)}, u32[]{:S(2)}, u32[]{:S(2)}) collective-permute-start(bf16[512,768]{1,0:T(8,128)(2,1)} %get-tuple-element.224.refs_4_.refs_7_.refs_8_), channel_id=1, source_target_pairs={{4,0},{0,4},{5,1},{1,5},{6,2},{2,6},{7,3},{3,7},{12,8},{8,12},{13,... | collective-permute-start | bytes 2359304 | tf_op jit(solution)/shard_map/ppermute | solution.py:65
  143.3 45.9 %collective-permute-start.18 = (bf16[512,768]{1,0:T(8,128)(2,1)}, bf16[512,768]{1,0:T(8,128)(2,1)}, u32[]{:S(2)}, u32[]{:S(2)}) collective-permute-start(bf16[512,768]{1,0:T(8,128)(2,1)} %get-tuple-element.224.refs_4_.refs_7_.refs_8_), channel_id=1, source_target_pairs={{16,0},{0,16},{17,1},{1,17},{18,2},{2,18},{19,3},{3,19},{20,4},{4,... | collective-permute-start | bytes 2359304 | tf_op jit(solution)/shard_map/ppermute | solution.py:52
  143.8 42.8 %collective-permute-start.19 = (bf16[128,2048]{1,0:T(8,128)(2,1)}, bf16[128,2048]{1,0:T(8,128)(2,1)}, u32[]{:S(2)}, u32[]{:S(2)}) collective-permute-start(bf16[128,2048]{1,0:T(8,128)(2,1)} %get-tuple-element.209.refs_0_.passed_ref), channel_id=1, source_target_pairs={{0,2},{2,0},{1,3},{3,1},{4,6},{6,4},{5,7},{7,5},{8,10},{10,8},{9,1... | collective-permute-start | bytes 1572872 | tf_op jit(solution)/shard_map/ppermute | solution.py:88
  145.8 43.4 %collective-permute-start.20 = (bf16[128,2048]{1,0:T(8,128)(2,1)}, bf16[128,2048]{1,0:T(8,128)(2,1)}, u32[]{:S(2)}, u32[]{:S(2)}) collective-permute-start(bf16[128,2048]{1,0:T(8,128)(2,1)} %collective-permute-done.12.refs_2_), channel_id=1, source_target_pairs={{0,2},{2,0},{1,3},{3,1},{4,6},{6,4},{5,7},{7,5},{8,10},{10,8},{9,1... | collective-permute-start | bytes 1572872 | tf_op jit(solution)/shard_map/ppermute | solution.py:88
  189.2 45.9 %all-to-all-start.4 = ((bf16[4,128,2048]{2,1,0:T(8,128)(2,1)}), bf16[4,128,2048]{2,1,0:T(8,128)(2,1)S(1)}, u32[]{:S(2)}, u32[]{:S(2)}) async-start(bf16[4,128,2048]{2,1,0:T(8,128)(2,1)} %copy-done.19), calls=%async_computation.4 | async-start | bytes 4194304 | tf_op jit(solution)/shard_map/all_to_all | solution.py:76
  195.0 38.9 %collective-permute-start.21 = (bf16[512,2048]{1,0:T(8,128)(2,1)S(1)}, bf16[512,2048]{1,0:T(8,128)(2,1)}, u32[]{:S(2)}, u32[]{:S(2)}) collective-permute-start(bf16[512,2048]{1,0:T(8,128)(2,1)S(1)} %bitcast.105), channel_id=1, source_target_pairs={{0,1},{1,0},{2,3},{3,2},{4,5},{5,4},{6,7},{7,6},{8,9},{9,8},{10,11... | collective-permute-start | bytes 6291464 | tf_op jit(solution)/shard_map/ppermute | solution.py:84
  195.5 36.6 %collective-permute-start.23 = (bf16[512,768]{1,0:T(8,128)(2,1)S(1)}, bf16[512,768]{1,0:T(8,128)(2,1)S(1)}, u32[]{:S(2)}, u32[]{:S(2)}) collective-permute-start(bf16[512,768]{1,0:T(8,128)(2,1)S(1)} %copy-done.36), channel_id=1, source_target_pairs={{4,0},{0,4},{5,1},{1,5},{6,2},{2,6},{7,3},{3,7},{12,8},{8,12},{13,... | collective-permute-start | bytes 2359304 | tf_op jit(solution)/shard_map/ppermute | solution.py:65
  197.2 35.3 %collective-permute-start.24 = (bf16[512,768]{1,0:T(8,128)(2,1)S(1)}, bf16[512,768]{1,0:T(8,128)(2,1)S(1)}, u32[]{:S(2)}, u32[]{:S(2)}) collective-permute-start(bf16[512,768]{1,0:T(8,128)(2,1)S(1)} %copy-done.36), channel_id=1, source_target_pairs={{16,0},{0,16},{17,1},{1,17},{18,2},{2,18},{19,3},{3,19},{20,4},{4,... | collective-permute-start | bytes 2359304 | tf_op jit(solution)/shard_map/ppermute | solution.py:52
  275.5 37.0 %collective-permute-start.28 = (bf16[1024,768]{1,0:T(8,128)(2,1)}, bf16[1024,768]{1,0:T(8,128)(2,1)}, u32[]{:S(2)}, u32[]{:S(2)}) collective-permute-start(bf16[1024,768]{1,0:T(8,128)(2,1)} %shard_map.197), channel_id=1, source_target_pairs={{0,4},{4,0},{1,5},{5,1},{2,6},{6,2},{3,7},{7,3},{8,12},{12,8},{9,1... | collective-permute-start | bytes 4718600 | tf_op jit(solution)/shard_map/ppermute | solution.py:69
  286.6 32.7 %all-to-all-start.5 = ((bf16[4,128,2048]{2,1,0:T(8,128)(2,1)}), bf16[4,128,2048]{2,1,0:T(8,128)(2,1)}, u32[]{:S(2)}, u32[]{:S(2)}) async-start(bf16[4,128,2048]{2,1,0:T(8,128)(2,1)} %bitcast.117), calls=%async_computation.5 | async-start | bytes 4194304 | tf_op jit(solution)/shard_map/all_to_all | solution.py:76
  324.3 36.2 %collective-permute-start.29 = (bf16[1024,768]{1,0:T(8,128)(2,1)}, bf16[1024,768]{1,0:T(8,128)(2,1)}, u32[]{:S(2)}, u32[]{:S(2)}) collective-permute-start(bf16[1024,768]{1,0:T(8,128)(2,1)} %shard_map.202), channel_id=1, source_target_pairs={{0,4},{4,0},{1,5},{5,1},{2,6},{6,2},{3,7},{7,3},{8,12},{12,8},{9,1... | collective-permute-start | bytes 4718600 | tf_op jit(solution)/shard_map/ppermute | solution.py:69
  324.7 42.7 %collective-permute-start.30 = (bf16[512,768]{1,0:T(8,128)(2,1)}, bf16[512,768]{1,0:T(8,128)(2,1)}, u32[]{:S(2)}, u32[]{:S(2)}) collective-permute-start(bf16[512,768]{1,0:T(8,128)(2,1)} %get-tuple-element.260), channel_id=1, source_target_pairs={{0,16},{16,0},{1,17},{17,1},{2,18},{18,2},{3,19},{19,3},{4,20},{20... | collective-permute-start | bytes 2359304 | tf_op jit(solution)/shard_map/ppermute | solution.py:72
  326.4 44.4 %all-to-all-start.6 = ((bf16[4,128,2048]{2,1,0:T(8,128)(2,1)}), bf16[4,128,2048]{2,1,0:T(8,128)(2,1)}, u32[]{:S(2)}, u32[]{:S(2)}) async-start(bf16[4,128,2048]{2,1,0:T(8,128)(2,1)} %copy-done.20), calls=%async_computation.6 | async-start | bytes 4194304 | tf_op jit(solution)/shard_map/all_to_all | solution.py:76
  370.8 37.8 %collective-permute-start.33 = (bf16[1024,768]{1,0:T(8,128)(2,1)}, bf16[1024,768]{1,0:T(8,128)(2,1)}, u32[]{:S(2)}, u32[]{:S(2)}) collective-permute-start(bf16[1024,768]{1,0:T(8,128)(2,1)} %copy-done.67), channel_id=1, source_target_pairs={{0,4},{4,0},{1,5},{5,1},{2,6},{6,2},{3,7},{7,3},{8,12},{12,8},{9,1... | collective-permute-start | bytes 4718600 | tf_op jit(solution)/shard_map/ppermute | solution.py:69
  373.2 42.5 %collective-permute-start.34 = (bf16[512,768]{1,0:T(8,128)(2,1)}, bf16[512,768]{1,0:T(8,128)(2,1)}, u32[]{:S(2)}, u32[]{:S(2)}) collective-permute-start(bf16[512,768]{1,0:T(8,128)(2,1)} %copy-done.102), channel_id=1, source_target_pairs={{0,16},{16,0},{1,17},{17,1},{2,18},{18,2},{3,19},{19,3},{4,20},{20... | collective-permute-start | bytes 2359304 | tf_op jit(solution)/shard_map/ppermute | solution.py:72
  427.7 47.3 %all-to-all-start.7 = ((bf16[8,64,1536]{2,1,0:T(8,128)(2,1)}), bf16[8,64,1536]{2,1,0:T(8,128)(2,1)}, u32[]{:S(2)}, u32[]{:S(2)}) async-start(bf16[8,64,1536]{2,1,0:T(8,128)(2,1)} %pad_maximum_fusion), calls=%async_computation.7 | async-start | bytes 3145728 | tf_op jit(solution)/shard_map/all_to_all | solution.py:96
  432.0 37.0 %collective-permute-start.37 = (bf16[1024,768]{1,0:T(8,128)(2,1)}, bf16[1024,768]{1,0:T(8,128)(2,1)}, u32[]{:S(2)}, u32[]{:S(2)}) collective-permute-start(bf16[1024,768]{1,0:T(8,128)(2,1)} %copy-done.66), channel_id=1, source_target_pairs={{0,4},{4,0},{1,5},{5,1},{2,6},{6,2},{3,7},{7,3},{8,12},{12,8},{9,1... | collective-permute-start | bytes 4718600 | tf_op jit(solution)/shard_map/ppermute | solution.py:69
  433.8 41.2 %collective-permute-start.38 = (bf16[512,768]{1,0:T(8,128)(2,1)}, bf16[512,768]{1,0:T(8,128)(2,1)}, u32[]{:S(2)}, u32[]{:S(2)}) collective-permute-start(bf16[512,768]{1,0:T(8,128)(2,1)} %copy-done.101), channel_id=1, source_target_pairs={{0,16},{16,0},{1,17},{17,1},{2,18},{18,2},{3,19},{19,3},{4,20},{20... | collective-permute-start | bytes 2359304 | tf_op jit(solution)/shard_map/ppermute | solution.py:72
  477.2 57.6 %all-to-all-start.8 = ((bf16[8,64,768]{2,1,0:T(8,128)(2,1)}), bf16[8,64,768]{2,1,0:T(8,128)(2,1)}, u32[]{:S(2)}, u32[]{:S(2)}) async-start(bf16[8,64,768]{2,1,0:T(8,128)(2,1)} %bitcast.144), calls=%async_computation.8 | async-start | bytes 1572864 | tf_op jit(solution)/shard_map/all_to_all | solution.py:96
  483.0 37.7 %collective-permute-start.44 = (bf16[128,2048]{1,0:T(8,128)(2,1)S(1)}, bf16[128,2048]{1,0:T(8,128)(2,1)S(1)}, u32[]{:S(2)}, u32[]{:S(2)}) collective-permute-start(bf16[128,2048]{1,0:T(8,128)(2,1)S(1)} %get-tuple-element.318), channel_id=1, source_target_pairs={{0,2},{2,0},{1,3},{3,1},{4,6},{6,4},{5,7},{7,5},{8,10},{10,8},{9,1... | collective-permute-start | bytes 1572872 | tf_op jit(solution)/shard_map/ppermute | solution.py:88
  485.0 35.8 %collective-permute-start.45 = (bf16[128,2048]{1,0:T(8,128)(2,1)S(1)}, bf16[128,2048]{1,0:T(8,128)(2,1)S(1)}, u32[]{:S(2)}, u32[]{:S(2)}) collective-permute-start(bf16[128,2048]{1,0:T(8,128)(2,1)S(1)} %copy-done.49), channel_id=1, source_target_pairs={{0,8},{8,0},{1,9},{9,1},{2,10},{10,2},{3,11},{11,3},{4,12},{12,4},... | collective-permute-start | bytes 1572872 | tf_op jit(solution)/shard_map/ppermute | solution.py:92
  487.0 47.8 %collective-permute-start.42 = (bf16[512,768]{1,0:T(8,128)(2,1)}, bf16[512,768]{1,0:T(8,128)(2,1)}, u32[]{:S(2)}, u32[]{:S(2)}) collective-permute-start(bf16[512,768]{1,0:T(8,128)(2,1)} %copy-done.100), channel_id=1, source_target_pairs={{0,16},{16,0},{1,17},{17,1},{2,18},{18,2},{3,19},{19,3},{4,20},{20... | collective-permute-start | bytes 2359304 | tf_op jit(solution)/shard_map/ppermute | solution.py:72
  488.3 44.2 %collective-permute-start.47 = (bf16[128,2048]{1,0:T(8,128)(2,1)S(1)}, bf16[128,2048]{1,0:T(8,128)(2,1)S(1)}, u32[]{:S(2)}, u32[]{:S(2)}) collective-permute-start(bf16[128,2048]{1,0:T(8,128)(2,1)S(1)} %shard_map.218), channel_id=1, source_target_pairs={{0,8},{8,0},{1,9},{9,1},{2,10},{10,2},{3,11},{11,3},{4,12},{12,4},... | collective-permute-start | bytes 1572872 | tf_op jit(solution)/shard_map/ppermute | solution.py:92
  (172 other events, 1532.9 us)

commit v6 on v5

--- a/solution.py
+++ b/solution.py
@@ -23,7 +23,7 @@
 VMEM_LIMIT = 32 << 20
 WEIGHT = 100
 FORWARD_STEPS = 4
-BACK_STEPS = 2
+BACK_STEPS = 1
 
 
 def hold(*values):
@@ -988,7 +988,7 @@
     out_total = back_rows(0, out_pairs, received, corner)
     out_both = other_x(out_total[3])
     sums[3] = own_terms(arriving[3], *attention)
-    head_gains = all_sum(head_gains, sizes, ("xl",))
+    head_gains = all_sum(head_gains, sizes, ("xl", "zl"))
     in_z = plain_sum(terms[2], in_both)
     back_first = [far_total(sums[j][0], arrived_far[j]) for j in range(CHUNKS - 1)]
     back_first = exchange(jnp.concatenate(back_first, axis=2))
@@ -1003,13 +1003,13 @@
     terms = jnp.stack([terms[0], other_x(terms[1]), other_z(in_z)])
     (token_grad,) = norm_back_step(terms, x_own, d_middle, g_attn, 1)
     token_grad, output = reorder([token_grad, output], places, True)
-    head_gains = all_sum(head_gains, sizes, ("zl",))
+    head_gains = all_sum(head_gains, sizes, ("y",))
     back, arrived_far[3], head_gains, token_grad, output = hold(
         back, arrived_far[3], head_gains, token_grad, output
     )
 
     last = exchange(far_total(sums[3][0], arrived_far[3]))
-    head_gains = all_sum(head_gains, sizes, ("y", "xh", "zh"))
+    head_gains = all_sum(head_gains, sizes, ("xh", "zh"))
     grad_gate_up, grad_down, grad_mlp_gain = unpack_chunks(
         back_first, back, w_gate_up_rows, mlp_gain.astype(F32).reshape(owned, 1), chunk
     )

time: 566 us -> 563 us (level)
    ppermute x10, waiting for transfers between devices: 63.1 us -> 32.9 us  [all_sum(): lax.ppermute(value, axis, [((i + k) % sizes[axis], i) for i in range(size...]
    ppermute x4, waiting for transfers between devices: 10.5 us -> 26.5 us  [other_z(): return lax.ppermute(value, 'zl', SWAP)]
    ppermute x8, waiting for transfers between devices: 18.2 us -> 31.7 us  [other_x(): return lax.ppermute(value, 'xl', SWAP)]
  transfers between devices with their start and end apart: 60 -> 60, of which waited for: 27 -> 28; matrix products, arithmetic and copies ran while one was open for 4% -> 4% of each run, Pallas kernels for 19% -> 19%
where the time goes in v6:
time: 563 us; the launch traced here: 554 us
  waiting for transfers between devices  244 us (43%)
  Pallas kernels  133 us (24%)
  starting transfers between devices  90.9 us (16%)
  local copies, waits for them, and re-layouts  68.7 us (12%)
  other arithmetic  14.8 us (3%)
    pallas_call x35, Pallas kernels, run(): pl.pallas_call(kernel, grid=grid, in_specs=in_specs, out_specs=out_specs,...  130 us
    unnamed x291, local copies, waits for them, and re-layouts  58.6 us
    ppermute x4, waiting for transfers between devices, to_near(): return lax.ppermute(value, ('y', 'xh'), self.shifted(n))  52 us
    all_to_all x4, waiting for transfers between devices, among_four(): return lax.all_to_all(value, ('zl', 'xl'), 0, 0, tiled=True)  42.2 us
    ppermute x8, waiting for transfers between devices, near_blocks(): lax.ppermute(block, ('y', 'xh'), [(b, a) for a, b in self.shifted(n)])  37.7 us
    ppermute x10, waiting for transfers between devices, all_sum(): lax.ppermute(value, axis, [((i + k) % sizes[axis], i) for i in range(size...  32.9 us
    ppermute x8, waiting for transfers between devices, other_x(): return lax.ppermute(value, 'xl', SWAP)  31.7 us
    all_to_all x6, starting transfers between devices, exchange(): return lax.all_to_all(value, TEAM, 0, 0, tiled=True)  27.2 us
  transfers between devices with their start and end apart: 60, of which 28 were waited for; matrix products, arithmetic and copies ran while one was open for 4% of the time, Pallas kernels for 19%

profile of v6, /device:TPU:0, one launch (start us, length us, event | category | flops | bytes accessed | tf_op | source)
XLA Modules:
  0.0 553.9 jit_solution(2362479895202238004)
XLA Ops:
  2.9 5.2 all-to-all-start
  37.4 12.1 %collective-permute-done.5 = bf16[32,264]{1,0:T(8,128)(2,1)S(1)} collective-permute-done((bf16[32,264]{1,0:T(8,128)(2,1)S(1)}, bf16[32,264]{1,0:T(8,128)(2,1)S(1)}, u32[]{:S(2)}, u32[]{:S(2)}) %collective-permute-start.5) | collective-permute-done | bytes 16928 | tf_op jit(solution)/shard_map/ppermute | solution.py:103
  52.1 16.5 %collective-permute-done.6 = bf16[32,264]{1,0:T(8,128)(2,1)S(1)} collective-permute-done((bf16[32,264]{1,0:T(8,128)(2,1)S(1)}, bf16[32,264]{1,0:T(8,128)(2,1)S(1)}, u32[]{:S(2)}, u32[]{:S(2)}) %collective-permute-start.6) | collective-permute-done | bytes 16928 | tf_op jit(solution)/shard_map/ppermute | solution.py:103
  77.7 8.7 %collective-permute-done.10.refs_3_ = bf16[128,2048]{1,0:T(8,128)(2,1)} collective-permute-done((bf16[128,2048]{1,0:T(8,128)(2,1)}, bf16[128,2048]{1,0:T(8,128)(2,1)}, u32[]{:S(2)}, u32[]{:S(2)}) %collective-permute-start.10) | collective-permute-done | bytes 524320 | tf_op jit(solution)/shard_map/ppermute | solution.py:88
  97.2 5.1 all-to-all-start.2
  108.4 6.7 %shard_map.190 = (bf16[1024,2048]{1,0:T(8,128)(2,1)S(1)}, f32[1024,384]{1,0:T(8,128)S(1)}, bf16[1024,512]{1,0:T(8,128)(2,1)S(1)}) custom-call(bf16[512,2048]{1,0:T(8,128)(2,1)S(1)} %bitcast.115, bf16[512,2048]{1,0:T(8,128)(2,1)} %collective-permute-done.11.x1, bf16[512,768]{1,0:T(8,128)(2,1)S(1)} %bitcast.120, bf16[512,768]{1,0:T(8,128)(2,1)S(1)} %copy-done.77, ...), custom_call_target="tpu_custom_call" | custom-call | flops 214748364800 | bytes 1521356800 | tf_op jit(solution)/shard_map/pallas_call | solution.py:144
  122.0 6.0 %all-to-all-done.2 = bf16[8,64,1536]{2,1,0:T(8,128)(2,1)} async-done(((bf16[8,64,1536]{2,1,0:T(8,128)(2,1)}), bf16[8,64,1536]{2,1,0:T(8,128)(2,1)}, u32[]{:S(2)}, u32[]{:S(2)}) %all-to-all-start.2) | async-done | bytes 1572896 | tf_op jit(solution)/shard_map/all_to_all | solution.py:96
  145.5 37.7 %all-to-all-done.3.parts_ref = bf16[4,128,2048]{2,1,0:T(8,128)(2,1)S(1)} async-done(((bf16[4,128,2048]{2,1,0:T(8,128)(2,1)}), bf16[4,128,2048]{2,1,0:T(8,128)(2,1)S(1)}, u32[]{:S(2)}, u32[]{:S(2)}) %all-to-all-start.3) | async-done | bytes 2097184 | tf_op jit(solution)/shard_map/all_to_all | solution.py:76
  196.9 18.3 %collective-permute-done.22.refs_7_.refs_10_.refs_11_ = bf16[512,768]{1,0:T(8,128)(2,1)S(1)} collective-permute-done((bf16[512,768]{1,0:T(8,128)(2,1)}, bf16[512,768]{1,0:T(8,128)(2,1)S(1)}, u32[]{:S(2)}, u32[]{:S(2)}) %collective-permute-start.22) | collective-permute-done | bytes 786464 | tf_op jit(solution)/shard_map/ppermute | solution.py:65
  215.1 16.4 %collective-permute-done.23.refs_2_.refs_13_.refs_14_ = bf16[512,768]{1,0:T(8,128)(2,1)S(1)} collective-permute-done((bf16[512,768]{1,0:T(8,128)(2,1)S(1)}, bf16[512,768]{1,0:T(8,128)(2,1)S(1)}, u32[]{:S(2)}, u32[]{:S(2)}) %collective-permute-start.23) | collective-permute-done | bytes 786464 | tf_op jit(solution)/shard_map/ppermute | solution.py:65
  240.1 11.7 %shard_map.196 = (bf16[1024,256]{1,0:T(8,128)(2,1)S(1)}, bf16[1024,512]{1,0:T(8,128)(2,1)S(1)}, bf16[1024,256]{1,0:T(8,128)(2,1)S(1)}, bf16[1024,512]{1,0:T(8,128)(2,1)S(1)}) custom-call(bf16[512,2048]{1,0:T(8,128)(2,1)} %bitcast.97, bf16[512,2048]{1,0:T(8,128)(2,1)} %copy-done.61, bf16[512,2048]{1,0:T(8,128)(2,1)} %bitcast.106, ...), custom_call_target="tpu_custom_call" | custom-call | flops 644245094400 | bytes 1782579200 | tf_op jit(solution)/shard_map/pallas_call | solution.py:144
  260.4 8.1 %shard_map.198 = (bf16[1024,256]{1,0:T(8,128)(2,1)S(1)}, bf16[1024,512]{1,0:T(8,128)(2,1)S(1)}) custom-call(bf16[512,2048]{1,0:T(8,128)(2,1)} %bitcast.98, bf16[512,2048]{1,0:T(8,128)(2,1)} %copy-done.61, bf16[512,2048]{1,0:T(8,128)(2,1)} %bitcast.107, bf16[512,2048]{1,0:T(8,128)(2,1)} %collective-permute-done.21.dy1.refs_3_, ...), custom_call_target="tpu_custom_call" | custom-call | flops 322122547200 | bytes 1310720000 | tf_op jit(solution)/shard_map/pallas_call | solution.py:144
  268.6 5.9 %shard_map.199 = bf16[512,2048]{1,0:T(8,128)(2,1)S(1)} custom-call(bf16[1024,512]{1,0:T(8,128)(2,1)S(1)} %copy-done.120, bf16[1024,512]{1,0:T(8,128)(2,1)S(1)} %get-tuple-element.255.refs_1_.refs_4_, bf16[1024,512]{1,0:T(8,128)(2,1)S(1)} %get-tuple-element.261.refs_2_.refs_4_, bf16[512,768]{1,0:T(8,128)(2,1)} %bitcast.13.refs_0_.refs_3_.refs_4_, ...), custom_call_target="tpu_custom_call" | custom-call | flops 322122547200 | bytes 1468006400 | tf_op jit(solution)/shard_map/pallas_call | solution.py:144
  278.8 5.5 shard_map.200
  285.6 5.0 all-to-all-start.5
  300.3 11.4 %collective-permute-done.28.refs_6_ = bf16[1024,768]{1,0:T(8,128)(2,1)} collective-permute-done((bf16[1024,768]{1,0:T(8,128)(2,1)}, bf16[1024,768]{1,0:T(8,128)(2,1)}, u32[]{:S(2)}, u32[]{:S(2)}) %collective-permute-start.28) | collective-permute-done | bytes 1572896 | tf_op jit(solution)/shard_map/ppermute | solution.py:69
  311.7 6.0 %shard_map.203 = (bf16[512,768]{1,0:T(8,128)(2,1)S(1)}, bf16[512,768]{1,0:T(8,128)(2,1)}) custom-call(bf16[512,2048]{1,0:T(8,128)(2,1)S(1)} %bitcast.101, bf16[512,2048]{1,0:T(8,128)(2,1)S(1)} %copy-done.63, bf16[512,2048]{1,0:T(8,128)(2,1)S(1)} %bitcast.110, bf16[512,2048]{1,0:T(8,128)(2,1)} %collective-permute-done.21.dy1.refs_3_, ...), custom_call_target="tpu_custom_call" | custom-call | flops 161061273600 | bytes 1310720000 | tf_op jit(solution)/shard_map/pallas_call | solution.py:144
  325.5 4.5 all-to-all-start.6
  340.4 19.3 %collective-permute-done.29.refs_6_ = bf16[1024,768]{1,0:T(8,128)(2,1)} collective-permute-done((bf16[1024,768]{1,0:T(8,128)(2,1)}, bf16[1024,768]{1,0:T(8,128)(2,1)}, u32[]{:S(2)}, u32[]{:S(2)}) %collective-permute-start.29) | collective-permute-done | bytes 1572896 | tf_op jit(solution)/shard_map/ppermute | solution.py:69
  359.7 5.1 shard_map.204
  381.6 5.5 shard_map.207
  407.7 5.3 shard_map.211
  414.9 4.7 shard_map.215
  426.8 4.7 all-to-all-start.7
  433.9 6.2 %collective-permute-done.36.refs_1_ = bf16[128,2048]{1,0:T(8,128)(2,1)S(1)} collective-permute-done((bf16[128,2048]{1,0:T(8,128)(2,1)}, bf16[128,2048]{1,0:T(8,128)(2,1)S(1)}, u32[]{:S(2)}, u32[]{:S(2)}) %collective-permute-start.36) | collective-permute-done | bytes 524320 | tf_op jit(solution)/shard_map/ppermute | solution.py:88
  451.6 17.1 %collective-permute-done.37.refs_5_ = bf16[1024,768]{1,0:T(8,128)(2,1)} collective-permute-done((bf16[1024,768]{1,0:T(8,128)(2,1)}, bf16[1024,768]{1,0:T(8,128)(2,1)}, u32[]{:S(2)}, u32[]{:S(2)}) %collective-permute-start.37) | collective-permute-done | bytes 1572896 | tf_op jit(solution)/shard_map/ppermute | solution.py:69
  468.7 5.0 shard_map.214
  476.8 4.3 all-to-all-start.8
  490.3 14.1 %collective-permute-done.45 = bf16[128,2048]{1,0:T(8,128)(2,1)S(1)} collective-permute-done((bf16[128,2048]{1,0:T(8,128)(2,1)S(1)}, bf16[128,2048]{1,0:T(8,128)(2,1)S(1)}, u32[]{:S(2)}, u32[]{:S(2)}) %collective-permute-start.45) | collective-permute-done | bytes 524320 | tf_op jit(solution)/shard_map/ppermute | solution.py:88
  504.3 13.3 %collective-permute-done.46 = bf16[128,2048]{1,0:T(8,128)(2,1)S(1)} collective-permute-done((bf16[128,2048]{1,0:T(8,128)(2,1)S(1)}, bf16[128,2048]{1,0:T(8,128)(2,1)S(1)}, u32[]{:S(2)}, u32[]{:S(2)}) %collective-permute-start.46) | collective-permute-done | bytes 524320 | tf_op jit(solution)/shard_map/ppermute | solution.py:92
  519.7 12.4 %collective-permute-done.48.refs_3_ = bf16[128,2048]{1,0:T(8,128)(2,1)S(1)} collective-permute-done((bf16[128,2048]{1,0:T(8,128)(2,1)S(1)}, bf16[128,2048]{1,0:T(8,128)(2,1)S(1)}, u32[]{:S(2)}, u32[]{:S(2)}) %collective-permute-start.48) | collective-permute-done | bytes 524320 | tf_op jit(solution)/shard_map/ppermute | solution.py:92
  541.0 8.1 %shard_map.222 = (f32[64,2,6144]{2,1,0:T(2,128)}, f32[64,6144]{1,0:T(8,128)}, f32[64,1]{1,0:T(8,128)S(1)}) custom-call(bf16[8,64,1536]{2,1,0:T(8,128)(2,1)} %all-to-all-done.7.first_ref, bf16[8,64,768]{2,1,0:T(8,128)(2,1)} %all-to-all-done.8.rest_ref, bf16[64,2,6144]{2,1,0:T(2,128)(2,1)} %w_ref.5, f32[64,1]{1,0:T(8,128)S(1)} %copy.38.gain_ref), custom_call_target="tpu_custom_call" | custom-call | bytes 865126400 | tf_op jit(solution)/shard_map/pallas_call | solution.py:144
  (487 shorter events, 235.4 us)
Async XLA Ops:
  24.9 45.4 %all-to-all-start.1 = ((bf16[8,64,768]{2,1,0:T(8,128)(2,1)}), bf16[8,64,768]{2,1,0:T(8,128)(2,1)}, u32[]{:S(2)}, u32[]{:S(2)}) async-start(bf16[8,64,768]{2,1,0:T(8,128)(2,1)} %get-tuple-element.169), calls=%async_computation.1 | async-start | bytes 1572864 | tf_op jit(solution)/shard_map/all_to_all | solution.py:96
  29.1 40.3 %collective-permute-start.3 = (bf16[512,768]{1,0:T(8,128)(2,1)S(1)}, bf16[512,768]{1,0:T(8,128)(2,1)S(1)}, u32[]{:S(2)}, u32[]{:S(2)}) collective-permute-start(bf16[512,768]{1,0:T(8,128)(2,1)S(1)} %bitcast.118), channel_id=1, source_target_pairs={{4,0},{0,4},{5,1},{1,5},{6,2},{2,6},{7,3},{3,7},{12,8},{8,12},{13,... | collective-permute-start | bytes 2359304 | tf_op jit(solution)/shard_map/ppermute | solution.py:65
  30.7 39.6 %collective-permute-start.4 = (bf16[512,768]{1,0:T(8,128)(2,1)S(1)}, bf16[512,768]{1,0:T(8,128)(2,1)S(1)}, u32[]{:S(2)}, u32[]{:S(2)}) collective-permute-start(bf16[512,768]{1,0:T(8,128)(2,1)S(1)} %bitcast.119), channel_id=1, source_target_pairs={{16,0},{0,16},{17,1},{1,17},{18,2},{2,18},{19,3},{3,19},{20,4},{4,... | collective-permute-start | bytes 2359304 | tf_op jit(solution)/shard_map/ppermute | solution.py:52
  33.5 35.2 %collective-permute-start.7 = (bf16[128,2048]{1,0:T(8,128)(2,1)S(1)}, bf16[128,2048]{1,0:T(8,128)(2,1)}, u32[]{:S(2)}, u32[]{:S(2)}) collective-permute-start(bf16[128,2048]{1,0:T(8,128)(2,1)S(1)} %get-tuple-element.180.refs_0_.x_ref.base_ref), channel_id=1, source_target_pairs={{0,2},{2,0},{1,3},{3,1},{4,6},{6,4},{5,7},{7,5},{8,10},{10,8},{9,1... | collective-permute-start | bytes 1572872 | tf_op jit(solution)/shard_map/ppermute | solution.py:88
  35.3 34.1 %collective-permute-start.8 = (bf16[128,2048]{1,0:T(8,128)(2,1)S(1)}, bf16[128,2048]{1,0:T(8,128)(2,1)}, u32[]{:S(2)}, u32[]{:S(2)}) collective-permute-start(bf16[128,2048]{1,0:T(8,128)(2,1)S(1)} %get-tuple-element.180.refs_0_.x_ref.base_ref), channel_id=1, source_target_pairs={{0,8},{8,0},{1,9},{9,1},{2,10},{10,2},{3,11},{11,3},{4,12},{12,4},... | collective-permute-start | bytes 1572872 | tf_op jit(solution)/shard_map/ppermute | solution.py:92
  74.5 56.4 %collective-permute-start.14 = (bf16[512,768]{1,0:T(8,128)(2,1)}, bf16[512,768]{1,0:T(8,128)(2,1)}, u32[]{:S(2)}, u32[]{:S(2)}) collective-permute-start(bf16[512,768]{1,0:T(8,128)(2,1)} %bitcast.13.refs_0_.refs_3_.refs_4_), channel_id=1, source_target_pairs={{16,0},{0,16},{17,1},{1,17},{18,2},{2,18},{19,3},{3,19},{20,4},{4,... | collective-permute-start | bytes 2359304 | tf_op jit(solution)/shard_map/ppermute | solution.py:52
  76.9 53.9 %collective-permute-start.12 = (bf16[128,2048]{1,0:T(8,128)(2,1)}, bf16[128,2048]{1,0:T(8,128)(2,1)}, u32[]{:S(2)}, u32[]{:S(2)}) collective-permute-start(bf16[128,2048]{1,0:T(8,128)(2,1)} %get-tuple-element.209.refs_0_.passed_ref), channel_id=1, source_target_pairs={{0,8},{8,0},{1,9},{9,1},{2,10},{10,2},{3,11},{11,3},{4,12},{12,4},... | collective-permute-start | bytes 1572872 | tf_op jit(solution)/shard_map/ppermute | solution.py:92
  137.2 46.1 %all-to-all-start.3 = ((bf16[4,128,2048]{2,1,0:T(8,128)(2,1)}), bf16[4,128,2048]{2,1,0:T(8,128)(2,1)S(1)}, u32[]{:S(2)}, u32[]{:S(2)}) async-start(bf16[4,128,2048]{2,1,0:T(8,128)(2,1)} %bitcast.116), calls=%async_computation.3 | async-start | bytes 4194304 | tf_op jit(solution)/shard_map/all_to_all | solution.py:76
  140.9 47.9 %collective-permute-start.16 = (bf16[512,768]{1,0:T(8,128)(2,1)}, bf16[512,768]{1,0:T(8,128)(2,1)}, u32[]{:S(2)}, u32[]{:S(2)}) collective-permute-start(bf16[512,768]{1,0:T(8,128)(2,1)} %collective-permute-done.14.refs_1_.refs_4_.refs_5_), channel_id=1, source_target_pairs={{4,0},{0,4},{5,1},{1,5},{6,2},{2,6},{7,3},{3,7},{12,8},{8,12},{13,... | collective-permute-start | bytes 2359304 | tf_op jit(solution)/shard_map/ppermute | solution.py:65
  141.3 47.5 %collective-permute-start.17 = (bf16[512,768]{1,0:T(8,128)(2,1)}, bf16[512,768]{1,0:T(8,128)(2,1)}, u32[]{:S(2)}, u32[]{:S(2)}) collective-permute-start(bf16[512,768]{1,0:T(8,128)(2,1)} %get-tuple-element.224.refs_4_.refs_7_.refs_8_), channel_id=1, source_target_pairs={{4,0},{0,4},{5,1},{1,5},{6,2},{2,6},{7,3},{3,7},{12,8},{8,12},{13,... | collective-permute-start | bytes 2359304 | tf_op jit(solution)/shard_map/ppermute | solution.py:65
  143.0 45.9 %collective-permute-start.18 = (bf16[512,768]{1,0:T(8,128)(2,1)}, bf16[512,768]{1,0:T(8,128)(2,1)}, u32[]{:S(2)}, u32[]{:S(2)}) collective-permute-start(bf16[512,768]{1,0:T(8,128)(2,1)} %get-tuple-element.224.refs_4_.refs_7_.refs_8_), channel_id=1, source_target_pairs={{16,0},{0,16},{17,1},{1,17},{18,2},{2,18},{19,3},{3,19},{20,4},{4,... | collective-permute-start | bytes 2359304 | tf_op jit(solution)/shard_map/ppermute | solution.py:52
  143.5 42.8 %collective-permute-start.19 = (bf16[128,2048]{1,0:T(8,128)(2,1)}, bf16[128,2048]{1,0:T(8,128)(2,1)}, u32[]{:S(2)}, u32[]{:S(2)}) collective-permute-start(bf16[128,2048]{1,0:T(8,128)(2,1)} %get-tuple-element.209.refs_0_.passed_ref), channel_id=1, source_target_pairs={{0,2},{2,0},{1,3},{3,1},{4,6},{6,4},{5,7},{7,5},{8,10},{10,8},{9,1... | collective-permute-start | bytes 1572872 | tf_op jit(solution)/shard_map/ppermute | solution.py:88
  145.5 43.4 %collective-permute-start.20 = (bf16[128,2048]{1,0:T(8,128)(2,1)}, bf16[128,2048]{1,0:T(8,128)(2,1)}, u32[]{:S(2)}, u32[]{:S(2)}) collective-permute-start(bf16[128,2048]{1,0:T(8,128)(2,1)} %collective-permute-done.12.refs_2_), channel_id=1, source_target_pairs={{0,2},{2,0},{1,3},{3,1},{4,6},{6,4},{5,7},{7,5},{8,10},{10,8},{9,1... | collective-permute-start | bytes 1572872 | tf_op jit(solution)/shard_map/ppermute | solution.py:88
  188.9 45.7 %all-to-all-start.4 = ((bf16[4,128,2048]{2,1,0:T(8,128)(2,1)}), bf16[4,128,2048]{2,1,0:T(8,128)(2,1)S(1)}, u32[]{:S(2)}, u32[]{:S(2)}) async-start(bf16[4,128,2048]{2,1,0:T(8,128)(2,1)} %copy-done.19), calls=%async_computation.4 | async-start | bytes 4194304 | tf_op jit(solution)/shard_map/all_to_all | solution.py:76
  194.4 38.9 %collective-permute-start.21 = (bf16[512,2048]{1,0:T(8,128)(2,1)S(1)}, bf16[512,2048]{1,0:T(8,128)(2,1)}, u32[]{:S(2)}, u32[]{:S(2)}) collective-permute-start(bf16[512,2048]{1,0:T(8,128)(2,1)S(1)} %bitcast.105), channel_id=1, source_target_pairs={{0,1},{1,0},{2,3},{3,2},{4,5},{5,4},{6,7},{7,6},{8,9},{9,8},{10,11... | collective-permute-start | bytes 6291464 | tf_op jit(solution)/shard_map/ppermute | solution.py:84
  194.9 36.6 %collective-permute-start.23 = (bf16[512,768]{1,0:T(8,128)(2,1)S(1)}, bf16[512,768]{1,0:T(8,128)(2,1)S(1)}, u32[]{:S(2)}, u32[]{:S(2)}) collective-permute-start(bf16[512,768]{1,0:T(8,128)(2,1)S(1)} %copy-done.36), channel_id=1, source_target_pairs={{4,0},{0,4},{5,1},{1,5},{6,2},{2,6},{7,3},{3,7},{12,8},{8,12},{13,... | collective-permute-start | bytes 2359304 | tf_op jit(solution)/shard_map/ppermute | solution.py:65
  196.6 35.3 %collective-permute-start.24 = (bf16[512,768]{1,0:T(8,128)(2,1)S(1)}, bf16[512,768]{1,0:T(8,128)(2,1)S(1)}, u32[]{:S(2)}, u32[]{:S(2)}) collective-permute-start(bf16[512,768]{1,0:T(8,128)(2,1)S(1)} %copy-done.36), channel_id=1, source_target_pairs={{16,0},{0,16},{17,1},{1,17},{18,2},{2,18},{19,3},{3,19},{20,4},{4,... | collective-permute-start | bytes 2359304 | tf_op jit(solution)/shard_map/ppermute | solution.py:52
  274.7 37.0 %collective-permute-start.28 = (bf16[1024,768]{1,0:T(8,128)(2,1)}, bf16[1024,768]{1,0:T(8,128)(2,1)}, u32[]{:S(2)}, u32[]{:S(2)}) collective-permute-start(bf16[1024,768]{1,0:T(8,128)(2,1)} %shard_map.197), channel_id=1, source_target_pairs={{0,4},{4,0},{1,5},{5,1},{2,6},{6,2},{3,7},{7,3},{8,12},{12,8},{9,1... | collective-permute-start | bytes 4718600 | tf_op jit(solution)/shard_map/ppermute | solution.py:69
  285.6 33.0 %all-to-all-start.5 = ((bf16[4,128,2048]{2,1,0:T(8,128)(2,1)}), bf16[4,128,2048]{2,1,0:T(8,128)(2,1)}, u32[]{:S(2)}, u32[]{:S(2)}) async-start(bf16[4,128,2048]{2,1,0:T(8,128)(2,1)} %bitcast.117), calls=%async_computation.5 | async-start | bytes 4194304 | tf_op jit(solution)/shard_map/all_to_all | solution.py:76
  323.5 36.2 %collective-permute-start.29 = (bf16[1024,768]{1,0:T(8,128)(2,1)}, bf16[1024,768]{1,0:T(8,128)(2,1)}, u32[]{:S(2)}, u32[]{:S(2)}) collective-permute-start(bf16[1024,768]{1,0:T(8,128)(2,1)} %shard_map.202), channel_id=1, source_target_pairs={{0,4},{4,0},{1,5},{5,1},{2,6},{6,2},{3,7},{7,3},{8,12},{12,8},{9,1... | collective-permute-start | bytes 4718600 | tf_op jit(solution)/shard_map/ppermute | solution.py:69
  323.8 42.7 %collective-permute-start.30 = (bf16[512,768]{1,0:T(8,128)(2,1)}, bf16[512,768]{1,0:T(8,128)(2,1)}, u32[]{:S(2)}, u32[]{:S(2)}) collective-permute-start(bf16[512,768]{1,0:T(8,128)(2,1)} %get-tuple-element.260), channel_id=1, source_target_pairs={{0,16},{16,0},{1,17},{17,1},{2,18},{18,2},{3,19},{19,3},{4,20},{20... | collective-permute-start | bytes 2359304 | tf_op jit(solution)/shard_map/ppermute | solution.py:72
  325.5 44.2 %all-to-all-start.6 = ((bf16[4,128,2048]{2,1,0:T(8,128)(2,1)}), bf16[4,128,2048]{2,1,0:T(8,128)(2,1)}, u32[]{:S(2)}, u32[]{:S(2)}) async-start(bf16[4,128,2048]{2,1,0:T(8,128)(2,1)} %copy-done.20), calls=%async_computation.6 | async-start | bytes 4194304 | tf_op jit(solution)/shard_map/all_to_all | solution.py:76
  369.8 37.8 %collective-permute-start.33 = (bf16[1024,768]{1,0:T(8,128)(2,1)}, bf16[1024,768]{1,0:T(8,128)(2,1)}, u32[]{:S(2)}, u32[]{:S(2)}) collective-permute-start(bf16[1024,768]{1,0:T(8,128)(2,1)} %copy-done.67), channel_id=1, source_target_pairs={{0,4},{4,0},{1,5},{5,1},{2,6},{6,2},{3,7},{7,3},{8,12},{12,8},{9,1... | collective-permute-start | bytes 4718600 | tf_op jit(solution)/shard_map/ppermute | solution.py:69
  372.2 42.6 %collective-permute-start.34 = (bf16[512,768]{1,0:T(8,128)(2,1)}, bf16[512,768]{1,0:T(8,128)(2,1)}, u32[]{:S(2)}, u32[]{:S(2)}) collective-permute-start(bf16[512,768]{1,0:T(8,128)(2,1)} %copy-done.102), channel_id=1, source_target_pairs={{0,16},{16,0},{1,17},{17,1},{2,18},{18,2},{3,19},{19,3},{4,20},{20... | collective-permute-start | bytes 2359304 | tf_op jit(solution)/shard_map/ppermute | solution.py:72
  426.8 47.8 %all-to-all-start.7 = ((bf16[8,64,1536]{2,1,0:T(8,128)(2,1)}), bf16[8,64,1536]{2,1,0:T(8,128)(2,1)}, u32[]{:S(2)}, u32[]{:S(2)}) async-start(bf16[8,64,1536]{2,1,0:T(8,128)(2,1)} %pad_maximum_fusion), calls=%async_computation.7 | async-start | bytes 3145728 | tf_op jit(solution)/shard_map/all_to_all | solution.py:96
  431.5 37.1 %collective-permute-start.37 = (bf16[1024,768]{1,0:T(8,128)(2,1)}, bf16[1024,768]{1,0:T(8,128)(2,1)}, u32[]{:S(2)}, u32[]{:S(2)}) collective-permute-start(bf16[1024,768]{1,0:T(8,128)(2,1)} %copy-done.66), channel_id=1, source_target_pairs={{0,4},{4,0},{1,5},{5,1},{2,6},{6,2},{3,7},{7,3},{8,12},{12,8},{9,1... | collective-permute-start | bytes 4718600 | tf_op jit(solution)/shard_map/ppermute | solution.py:69
  433.3 41.3 %collective-permute-start.38 = (bf16[512,768]{1,0:T(8,128)(2,1)}, bf16[512,768]{1,0:T(8,128)(2,1)}, u32[]{:S(2)}, u32[]{:S(2)}) collective-permute-start(bf16[512,768]{1,0:T(8,128)(2,1)} %copy-done.100), channel_id=1, source_target_pairs={{0,16},{16,0},{1,17},{17,1},{2,18},{18,2},{3,19},{19,3},{4,20},{20... | collective-permute-start | bytes 2359304 | tf_op jit(solution)/shard_map/ppermute | solution.py:72
  476.8 57.5 %all-to-all-start.8 = ((bf16[8,64,768]{2,1,0:T(8,128)(2,1)}), bf16[8,64,768]{2,1,0:T(8,128)(2,1)}, u32[]{:S(2)}, u32[]{:S(2)}) async-start(bf16[8,64,768]{2,1,0:T(8,128)(2,1)} %bitcast.144), calls=%async_computation.8 | async-start | bytes 1572864 | tf_op jit(solution)/shard_map/all_to_all | solution.py:96
  484.6 33.1 %collective-permute-start.46 = (bf16[128,2048]{1,0:T(8,128)(2,1)S(1)}, bf16[128,2048]{1,0:T(8,128)(2,1)S(1)}, u32[]{:S(2)}, u32[]{:S(2)}) collective-permute-start(bf16[128,2048]{1,0:T(8,128)(2,1)S(1)} %copy-done.49), channel_id=1, source_target_pairs={{0,8},{8,0},{1,9},{9,1},{2,10},{10,2},{3,11},{11,3},{4,12},{12,4},... | collective-permute-start | bytes 1572872 | tf_op jit(solution)/shard_map/ppermute | solution.py:92
  487.8 46.5 %collective-permute-start.43 = (bf16[512,768]{1,0:T(8,128)(2,1)}, bf16[512,768]{1,0:T(8,128)(2,1)}, u32[]{:S(2)}, u32[]{:S(2)}) collective-permute-start(bf16[512,768]{1,0:T(8,128)(2,1)} %copy-done.101), channel_id=1, source_target_pairs={{0,16},{16,0},{1,17},{17,1},{2,18},{18,2},{3,19},{19,3},{4,20},{20... | collective-permute-start | bytes 2359304 | tf_op jit(solution)/shard_map/ppermute | solution.py:72
  489.1 43.0 %collective-permute-start.48 = (bf16[128,2048]{1,0:T(8,128)(2,1)S(1)}, bf16[128,2048]{1,0:T(8,128)(2,1)S(1)}, u32[]{:S(2)}, u32[]{:S(2)}) collective-permute-start(bf16[128,2048]{1,0:T(8,128)(2,1)S(1)} %shard_map.218), channel_id=1, source_target_pairs={{0,8},{8,0},{1,9},{9,1},{2,10},{10,2},{3,11},{11,3},{4,12},{12,4},... | collective-permute-start | bytes 1572872 | tf_op jit(solution)/shard_map/ppermute | solution.py:92
  489.7 42.4 %collective-permute-start.47 = (bf16[128,2048]{1,0:T(8,128)(2,1)S(1)}, bf16[128,2048]{1,0:T(8,128)(2,1)S(1)}, u32[]{:S(2)}, u32[]{:S(2)}) collective-permute-start(bf16[128,2048]{1,0:T(8,128)(2,1)S(1)} %get-tuple-element.315), channel_id=1, source_target_pairs={{0,2},{2,0},{1,3},{3,1},{4,6},{6,4},{5,7},{7,5},{8,10},{10,8},{9,1... | collective-permute-start | bytes 1572872 | tf_op jit(solution)/shard_map/ppermute | solution.py:88
  (172 other events, 1506.4 us)
